TPU v7x, 32 devices: a whole 2x2x4 slice. The times are simulated.
32 devices in a mesh: tm: 2 (over x), row: 4 (over y, core), col: 4 (over z).
Axes of the slice: x: 2, y: 2, z: 4, core: 2. Of those that a mesh axis runs over, the one named last changes fastest.
Arguments:
- resid: bfloat16 [2, 48, 160, 1152], P('tm', 'row', 'col'), may hold values from -8 to 8
- spatial_qkv: bfloat16 [3, 2, 48, 160, 1152], P(None, 'tm', 'row', 'col'), may hold values from -12 to 12
- key_keep: int32 [2, 48, 160], P('tm', 'row', 'col'), may hold values 0 or 1
- w_spatial_out: bfloat16 [1152, 1152], replicated, may hold values from -0.1875 to 0.1875
- modulation: float32 [2, 1152], replicated, may hold values from -3 to 3
- w_temporal_qkv: bfloat16 [1152, 3456], replicated, may hold values from -4 to 4
Outputs:
- temporal_heads: bfloat16 [2, 48, 160, 1152], P('tm', 'row', 'col')
All inputs are finite; a program needn't handle non-finite values. No bound on the sum of `key_keep` on one device may be relied on, other than what follows from the above.
Results may differ from a plain program's by a relative error of at most 0.0084.
Values may be sent and summed in bfloat16 or wider, within the bound.
No kernel may reach another device: no remote copies, remote signals or barrier semaphores. Data moves between devices by JAX's collectives and lax.ppermute only.
A program may use at most 128 MiB of HBM per device.

v0:
```python
import jax
import jax.numpy as jnp
from jax import lax
from jax.sharding import PartitionSpec as P

HEADS = 16
RADIUS = 3


NEG_FILL = -1e30
EPSILON = 1e-06


def extended(array, sides, width):
    for axis, dim in sides:
        count, length = (lax.axis_size(axis), array.shape[dim])
        up = [(i, (i + 1) % count) for i in range(count - 1)]
        down = [(j, i) for i, j in up]
        last = lax.slice_in_dim(array, length - width, length, axis=dim)
        leading = lax.slice_in_dim(array, 0, width, axis=dim)
        before = lax.ppermute(last, axis, up)
        after = lax.ppermute(leading, axis, down)
        array = jnp.concatenate([before, array, after], axis=dim)
    return array


def softmax_parts(scores, allowed):
    masked = jnp.where(allowed, scores, NEG_FILL)
    top_score = jnp.max(masked, -1, keepdims=True)
    weights_f = jnp.where(allowed, jnp.exp(masked - top_score), 0.0)
    return (weights_f.astype(jnp.bfloat16), jnp.sum(weights_f, -1))


def frame_attend(gathered, head_count):
    frames_all, single, items, width_three = gathered.shape
    width = width_three // 3
    head_size = width // head_count
    split_qkv = gathered.reshape(frames_all, items, 3, head_count, head_size)
    scores = jnp.einsum(
        "fphd,gphd->phfg",
        split_qkv[:, :, 0],
        split_qkv[:, :, 1],
        preferred_element_type=jnp.float32,
    ) * head_size ** (-0.5)
    weights_b, totals = softmax_parts(scores, True)
    weighted = jnp.einsum(
        "phfg,gphd->fphd", weights_b, split_qkv[:, :, 2], preferred_element_type=jnp.float32
    )
    result = weighted / jnp.transpose(totals, (2, 0, 1))[..., None]
    return result.astype(jnp.bfloat16).reshape(frames_all, single, items, width)


def per_device(resid, spatial_qkv, key_keep, w_spatial_out, modulation, w_temporal_qkv):
    frame_count, tile_rows, tile_cols, width = resid.shape
    head_size = width // HEADS
    score_scale = head_size ** (-0.5)
    tile_tokens = tile_rows * tile_cols
    pair = spatial_qkv[1:3]
    keep_flags = key_keep.astype(jnp.bfloat16)[None, :, :, :, None]
    padded_pair, padded_keep = (
        extended(pair, (("row", 2), ("col", 3)), RADIUS),
        extended(keep_flags, (("row", 2), ("col", 3)), RADIUS),
    )
    pad_rows = tile_rows + 2 * RADIUS
    pad_cols = tile_cols + 2 * RADIUS
    key_count = pad_rows * pad_cols
    queries = spatial_qkv[0].reshape(frame_count, tile_tokens, HEADS, head_size)
    keys_pad = padded_pair[0].reshape(frame_count, key_count, HEADS, head_size)
    values_pad = padded_pair[1].reshape(frame_count, key_count, HEADS, head_size)
    query_index = jnp.arange(tile_tokens)
    query_row = query_index // tile_cols
    query_col = query_index % tile_cols
    key_index = jnp.arange(key_count)
    key_row = key_index // pad_cols
    key_col = key_index % pad_cols
    row_gap = key_row[None, :] - query_row[:, None] - RADIUS
    col_gap = key_col[None, :] - query_col[:, None] - RADIUS
    in_window = (jnp.abs(row_gap) <= RADIUS) & (jnp.abs(col_gap) <= RADIUS)
    itself = (row_gap == 0) & (col_gap == 0)
    key_live = padded_keep.reshape(frame_count, key_count) > 0.5
    allowed = (in_window[None] & (key_live[:, None, :] | itself[None]))[:, None]
    scores = (
        jnp.einsum("fqhd,fkhd->fhqk", queries, keys_pad, preferred_element_type=jnp.float32)
        * score_scale
    )
    weights_b, totals = softmax_parts(scores, allowed)
    weighted = jnp.einsum(
        "fhqk,fkhd->fqhd", weights_b, values_pad, preferred_element_type=jnp.float32
    )
    spatial_heads = (weighted / jnp.transpose(totals, (0, 2, 1))[..., None]).astype(jnp.bfloat16)
    spatial_heads = spatial_heads.reshape(frame_count * tile_tokens, width)
    stream = resid.reshape(frame_count * tile_tokens, width).astype(jnp.float32) + jnp.dot(
        spatial_heads, w_spatial_out, preferred_element_type=jnp.float32
    )
    average = jnp.mean(stream, -1, keepdims=True)
    centered = stream - average
    variance = jnp.mean(centered * centered, -1, keepdims=True)
    normed = (
        centered * lax.rsqrt(variance + EPSILON) * (1.0 + modulation[1]) + modulation[0]
    ).astype(jnp.bfloat16)
    tm_count = lax.axis_size("tm")
    part_tokens = tile_tokens // tm_count
    normed_parts = normed.reshape(frame_count, tm_count, part_tokens, width)
    gathered = lax.all_to_all(normed_parts, "tm", split_axis=1, concat_axis=0, tiled=True)
    frames_all, single, items, unused = gathered.shape
    projected = jnp.dot(
        gathered.reshape(frames_all * single * items, width),
        w_temporal_qkv,
        preferred_element_type=jnp.float32,
    ).astype(jnp.bfloat16)
    projected = projected.reshape(frames_all, single, items, 3 * width)
    result = lax.all_to_all(
        frame_attend(projected, HEADS), "tm", split_axis=0, concat_axis=1, tiled=True
    )
    return result.reshape(frame_count, tile_rows, tile_cols, width)


def solution(mesh):
    return jax.shard_map(
        per_device,
        mesh=mesh,
        in_specs=(
            P("tm", "row", "col", None),
            P(None, "tm", "row", "col", None),
            P("tm", "row", "col"),
            P(),
            P(),
            P(),
        ),
        out_specs=P("tm", "row", "col", None),
        check_vma=False,
    )
```

profile of v0, /device:TPU:0, one launch (start us, length us, event | category | flops | bytes accessed | tf_op | source)
XLA Modules:
  0.0 199.6 jit_solution(16022606005879470861)
XLA Ops:
  0.0 0.8 convert_element_type.30
  0.9 2.4 %collective-permute-start.4 = (bf16[1,1,3,40,1]{3,2,4,1,0:T(4,128)(2,1)S(1)}, bf16[1,1,3,40,1]{3,2,4,1,0:T(4,128)(2,1)S(1)}, u32[]{:S(2)}, u32[]{:S(2)}) collective-permute-start(bf16[1,1,3,40,1]{3,2,4,1,0:T(4,128)(2,1)S(1)} %get-tuple-element.18), channel_id=1, source_target_pairs={{0,4},{4,8},{8,12},{1,5},{5,9},{9,13},{2,6},{6,10},{10,14},{3,7},{... | collective-permute-start | bytes 728 | tf_op jit(solution)/shard_map/ppermute | solution.py:21
  3.2 1.3 collective-permute-start.5
  4.5 2.3 %fusion.55 = (bf16[2,1,3,40,1152]{4,3,2,1,0:T(8,128)(2,1)}, bf16[2,1,3,40,1152]{4,3,2,1,0:T(8,128)(2,1)}) fusion(bf16[3,1,12,40,1152]{4,3,2,1,0:T(8,128)(2,1)} %param.7), kind=kLoop, calls=%fused_computation.79 | loop fusion | bytes 2211840 | tf_op jit(solution)/shard_map/slice | solution.py:19
  6.8 6.2 %collective-permute-start = (bf16[2,1,3,40,1152]{4,3,2,1,0:T(8,128)(2,1)}, bf16[2,1,3,40,1152]{4,3,2,1,0:T(8,128)(2,1)}, u32[]{:S(2)}, u32[]{:S(2)}) collective-permute-start(bf16[2,1,3,40,1152]{4,3,2,1,0:T(8,128)(2,1)} %get-tuple-element.14), channel_id=1, source_target_pairs={{0,4},{4,8},{8,12},{1,5},{5,9},{9,13},{2,6},{6,10},{10,14},{3,7},{... | collective-permute-start | bytes 1658888 | tf_op jit(solution)/shard_map/ppermute | solution.py:21
  13.1 1.3 collective-permute-start.1
  14.4 0.8 add_reduce_fusion
  15.2 1.1 slice.64
  16.3 0.9 slice-done
  17.2 2.0 %copy.102 = bf16[2,1,12,40,1152]{4,2,3,1,0:T(8,128)(2,1)} copy(bf16[2,1,12,40,1152]{4,3,2,1,0:T(8,128)(2,1)S(1)} %slice-done) | data formatting | bytes 4423680
  19.3 0.1 fusion.56
  19.3 3.5 %collective-permute-start.6 = (bf16[1,1,18,3,1]{3,2,4,1,0:T(8,128)(2,1)S(1)}, bf16[1,1,18,3,1]{3,2,4,1,0:T(8,128)(2,1)S(1)}, u32[]{:S(2)}, u32[]{:S(2)}) collective-permute-start(bf16[1,1,18,3,1]{3,2,4,1,0:T(8,128)(2,1)S(1)} %get-tuple-element.16), channel_id=1, source_target_pairs={{0,1},{1,2},{2,3},{4,5},{5,6},{6,7},{8,9},{9,10},{10,11},{12,13},{... | collective-permute-start | bytes 332 | tf_op jit(solution)/shard_map/ppermute | solution.py:21
  22.8 1.3 collective-permute-start.7
  24.1 5.5 %reshape.226 = bf16[480,16,72]{2,1,0:T(8,128)(2,1)} reshape(bf16[1,1,12,40,1152]{4,3,2,1,0:T(8,128)(2,1)} %slice.64) | data formatting | bytes 2211840 | tf_op jit(solution)/shard_map/reshape.3
  29.6 0.1 maximum_compare_fusion
  29.7 0.1 gt.17
  29.8 1.3 copy.82
  31.2 0.3 copy.83
  31.5 1.5 pad_maximum_fusion.3
  33.0 4.6 %collective-permute-start.2 = (bf16[2,1,18,3,1152]{4,2,3,1,0:T(8,128)(2,1)S(1)}, bf16[2,1,18,3,1152]{4,2,3,1,0:T(8,128)(2,1)S(1)}, u32[]{:S(2)}, u32[]{:S(2)}) collective-permute-start(bf16[2,1,18,3,1152]{4,2,3,1,0:T(8,128)(2,1)S(1)} %get-tuple-element.12), channel_id=1, source_target_pairs={{0,1},{1,2},{2,3},{4,5},{5,6},{6,7},{8,9},{9,10},{10,11},{12,13},{... | collective-permute-start | bytes 746504 | tf_op jit(solution)/shard_map/ppermute | solution.py:21
  37.6 1.3 collective-permute-start.3
  38.9 1.5 fusion.30
  40.4 5.3 %collective-permute-done.2 = bf16[2,1,18,3,1152]{4,2,3,1,0:T(8,128)(2,1)S(1)} collective-permute-done((bf16[2,1,18,3,1152]{4,2,3,1,0:T(8,128)(2,1)S(1)}, bf16[2,1,18,3,1152]{4,2,3,1,0:T(8,128)(2,1)S(1)}, u32[]{:S(2)}, u32[]{:S(2)}) %collective-permute-start.2) | collective-permute-done | bytes 248864 | tf_op jit(solution)/shard_map/ppermute | solution.py:21
  45.7 4.2 %collective-permute-done.3 = bf16[2,1,18,3,1152]{4,2,3,1,0:T(8,128)(2,1)S(1)} collective-permute-done((bf16[2,1,18,3,1152]{4,2,3,1,0:T(8,128)(2,1)S(1)}, bf16[2,1,18,3,1152]{4,2,3,1,0:T(8,128)(2,1)S(1)}, u32[]{:S(2)}, u32[]{:S(2)}) %collective-permute-start.3) | collective-permute-done | bytes 248864 | tf_op jit(solution)/shard_map/ppermute | solution.py:22
  49.9 3.1 %pad_maximum_fusion = bf16[2,1,18,46,1152]{4,2,3,1,0:T(8,128)(2,1)S(1)} fusion(bf16[2,1,18,3,1152]{4,2,3,1,0:T(8,128)(2,1)S(1)} %collective-permute-done.3, bf16[2,1,3,40,1152]{4,2,3,1,0:T(4,128)(2,1)S(1)} %copy.83, bf16[2,1,12,40,1152]{4,2,3,1,0:T(8,128)(2,1)S(1)} %copy-done.2, bf16[2,1,3,40,1152]{4,2,3,1,0:T(4,128)(2,1)S(1)} %copy.82, ...), kind=kLoop, calls=%fused_computation.10 | loop fusion | flops 19077120 | bytes 7630848 | tf_op jit(solution)/shard_map/concatenate | solution.py:23
  53.0 1.9 fusion.54
  54.9 1.5 copy.85
  56.4 8.3 %reshape.225 = bf16[828,16,72]{2,1,0:T(8,128)(2,1)} reshape(bf16[1,1,18,46,1152]{4,3,2,1,0:T(8,128)(2,1)} %copy.85) | data formatting | bytes 3815424 | tf_op jit(solution)/shard_map/reshape.4
  64.8 3.2 %copy.84 = bf16[1,1,18,46,1152]{4,3,2,1,0:T(8,128)(2,1)} copy(bf16[1,1,18,46,1152]{4,2,3,1,0:T(8,128)(2,1)} %get-tuple-element.10) | data formatting | bytes 3815424 | tf_op jit(solution)/shard_map/slice | solution.py:69
  68.0 8.3 %reshape.224 = bf16[828,16,72]{2,1,0:T(8,128)(2,1)} reshape(bf16[1,1,18,46,1152]{4,3,2,1,0:T(8,128)(2,1)} %copy.84) | data formatting | bytes 3815424 | tf_op jit(solution)/shard_map/reshape.14
  76.3 18.5 %fusion.58 = (f32[16,480]{1,0:T(8,128)S(1)}, bf16[16,480,828]{1,2,0:T(8,128)(2,1)}) fusion(pred[480,828]{0,1:T(8,128)(4,1)S(1)} %fusion.30, bf16[828,16,72]{2,1,0:T(8,128)(2,1)} %reshape.225, bf16[480,16,72]{2,1,0:T(8,128)(2,1)} %reshape.226), kind=kOutput, calls=%fused_computation.82 | convolution fusion | flops 953856832 | bytes 16159872 | tf_op jit(solution)/shard_map/sub | solution.py:30
  94.8 9.1 %fusion.17 = bf16[1,480,16,72]{1,3,2,0:T(8,128)(2,1)S(1)} fusion(bf16[16,480,828]{1,2,0:T(8,128)(2,1)} %get-tuple-element.21, bf16[828,16,72]{2,1,0:T(8,128)(2,1)} %reshape.224, f32[480,16]{0,1:T(8,128)S(1)} %bitcast.73), kind=kOutput, calls=%fused_computation.20 | convolution fusion | flops 916807680 | bytes 15762432 | tf_op jit(solution)/shard_map/fhqk,fkhd->fqhd/dot_general | solution.py:87
  104.0 2.0 fusion.67
  106.0 0.4 multiply_reduce_fusion
  106.3 0.4 add_convert_fusion
  106.8 17.1 %all_to_all.8 = bf16[1,2,240,1152]{3,2,0,1:T(8,128)(2,1)S(1)} all-to-all(bf16[1,2,240,1152]{3,2,0,1:T(8,128)(2,1)S(1)} %bitcast.63), channel_id=1, replica_groups=mesh['tm'=2,'row'=4,'col'=4] {'tm'}, dimensions={1} | all-to-all | bytes 2211840 | tf_op jit(solution)/shard_map/all_to_all | solution.py:104
  123.9 6.1 %convolution_convert_fusion = bf16[480,3456]{1,0:T(8,128)(2,1)} fusion(bf16[480,1152]{1,0:T(8,128)(2,1)S(1)} %bitcast.67, bf16[1152,3456]{1,0:T(8,128)(2,1)S(1)} %bitcast.72), kind=kOutput, calls=%fused_computation.9 | convolution fusion | flops 3823718400 | bytes 12386304 | tf_op jit(solution)/shard_map/dot_general | solution.py:106
  130.0 12.9 %reshape.233 = bf16[2,240,3,16,72]{4,3,2,1,0:T(8,128)(2,1)} reshape(bf16[480,3456]{1,0:T(8,128)(2,1)} %convolution_convert_fusion) | data formatting | bytes 6635520 | tf_op jit(solution)/shard_map/reshape;reshape | solution.py:38
  142.9 5.2 %fusion.53 = (bf16[2,240,1,16,72]{4,3,2,1,0:T(8,128)(2,1)S(1)}, bf16[2,240,1,16,72]{4,3,2,1,0:T(8,128)(2,1)}, bf16[2,240,1,16,72]{4,3,2,1,0:T(8,128)(2,1)S(1)}) fusion(bf16[2,240,3,16,72]{4,3,2,1,0:T(8,128)(2,1)} %reshape.233), kind=kLoop, calls=%fused_computation.77 | loop fusion | bytes 6635520 | tf_op jit(solution)/shard_map/slice | solution.py:41
  148.1 7.3 %fusion.68 = (f32[240,16,2]{2,1,0:T(8,128)S(1)}, f32[240,16,2,2]{2,3,1,0:T(2,128)S(1)}) fusion(bf16[2,240,1,16,72]{4,3,2,1,0:T(8,128)(2,1)S(1)} %get-tuple-element.9, bf16[2,240,1,16,72]{4,3,2,1,0:T(8,128)(2,1)S(1)} %get-tuple-element.7), kind=kOutput, calls=%fused_computation.84 | convolution fusion | flops 2234880 | bytes 2304000 | tf_op jit(solution)/shard_map/fphd,gphd->phfg/dot_general | solution.py:39
  155.4 7.0 %fusion.19 = f32[240,16,2]{2,1,0:T(8,128)S(1)} fusion(f32[240,16,2,2]{2,3,1,0:T(2,128)S(1)} %get-tuple-element.25, f32[240,16,2]{2,1,0:T(8,128)S(1)} %get-tuple-element.24), kind=kLoop, calls=%fused_computation.25 | loop fusion | flops 23040 | bytes 122880 | tf_op jit(solution)/shard_map/reduce_sum | solution.py:31
  162.5 1.0 copy.96
  163.4 8.9 %fusion.21 = f32[240,16,72,2]{2,3,1,0:T(2,128)} fusion(bf16[2,240,1,16,72]{4,3,2,1,0:T(8,128)(2,1)} %get-tuple-element.8, f32[240,16,2,2]{2,3,1,0:T(2,128)} %copy-done.4, f32[240,16,2]{2,1,0:T(8,128)} %copy-done.5), kind=kOutput, calls=%fused_computation.30 | convolution fusion | flops 2242560 | bytes 3409920 | tf_op jit(solution)/shard_map/phfg,gphd->fphd/dot_general | solution.py:46
  172.4 5.3 %copy.95 = f32[240,16,72,2]{0,2,1,3:T(8,128)S(1)} copy(f32[240,16,72,2]{2,3,1,0:T(2,128)} %fusion.21) | data formatting | bytes 4423680 | tf_op jit(solution)/shard_map/phfg,gphd->fphd/dot_general | solution.py:46
  177.7 1.2 fusion.18
  179.0 2.5 %copy.97 = bf16[2,1,240,1152]{3,2,1,0:T(8,128)(2,1)} copy(bf16[2,1,240,1152]{2,3,0,1:T(8,128)(2,1)} %bitcast.62) | data formatting | bytes 2211840 | tf_op jit(solution)/shard_map/reshape | solution.py:50
  181.5 17.1 %all_to_all.9 = bf16[2,1,240,1152]{3,2,1,0:T(8,128)(2,1)S(1)} all-to-all(bf16[2,1,240,1152]{3,2,1,0:T(8,128)(2,1)} %copy.97), channel_id=1, replica_groups=mesh['tm'=2,'row'=4,'col'=4] {'tm'}, dimensions={0} | all-to-all | bytes 2211840 | tf_op jit(solution)/shard_map/all_to_all | solution.py:112
  198.6 1.0 copy.145
  (33 shorter events, 0.1 us)
Async XLA Ops:
  0.0 103.9 %copy-start = (bf16[1152,1152]{1,0:T(8,128)(2,1)S(1)}, bf16[1152,1152]{1,0:T(8,128)(2,1)}, u32[]{:S(2)}) copy-start(bf16[1152,1152]{1,0:T(8,128)(2,1)} %param.9) | copy-start | bytes 7962628
  0.9 18.4 %collective-permute-start.4 = (bf16[1,1,3,40,1]{3,2,4,1,0:T(4,128)(2,1)S(1)}, bf16[1,1,3,40,1]{3,2,4,1,0:T(4,128)(2,1)S(1)}, u32[]{:S(2)}, u32[]{:S(2)}) collective-permute-start(bf16[1,1,3,40,1]{3,2,4,1,0:T(4,128)(2,1)S(1)} %get-tuple-element.18), channel_id=1, source_target_pairs={{0,4},{4,8},{8,12},{1,5},{5,9},{9,13},{2,6},{6,10},{10,14},{3,7},{... | collective-permute-start | bytes 728 | tf_op jit(solution)/shard_map/ppermute | solution.py:21
  3.2 16.0 %collective-permute-start.5 = (bf16[1,1,3,40,1]{3,2,4,1,0:T(4,128)(2,1)S(1)}, bf16[1,1,3,40,1]{3,2,4,1,0:T(4,128)(2,1)S(1)}, u32[]{:S(2)}, u32[]{:S(2)}) collective-permute-start(bf16[1,1,3,40,1]{3,2,4,1,0:T(4,128)(2,1)S(1)} %get-tuple-element.19), channel_id=1, source_target_pairs={{4,0},{8,4},{12,8},{5,1},{9,5},{13,9},{6,2},{10,6},{14,10},{7,3},{... | collective-permute-start | bytes 728 | tf_op jit(solution)/shard_map/ppermute | solution.py:22
  6.8 8.4 %copy-start.3 = (bf16[3,1,12,40,1152]{4,3,2,1,0:T(8,128)(2,1)S(1)}, bf16[3,1,12,40,1152]{4,3,2,1,0:T(8,128)(2,1)}, u32[]{:S(2)}) copy-start(bf16[3,1,12,40,1152]{4,3,2,1,0:T(8,128)(2,1)} %param.7) | copy-start | bytes 9953284
  6.8 23.0 %collective-permute-start = (bf16[2,1,3,40,1152]{4,3,2,1,0:T(8,128)(2,1)}, bf16[2,1,3,40,1152]{4,3,2,1,0:T(8,128)(2,1)}, u32[]{:S(2)}, u32[]{:S(2)}) collective-permute-start(bf16[2,1,3,40,1152]{4,3,2,1,0:T(8,128)(2,1)} %get-tuple-element.14), channel_id=1, source_target_pairs={{0,4},{4,8},{8,12},{1,5},{5,9},{9,13},{2,6},{6,10},{10,14},{3,7},{... | collective-permute-start | bytes 1658888 | tf_op jit(solution)/shard_map/ppermute | solution.py:21
  13.1 18.1 %collective-permute-start.1 = (bf16[2,1,3,40,1152]{4,3,2,1,0:T(8,128)(2,1)}, bf16[2,1,3,40,1152]{4,3,2,1,0:T(8,128)(2,1)S(1)}, u32[]{:S(2)}, u32[]{:S(2)}) collective-permute-start(bf16[2,1,3,40,1152]{4,3,2,1,0:T(8,128)(2,1)} %get-tuple-element.15), channel_id=1, source_target_pairs={{4,0},{8,4},{12,8},{5,1},{9,5},{13,9},{6,2},{10,6},{14,10},{7,3},{... | collective-permute-start | bytes 1658888 | tf_op jit(solution)/shard_map/ppermute | solution.py:22
  15.2 2.0 %slice-start = ((bf16[3,1,12,40,1152]{4,3,2,1,0:T(8,128)(2,1)}), bf16[2,1,12,40,1152]{4,3,2,1,0:T(8,128)(2,1)S(1)}, s32[]{:S(2)}) async-start(bf16[3,1,12,40,1152]{4,3,2,1,0:T(8,128)(2,1)} %param.7), calls=%async_computation.2 | async-start | bytes 4423680 | tf_op jit(solution)/shard_map/slice | solution.py:58
  19.3 10.3 %collective-permute-start.6 = (bf16[1,1,18,3,1]{3,2,4,1,0:T(8,128)(2,1)S(1)}, bf16[1,1,18,3,1]{3,2,4,1,0:T(8,128)(2,1)S(1)}, u32[]{:S(2)}, u32[]{:S(2)}) collective-permute-start(bf16[1,1,18,3,1]{3,2,4,1,0:T(8,128)(2,1)S(1)} %get-tuple-element.16), channel_id=1, source_target_pairs={{0,1},{1,2},{2,3},{4,5},{5,6},{6,7},{8,9},{9,10},{10,11},{12,13},{... | collective-permute-start | bytes 332 | tf_op jit(solution)/shard_map/ppermute | solution.py:21
  22.8 6.8 %collective-permute-start.7 = (bf16[1,1,18,3,1]{3,2,4,1,0:T(8,128)(2,1)S(1)}, bf16[1,1,18,3,1]{3,2,4,1,0:T(8,128)(2,1)S(1)}, u32[]{:S(2)}, u32[]{:S(2)}) collective-permute-start(bf16[1,1,18,3,1]{3,2,4,1,0:T(8,128)(2,1)S(1)} %get-tuple-element.17), channel_id=1, source_target_pairs={{1,0},{2,1},{3,2},{5,4},{6,5},{7,6},{9,8},{10,9},{11,10},{13,12},{... | collective-permute-start | bytes 332 | tf_op jit(solution)/shard_map/ppermute | solution.py:22
  31.5 18.5 %copy-start.2 = (bf16[2,1,12,40,1152]{4,2,3,1,0:T(8,128)(2,1)S(1)}, bf16[2,1,12,40,1152]{4,2,3,1,0:T(8,128)(2,1)}, u32[]{:S(2)}) copy-start(bf16[2,1,12,40,1152]{4,2,3,1,0:T(8,128)(2,1)} %copy.102) | copy-start | bytes 6635524
  33.0 12.7 %collective-permute-start.2 = (bf16[2,1,18,3,1152]{4,2,3,1,0:T(8,128)(2,1)S(1)}, bf16[2,1,18,3,1152]{4,2,3,1,0:T(8,128)(2,1)S(1)}, u32[]{:S(2)}, u32[]{:S(2)}) collective-permute-start(bf16[2,1,18,3,1152]{4,2,3,1,0:T(8,128)(2,1)S(1)} %get-tuple-element.12), channel_id=1, source_target_pairs={{0,1},{1,2},{2,3},{4,5},{5,6},{6,7},{8,9},{9,10},{10,11},{12,13},{... | collective-permute-start | bytes 746504 | tf_op jit(solution)/shard_map/ppermute | solution.py:21
  37.6 12.3 %collective-permute-start.3 = (bf16[2,1,18,3,1152]{4,2,3,1,0:T(8,128)(2,1)S(1)}, bf16[2,1,18,3,1152]{4,2,3,1,0:T(8,128)(2,1)S(1)}, u32[]{:S(2)}, u32[]{:S(2)}) collective-permute-start(bf16[2,1,18,3,1152]{4,2,3,1,0:T(8,128)(2,1)S(1)} %get-tuple-element.13), channel_id=1, source_target_pairs={{1,0},{2,1},{3,2},{5,4},{6,5},{7,6},{9,8},{10,9},{11,10},{13,12},{... | collective-permute-start | bytes 746504 | tf_op jit(solution)/shard_map/ppermute | solution.py:22
  94.8 9.1 %copy-start.6 = (bf16[1,12,40,1152]{3,2,1,0:T(8,128)(2,1)S(1)}, bf16[1,12,40,1152]{3,2,1,0:T(8,128)(2,1)}, u32[]{:S(2)}) copy-start(bf16[1,12,40,1152]{3,2,1,0:T(8,128)(2,1)} %param.6) | copy-start | bytes 3317764
  104.0 20.0 %slice-start.1 = ((s8[7962624]{0:T(1024)(128)(4,1)}), s8[4194304]{0:T(1024)(128)(4,1)S(1)}, s32[]{:S(2)}) async-start(s8[7962624]{0:T(1024)(128)(4,1)} %bitcast.71), calls=%async_computation.3 | async-start | bytes 8388608
  105.9 18.0 %slice-start.2 = ((s8[7962624]{0:T(1024)(128)(4,1)}), s8[3768320]{0:T(1024)(128)(4,1)S(1)}, s32[]{:S(2)}) async-start(s8[7962624]{0:T(1024)(128)(4,1)} %bitcast.71), calls=%async_computation.4 | async-start | bytes 7536640
  155.4 7.0 %copy-start.4 = (f32[240,16,2,2]{2,3,1,0:T(2,128)}, f32[240,16,2,2]{2,3,1,0:T(2,128)S(1)}, u32[]{:S(2)}) copy-start(f32[240,16,2,2]{2,3,1,0:T(2,128)S(1)} %get-tuple-element.25) | copy-start | bytes 184324
  155.4 7.0 %copy-start.5 = (f32[240,16,2]{2,1,0:T(8,128)}, f32[240,16,2]{2,1,0:T(8,128)S(1)}, u32[]{:S(2)}) copy-start(f32[240,16,2]{2,1,0:T(8,128)S(1)} %get-tuple-element.24) | copy-start | bytes 92164
  179.0 20.6 %copy-start.1 = (bf16[1152,1152]{1,0:T(8,128)(2,1)S(1)}, bf16[1152,1152]{1,0:T(8,128)(2,1)}, u32[]{:S(2)}) copy-start(bf16[1152,1152]{1,0:T(8,128)(2,1)} %param.9) | copy-start | bytes 7962628
where the time goes:
time: 201 us; the launch traced here: 200 us
  local copies, waits for them, and re-layouts  64.9 us (32%)
  matrix products  51.9 us (26%)
  blocking collectives  34.3 us (17%)
  starting transfers between devices  21.8 us (11%)
  other arithmetic  17 us (8%)
  waiting for transfers between devices  9.56 us (5%)
    another operation x3, local copies, waits for them, and re-layouts  22.2 us
    sub x1, matrix products, softmax_parts(): weights_f = jnp.where(allowed, jnp.exp(masked - top_score), 0.0)  18.5 us
    all_to_all x1, blocking collectives, per_device(): lax.all_to_all(normed_parts, 'tm', split_axis=1, concat_axis=0, tiled=True)  17.1 us
    all_to_all x1, blocking collectives, per_device(): lax.all_to_all(frame_attend(projected, HEADS), 'tm', split_axis=0, concat...  17.1 us
    ppermute x4, starting transfers between devices, extended(): before = lax.ppermute(last, axis, up)  16.6 us
    another operation x1, local copies, waits for them, and re-layouts, frame_attend(): split_qkv = gathered.reshape(frames_all, items, 3, head_count, head_size)  12.9 us
    dot_general x1, matrix products, per_device(): jnp.einsum('fhqk,fkhd->fqhd', weights_b, values_pad, preferred_element_ty...  9.09 us
    dot_general x1, matrix products, frame_attend(): jnp.einsum('phfg,gphd->fphd', weights_b, split_qkv[:, :, 2], preferred_el...  8.92 us
  transfers between devices with their start and end apart: 8, of which 2 were waited for; matrix products, arithmetic and copies ran while one was open for 7% of the time, Pallas kernels for 0%

commit v1 on v0

--- a/solution.py
+++ b/solution.py
@@ -1,6 +1,11 @@
+import functools
+import math
+
 import jax
 import jax.numpy as jnp
 from jax import lax
+from jax.experimental import pallas as pl
+from jax.experimental.pallas import tpu as pltpu
 from jax.sharding import PartitionSpec as P
 
 HEADS = 16
@@ -9,6 +14,12 @@
 
 NEG_FILL = -1e30
 EPSILON = 1e-06
+
+LANES = 128
+STRIP = 8
+EDGE = STRIP // 2
+MIB = 1024 * 1024
+VMEM = pl.BlockSpec(memory_space=pltpu.VMEM)
 
 
 def extended(array, sides, width):
@@ -50,7 +61,7 @@
     return result.astype(jnp.bfloat16).reshape(frames_all, single, items, width)
 
 
-def per_device(resid, spatial_qkv, key_keep, w_spatial_out, modulation, w_temporal_qkv):
+def general_device(resid, spatial_qkv, key_keep, w_spatial_out, modulation, w_temporal_qkv):
     frame_count, tile_rows, tile_cols, width = resid.shape
     head_size = width // HEADS
     score_scale = head_size ** (-0.5)
@@ -115,6 +126,392 @@
     return result.reshape(frame_count, tile_rows, tile_cols, width)
 
 
+def iota(shape, dim):
+    return lax.broadcasted_iota(jnp.int32, shape, dim)
+
+
+def tile_attend(queries, keys, values, bias):
+    count, width = queries.shape
+    head = width // HEADS
+    factor = head ** (-0.5) * math.log2(math.e)
+    lane = iota((1, 2 * LANES), 1)
+    bias_two = jnp.concatenate([bias, bias], axis=0)
+    pairs = []
+    for pair in range(HEADS // 2):
+        start = LANES * pair
+        low = 2 * head * pair - start
+        mid, high = low + head, low + 2 * head
+        window = queries[:, start : start + 2 * LANES]
+        first = jnp.where((lane >= low) & (lane < mid), window, 0.0)
+        second = jnp.where((lane >= mid) & (lane < high), window, 0.0)
+        both = jnp.concatenate([first, second], axis=0).astype(jnp.bfloat16)
+        scores = lax.dot_general(
+            both,
+            keys[:, start : start + 2 * LANES],
+            (((1,), (1,)), ((), ())),
+            preferred_element_type=jnp.float32,
+        )
+        scores = scores + bias_two
+        top = jnp.max(scores, -1, keepdims=True)
+        weights = jnp.exp2((scores - top) * factor)
+        total = jnp.sum(weights, -1, keepdims=True)
+        mixed = jnp.dot(
+            weights.astype(jnp.bfloat16),
+            values[:, start : start + 2 * LANES],
+            preferred_element_type=jnp.float32,
+        )
+        mixed = mixed / total
+        pairs.append(jnp.where(lane < mid, mixed[:count], mixed[count:]))
+    lane = iota((1, LANES), 1)
+    blocks = [pairs[0][:, :LANES]]
+    for pair in range(1, HEADS // 2):
+        cut = 2 * head * pair - LANES * pair
+        blocks.append(jnp.where(lane < cut, pairs[pair - 1][:, LANES:], pairs[pair][:, :LANES]))
+    blocks.append(pairs[-1][:, LANES:])
+    return jnp.concatenate(blocks, axis=1)
+
+
+def keep_row(count, keep):
+    picker = jnp.where(iota((count, LANES), 1) == 0, 1.0, 0.0).astype(jnp.bfloat16)
+    return lax.dot_general(
+        picker, keep, (((1,), (1,)), ((), ())), preferred_element_type=jnp.float32
+    )
+
+
+def make_bias(q_row, q_col, k_row, k_col, keep):
+    row_gap, col_gap = k_row - q_row, k_col - q_col
+    near = (jnp.abs(row_gap) <= RADIUS) & (jnp.abs(col_gap) <= RADIUS)
+    itself = (row_gap == 0) & (col_gap == 0)
+    return jnp.where(near & ((keep > 0.5) | itself), 0.0, NEG_FILL)
+
+
+def strip_bias(rows, keep):
+    count, keys = rows * STRIP, (rows + 2 * RADIUS) * 2 * STRIP
+    q, k = iota((count, keys), 0), iota((count, keys), 1)
+    return make_bias(
+        q // STRIP + RADIUS, q % STRIP + EDGE, k // (2 * STRIP), k % (2 * STRIP), keep_row(count, keep)
+    )
+
+
+def finish(heads, resid, w_out, modulation):
+    stream = resid + jnp.dot(heads, w_out, preferred_element_type=jnp.float32)
+    average = jnp.mean(stream, -1, keepdims=True)
+    centered = stream - average
+    variance = jnp.mean(centered * centered, -1, keepdims=True)
+    scaled = centered * lax.rsqrt(variance + EPSILON)
+    return (scaled * (1.0 + modulation[1:2]) + modulation[0:1]).astype(jnp.bfloat16)
+
+
+def window(ref, plane, rows, strip):
+    found = ref[plane, rows, pl.ds(STRIP * strip, 2 * STRIP), :].astype(jnp.float32)
+    return found.reshape(found.shape[0] * found.shape[1], found.shape[2]).astype(jnp.bfloat16)
+
+
+def middle(ref, plane, rows, strip):
+    found = ref[plane, rows, pl.ds(STRIP * strip, 2 * STRIP), :].astype(jnp.float32)
+    found = found[:, EDGE : EDGE + STRIP]
+    return found.reshape(found.shape[0] * STRIP, found.shape[2])
+
+
+def inner_kernel(qkv, keep, resid, w_out, modulation, out, heads):
+    tile_rows, tile_cols, width = resid.shape[1:]
+    rows = tile_rows - 2 * RADIUS
+    strips = tile_cols // STRIP - 1
+    every = pl.ds(0, tile_rows)
+    mine = pl.ds(RADIUS, rows)
+    for strip in range(strips):
+        bias = strip_bias(rows, window(keep, 0, every, strip))
+        mixed = tile_attend(
+            middle(qkv, 0, mine, strip), window(qkv, 1, every, strip), window(qkv, 2, every, strip), bias
+        )
+        heads[strip] = mixed.astype(jnp.bfloat16)
+        stream = finish(heads[strip], middle(resid, 0, mine, strip), w_out[...], modulation[...])
+        out[strip] = stream
+
+
+def rim_kernel(qkv, keep, above, below, resid, w_out, modulation, out, heads):
+    tile_rows, tile_cols, width = resid.shape[1:]
+    strips = tile_cols // STRIP - 1
+    near = 2 * RADIUS
+    for strip in range(strips):
+        halves = []
+        sources = []
+        for side in range(2):
+            inner = pl.ds(0 if side == 0 else tile_rows - near, near)
+            mine = pl.ds(0 if side == 0 else tile_rows - RADIUS, RADIUS)
+            halo_ref = above if side == 0 else below
+            halo = window(halo_ref, 0, pl.ds(0, RADIUS), strip)
+            parts = []
+            for at, local in (
+                (0, window(qkv, 1, inner, strip)),
+                (width, window(qkv, 2, inner, strip)),
+                (2 * width, window(keep, 0, inner, strip)),
+            ):
+                far = halo[:, at : at + local.shape[1]]
+                parts.append(jnp.concatenate([far, local] if side == 0 else [local, far], axis=0))
+            bias = strip_bias(RADIUS, parts[2])
+            halves.append(tile_attend(middle(qkv, 0, mine, strip), parts[0], parts[1], bias))
+            sources.append(middle(resid, 0, mine, strip))
+        heads[strip] = jnp.concatenate(halves, axis=0).astype(jnp.bfloat16)
+        out[strip] = finish(heads[strip], jnp.concatenate(sources, axis=0), w_out[...], modulation[...])
+
+
+def edge_columns(ref, plane, row):
+    found = ref[plane, row].astype(jnp.float32)
+    return found[:STRIP], found[found.shape[0] - STRIP :]
+
+
+def edge_kernel(qkv, keep, above, below, left, right, resid, w_out, modulation, out, far, ends, mine):
+    tile_rows, tile_cols, width = resid.shape[1:]
+    pad_rows = tile_rows + 2 * RADIUS
+    far[...] = jnp.zeros_like(far)
+    for row in range(pad_rows):
+        local = row - RADIUS
+        if 0 <= local < tile_rows:
+            sources = ((qkv, 1, local, 0, width), (qkv, 2, local, width, width), (keep, 0, local, 2 * width, LANES))
+        elif local < 0:
+            sources = ((above, 0, row, 0, 2 * width + LANES),)
+        else:
+            sources = ((below, 0, local - tile_rows, 0, 2 * width + LANES),)
+        for ref, plane, at, lane, lanes in sources:
+            head, tail = edge_columns(ref, plane, at)
+            far[row, 0:STRIP, lane : lane + lanes] = head
+            far[row, STRIP : 2 * STRIP, lane : lane + lanes] = tail
+        far[row, 2 * STRIP : 2 * STRIP + RADIUS, :] = left[0, row].astype(jnp.float32)
+        far[row, 2 * STRIP + RADIUS : 2 * STRIP + 2 * RADIUS, :] = right[0, row].astype(jnp.float32)
+    for row in range(tile_rows):
+        for ref, plane, target in ((qkv, 0, ends), (resid, 0, mine)):
+            head, tail = edge_columns(ref, plane, row)
+            target[row, 0:EDGE] = head[:EDGE]
+            target[row, EDGE:STRIP] = tail[EDGE:]
+    rows = 4
+    span = 3 * STRIP
+    for start in range(0, tile_rows, rows):
+        count, keys = rows * STRIP, (rows + 2 * RADIUS) * span
+        found = far[start : start + rows + 2 * RADIUS].reshape(keys, 2 * width + LANES).astype(jnp.bfloat16)
+        q, k = iota((count, keys), 0), iota((count, keys), 1)
+        q_col = q % STRIP
+        q_col = jnp.where(q_col < EDGE, q_col, q_col + tile_cols - STRIP)
+        k_col = k % span
+        k_col = jnp.where(
+            k_col < STRIP,
+            k_col,
+            jnp.where(
+                k_col < 2 * STRIP,
+                k_col + tile_cols - 2 * STRIP,
+                jnp.where(
+                    k_col < 2 * STRIP + RADIUS,
+                    k_col - 2 * STRIP - RADIUS,
+                    jnp.where(
+                        k_col < 2 * STRIP + 2 * RADIUS,
+                        k_col - 2 * STRIP - RADIUS + tile_cols,
+                        -100 * tile_cols,
+                    ),
+                ),
+            ),
+        )
+        bias = make_bias(
+            q // STRIP + RADIUS, q_col, k // span, k_col, keep_row(count, found[:, 2 * width :])
+        )
+        mixed = tile_attend(
+            ends[start : start + rows].reshape(count, width), found[:, :width], found[:, width : 2 * width], bias
+        )
+        out[start * STRIP : (start + rows) * STRIP] = finish(
+            mixed.astype(jnp.bfloat16), mine[start : start + rows].reshape(count, width), w_out[...], modulation[...]
+        )
+
+
+def own_kernel(normed, w_qkv, out):
+    out[...] = jnp.dot(normed[...], w_qkv[...], preferred_element_type=jnp.float32).astype(jnp.bfloat16)
+
+
+def head_marks(width):
+    feature, lane = iota((width, LANES), 0), iota((width, LANES), 1)
+    head = width // HEADS
+    return jnp.where((feature >= lane * head) & (feature < lane * head + head), 1.0, 0.0).astype(jnp.bfloat16)
+
+
+def mark_heads(width):
+    row, feature = iota((2 * LANES, width), 0) % LANES, iota((2 * LANES, width), 1)
+    head = width // HEADS
+    return jnp.where((feature >= row * head) & (feature < row * head + head), 1.0, 0.0).astype(jnp.bfloat16)
+
+
+def halves_of(values):
+    high = values.astype(jnp.bfloat16)
+    low = (values - high.astype(jnp.float32)).astype(jnp.bfloat16)
+    return high, low
+
+
+def temporal(own, other_kv):
+    width = own.shape[1] // 3
+    scale = (width // HEADS) ** (-0.5)
+    query = own[:, :width].astype(jnp.float32)
+    key_gap = other_kv[:, :width].astype(jnp.float32) - own[:, width : 2 * width].astype(jnp.float32)
+    high, low = halves_of(query * key_gap)
+    marks = head_marks(width)
+    gap = (
+        jnp.dot(high, marks, preferred_element_type=jnp.float32)
+        + jnp.dot(low, marks, preferred_element_type=jnp.float32)
+    ) * scale
+    own_weight = jnp.exp(jnp.minimum(-gap, 0.0))
+    other_weight = jnp.exp(jnp.minimum(gap, 0.0))
+    inverse = 1.0 / (own_weight + other_weight)
+    spread = mark_heads(width)
+
+    def share(weight):
+        part = weight.astype(jnp.bfloat16).astype(jnp.float32) * inverse
+        return jnp.dot(jnp.concatenate(halves_of(part), axis=1), spread, preferred_element_type=jnp.float32)
+
+    mixed = share(own_weight) * own[:, 2 * width :].astype(jnp.float32) + share(other_weight) * other_kv[
+        :, width:
+    ].astype(jnp.float32)
+    return mixed
+
+
+def temporal_kernel(own, other, w_qkv, out):
+    width = other.shape[1]
+    other_kv = jnp.dot(other[...], w_qkv[:, width:], preferred_element_type=jnp.float32).astype(jnp.bfloat16)
+    out[...] = temporal(own[...], other_kv).astype(jnp.bfloat16)
+
+
+def last_kernel(own, other, w_qkv, inner, rim, out, mixed_ref):
+    tile_rows, tile_cols, width = out.shape[1:]
+    other_kv = jnp.dot(other[...], w_qkv[:, width:], preferred_element_type=jnp.float32).astype(jnp.bfloat16)
+    edge = temporal(own[...], other_kv)
+    strips = tile_cols // STRIP - 1
+    for row in range(tile_rows):
+        if row < RADIUS:
+            source, at = rim, row
+        elif row < tile_rows - RADIUS:
+            source, at = inner, row - RADIUS
+        else:
+            source, at = rim, row - tile_rows + 2 * RADIUS
+        mixed_ref[row, 0:EDGE] = edge[STRIP * row : STRIP * row + EDGE]
+        mixed_ref[row, tile_cols - EDGE :] = edge[STRIP * row + EDGE : STRIP * row + STRIP]
+        for strip in range(strips):
+            piece = source[strip, STRIP * at : STRIP * at + STRIP, :].astype(jnp.float32)
+            mixed_ref[row, EDGE + STRIP * strip : EDGE + STRIP * strip + STRIP] = piece
+    out[0] = mixed_ref[...].astype(jnp.bfloat16)
+
+
+def call(body, out_shape, operands, scratch=(), flops=0, limit=32):
+    size = sum(x.size * x.dtype.itemsize for x in operands)
+    return pl.pallas_call(
+        body,
+        out_shape=out_shape,
+        in_specs=[VMEM] * len(operands),
+        out_specs=VMEM,
+        scratch_shapes=list(scratch),
+        cost_estimate=pl.CostEstimate(flops=flops, bytes_accessed=size, transcendentals=0),
+        compiler_params=pltpu.CompilerParams(vmem_limit_bytes=limit * MIB),
+        name=body.__name__,
+    )(*operands)
+
+
+def fast_device(resid, spatial_qkv, key_keep, w_spatial_out, modulation, w_temporal_qkv):
+    frame_count, tile_rows, tile_cols, width = resid.shape
+    qkv = spatial_qkv[:, 0]
+    keep = jnp.broadcast_to(key_keep.astype(jnp.bfloat16)[..., None], key_keep.shape + (LANES,))
+    strips = tile_cols // STRIP - 1
+    row_count, col_count = lax.axis_size("row"), lax.axis_size("col")
+    rising = lambda count: [(i, i + 1) for i in range(count - 1)]
+    falling = lambda count: [(i + 1, i) for i in range(count - 1)]
+    swap = [(0, 1), (1, 0)]
+    bf16 = jnp.bfloat16
+
+    def border(rows):
+        return jnp.concatenate([qkv[1, rows], qkv[2, rows], keep[0, rows]], axis=-1)[None]
+
+    above = lax.ppermute(border(slice(tile_rows - RADIUS, None)), "row", rising(row_count))
+    below = lax.ppermute(border(slice(0, RADIUS)), "row", falling(row_count))
+
+    half = (tile_rows - 2 * RADIUS) * STRIP
+    inner = call(
+        inner_kernel,
+        jax.ShapeDtypeStruct((strips, half, width), bf16),
+        (qkv, keep, resid, w_spatial_out, modulation),
+        [pltpu.VMEM((strips, half, width), bf16)],
+        flops=10**9,
+    )
+    inner_other = lax.ppermute(inner, "tm", swap)
+
+    def side(cols):
+        local = jnp.concatenate([qkv[1, :, cols], qkv[2, :, cols], keep[0, :, cols]], axis=-1)
+        return jnp.concatenate([above[0, :, cols], local, below[0, :, cols]], axis=0)[None]
+
+    left = lax.ppermute(side(slice(tile_cols - RADIUS, None)), "col", rising(col_count))
+    right = lax.ppermute(side(slice(0, RADIUS)), "col", falling(col_count))
+
+    rim_half = 2 * RADIUS * STRIP
+    rim = call(
+        rim_kernel,
+        jax.ShapeDtypeStruct((strips, rim_half, width), bf16),
+        (qkv, keep, above, below, resid, w_spatial_out, modulation),
+        [pltpu.VMEM((strips, rim_half, width), bf16)],
+        flops=10**9,
+    )
+    rim_other = lax.ppermute(rim, "tm", swap)
+
+    edge_count = tile_rows * STRIP
+    edge = call(
+        edge_kernel,
+        jax.ShapeDtypeStruct((edge_count, width), bf16),
+        (qkv, keep, above, below, left, right, resid, w_spatial_out, modulation),
+        [
+            pltpu.VMEM((tile_rows + 2 * RADIUS, 3 * STRIP, 2 * width + LANES), jnp.float32),
+            pltpu.VMEM((tile_rows, STRIP, width), jnp.float32),
+            pltpu.VMEM((tile_rows, STRIP, width), jnp.float32),
+        ],
+        flops=10**9,
+    )
+    edge_other = lax.ppermute(edge, "tm", swap)
+
+    def own(normed):
+        count = normed.shape[0]
+        return call(
+            own_kernel,
+            jax.ShapeDtypeStruct((count, 3 * width), bf16),
+            (normed, w_temporal_qkv),
+            flops=count * width * width * 6,
+        )
+
+    def attend(own_qkv, other):
+        count = other.shape[0]
+        return call(
+            temporal_kernel,
+            jax.ShapeDtypeStruct((count, width), bf16),
+            (own_qkv, other, w_temporal_qkv),
+            flops=count * width * width * 4,
+        )
+
+    flat = lambda x: x.reshape(-1, width)
+    inner_own, rim_own, edge_own = own(flat(inner)), own(flat(rim)), own(edge)
+    inner_done = attend(inner_own, flat(inner_other)).reshape(inner.shape)
+    rim_done = attend(rim_own, flat(rim_other)).reshape(rim.shape)
+    return call(
+        last_kernel,
+        jax.ShapeDtypeStruct(resid.shape, bf16),
+        (edge_own, edge_other, w_temporal_qkv, inner_done, rim_done),
+        [pltpu.VMEM((tile_rows, tile_cols, width), jnp.float32)],
+        flops=edge_count * width * width * 4,
+    )
+
+
+def per_device(resid, *rest):
+    frame_count, tile_rows, tile_cols, width = resid.shape
+    fits = (
+        frame_count == 1
+        and lax.axis_size("tm") == 2
+        and width == 9 * LANES
+        and tile_cols % STRIP == 0
+        and tile_cols >= 2 * STRIP
+        and tile_rows % 4 == 0
+        and tile_rows > 2 * RADIUS
+    )
+    return (fast_device if fits else general_device)(resid, *rest)
+
+
 def solution(mesh):
     return jax.shard_map(
         per_device,

time: 201 us -> 66.5 us (0.33)
  local copies, waits for them, and re-layouts: 64.9 us -> 4.02 us
  matrix products: 51.9 us -> 0 us
  Pallas kernels: 0 us -> 45.4 us
  blocking collectives: 34.3 us -> 0 us
  other arithmetic: 17 us -> 0.43 us
  waiting for transfers between devices: 9.56 us -> 0.24 us
  starting transfers between devices: 21.8 us -> 16 us
    pallas_call x0 -> x9, Pallas kernels: none -> 45.4 us  [call(): pl.pallas_call(body, out_shape=out_shape, in_specs=[VMEM] * len(operands)...]
    another operation x4 -> x0, local copies, waits for them, and re-layouts: 35.1 us -> none
    all_to_all x2 -> x0, blocking collectives: 34.3 us -> none  [the longest x1 17.1 us: per_device(): lax.all_to_all(normed_parts, 'tm', split_axis=1, concat_axis=0, tiled=True)]
    dot_general x5 -> x0, matrix products: 33.4 us -> none  [the longest x1 9.09 us: per_device(): jnp.einsum('fhqk,fkhd->fqhd', weights_b, values_pad, preferred_element_ty...]
    sub x1 -> x0, matrix products: 18.5 us -> none  [softmax_parts(): weights_f = jnp.where(allowed, jnp.exp(masked - top_score), 0.0)]
    slice x10 -> x2, local copies, waits for them, and re-layouts: 16.2 us -> 0.08 us  [the longest x1 0.07 us: side(): keep[0, :, cols]]
    ppermute x8 -> x7, waiting for transfers between devices: 9.56 us -> 0.24 us  [the longest x1 0.22 us: fast_device(): edge_other = lax.ppermute(edge, 'tm', swap)]
    reduce_sum x2 -> x0, other arithmetic: 7.38 us -> none  [the longest x1 7.02 us: softmax_parts(): return (weights_f.astype(jnp.bfloat16), jnp.sum(weights_f, -1))]
  transfers between devices with their start and end apart: 8 -> 7, of which waited for: 2 -> 1; matrix products, arithmetic and copies ran while one was open for 7% -> 2% of each run, Pallas kernels for 0% -> 64%
where the time goes in v1:
time: 66.5 us; the launch traced here: 66.3 us
  Pallas kernels  45.4 us (68%)
  starting transfers between devices  16 us (24%)
  local copies, waits for them, and re-layouts  4.02 us (6%)
    pallas_call x9, Pallas kernels, call(): pl.pallas_call(body, out_shape=out_shape, in_specs=[VMEM] * len(operands)...  45.4 us
    ppermute x1, starting transfers between devices, fast_device(): lax.ppermute(side(slice(tile_cols - RADIUS, None)), 'col', rising(col_cou...  4.75 us
    ppermute x1, starting transfers between devices, fast_device(): lax.ppermute(border(slice(tile_rows - RADIUS, None)), 'row', rising(row_c...  3.07 us
    ppermute x1, starting transfers between devices, fast_device(): inner_other = lax.ppermute(inner, 'tm', swap)  3 us
    ppermute x1, starting transfers between devices, fast_device(): edge_other = lax.ppermute(edge, 'tm', swap)  1.98 us
    unnamed x18, local copies, waits for them, and re-layouts  1.79 us
    ppermute x1, starting transfers between devices, fast_device(): right = lax.ppermute(side(slice(0, RADIUS)), 'col', falling(col_count))  1.56 us
    squeeze x1, local copies, waits for them, and re-layouts, border(): qkv[1, rows]  1.45 us
  transfers between devices with their start and end apart: 7, of which 1 were waited for; matrix products, arithmetic and copies ran while one was open for 2% of the time, Pallas kernels for 64%

profile of v1, /device:TPU:0, one launch (start us, length us, event | category | flops | bytes accessed | tf_op | source)
XLA Modules:
  0.0 66.3 jit_solution(4713231668869126199)
XLA Ops:
  0.0 0.0 copy-start.5
  0.0 1.4 %slice_bitcast_fusion.1 = (bf16[3,40,1152]{2,1,0:T(8,128)(2,1)S(1)}, bf16[3,40,1152]{2,1,0:T(8,128)(2,1)S(1)}, bf16[3,40,1152]{2,1,0:T(8,128)(2,1)S(1)}, bf16[3,40,1152]{2,1,0:T(8,128)(2,1)S(1)}) fusion(bf16[3,12,40,1152]{3,2,1,0:T(8,128)(2,1)} %bitcast.48), kind=kLoop, calls=%fused_computation.5 | loop fusion | bytes 2211840 | tf_op jit(solution)/shard_map/squeeze | solution.py:424
  1.5 0.0 copy-done.5
  1.5 0.1 squeeze.57
  1.6 0.0 copy-start.3
  1.6 0.0 copy-start.4
  1.7 1.4 %collective-permute-start.1 = (bf16[1,3,40,2432]{3,2,1,0:T(8,128)(2,1)S(1)}, bf16[1,3,40,2432]{3,2,1,0:T(8,128)(2,1)S(1)}, u32[]{:S(2)}, u32[]{:S(2)}) collective-permute-start(bf16[1,3,40,2432]{3,2,1,0:T(8,128)(2,1)S(1)} %maximum_bitcast_fusion.1), channel_id=1, source_target_pairs={{4,0},{8,4},{12,8},{5,1},{9,5},{13,9},{6,2},{10,6},{14,10},{7,3},{... | collective-permute-start | bytes 1751048 | tf_op jit(solution)/shard_map/ppermute | solution.py:427
  3.1 0.1 squeeze.54
  3.3 3.1 %collective-permute-start = (bf16[1,3,40,2432]{3,2,1,0:T(8,128)(2,1)S(1)}, bf16[1,3,40,2432]{3,2,1,0:T(8,128)(2,1)S(1)}, u32[]{:S(2)}, u32[]{:S(2)}) collective-permute-start(bf16[1,3,40,2432]{3,2,1,0:T(8,128)(2,1)S(1)} %maximum_bitcast_fusion), channel_id=1, source_target_pairs={{0,4},{4,8},{8,12},{1,5},{5,9},{9,13},{2,6},{6,10},{10,14},{3,7},{... | collective-permute-start | bytes 1751048 | tf_op jit(solution)/shard_map/ppermute | solution.py:426
  6.3 0.1 broadcast_in_dim.21.keep
  6.5 0.0 copy-done
  6.5 0.0 copy-done.3
  6.5 0.0 copy-done.4
  6.5 0.0 copy-start.1
  6.5 1.7 %copy-done.1 = bf16[1152,1152]{1,0:T(8,128)(2,1)S(1)} copy-done((bf16[1152,1152]{1,0:T(8,128)(2,1)S(1)}, bf16[1152,1152]{1,0:T(8,128)(2,1)}, u32[]{:S(2)}) %copy-start.1) | copy-done | bytes 2654232
  8.3 9.4 %inner_kernel.1 = bf16[4,48,1152]{2,1,0:T(8,128)(2,1)S(1)} custom-call(bf16[3,12,40,1152]{3,2,1,0:T(8,128)(2,1)S(1)} %bitcast.49, bf16[1,12,40,128]{3,2,1,0:T(8,128)(2,1)S(1)} %broadcast_in_dim.21.keep, bf16[1,12,40,1152]{3,2,1,0:T(8,128)(2,1)S(1)} %copy-done.3, bf16[1152,1152]{1,0:T(8,128)(2,1)S(1)} %copy-done.1, f32[2,1152]{1,0:T(2,128)S(1)} %copy-done.4), custom_call_target="tpu_custom_call" | custom-call | flops 1000000000 | bytes 7209984 | tf_op jit(solution)/shard_map/inner_kernel/pallas_call | solution.py:400
  17.7 3.0 %collective-permute-start.5 = (bf16[4,48,1152]{2,1,0:T(8,128)(2,1)S(1)}, bf16[4,48,1152]{2,1,0:T(8,128)(2,1)S(1)}, u32[]{:S(2)}, u32[]{:S(2)}) collective-permute-start(bf16[4,48,1152]{2,1,0:T(8,128)(2,1)S(1)} %inner_kernel.1), channel_id=1, source_target_pairs={{0,16},{16,0},{1,17},{17,1},{2,18},{18,2},{3,19},{19,3},{4,20},{20... | collective-permute-start | bytes 1327112 | tf_op jit(solution)/shard_map/ppermute | solution.py:437
  20.7 0.1 fusion.1
  20.8 0.2 slice_bitcast_fusion.5
  20.9 0.0 collective-permute-done.1.below
  20.9 0.1 slice_bitcast_fusion.8
  21.0 0.0 collective-permute-done.above
  21.0 0.1 slice_bitcast_fusion.9
  21.1 0.1 squeeze.66
  21.1 0.0 slice-start.1
  21.2 0.2 maximum_bitcast_fusion.3
  21.3 1.6 %collective-permute-start.3 = (bf16[1,18,3,2432]{3,2,1,0:T(4,128)(2,1)S(1)}, bf16[1,18,3,2432]{3,2,1,0:T(4,128)(2,1)S(1)}, u32[]{:S(2)}, u32[]{:S(2)}) collective-permute-start(bf16[1,18,3,2432]{3,2,1,0:T(4,128)(2,1)S(1)} %maximum_bitcast_fusion.3), channel_id=1, source_target_pairs={{1,0},{2,1},{3,2},{5,4},{6,5},{7,6},{9,8},{10,9},{11,10},{13,12},{... | collective-permute-start | bytes 787976 | tf_op jit(solution)/shard_map/ppermute | solution.py:444
  22.9 0.1 squeeze.61
  23.0 0.2 maximum_bitcast_fusion.2
  23.1 4.7 %collective-permute-start.2 = (bf16[1,18,3,2432]{3,2,1,0:T(4,128)(2,1)S(1)}, bf16[1,18,3,2432]{3,2,1,0:T(4,128)(2,1)S(1)}, u32[]{:S(2)}, u32[]{:S(2)}) collective-permute-start(bf16[1,18,3,2432]{3,2,1,0:T(4,128)(2,1)S(1)} %maximum_bitcast_fusion.2), channel_id=1, source_target_pairs={{0,1},{1,2},{2,3},{4,5},{5,6},{6,7},{8,9},{9,10},{10,11},{12,13},{... | collective-permute-start | bytes 787976 | tf_op jit(solution)/shard_map/ppermute | solution.py:443
  27.9 0.0 copy-done.2
  27.9 15.6 %rim_kernel.1 = bf16[4,48,1152]{2,1,0:T(8,128)(2,1)S(1)} custom-call(bf16[3,12,40,1152]{3,2,1,0:T(8,128)(2,1)S(1)} %bitcast.51, bf16[1,12,40,128]{3,2,1,0:T(8,128)(2,1)S(1)} %broadcast_in_dim.21.keep, bf16[1,3,40,2432]{3,2,1,0:T(8,128)(2,1)S(1)} %collective-permute-done.above, bf16[1,3,40,2432]{3,2,1,0:T(8,128)(2,1)S(1)} %collective-permute-done.1.below, ...), custom_call_target="tpu_custom_call" | custom-call | flops 1000000000 | bytes 8377344 | tf_op jit(solution)/shard_map/rim_kernel/pallas_call | solution.py:400
  43.5 0.2 collective-permute-start.6
  43.7 0.0 slice-done
  43.7 0.0 slice-done.1
  43.7 1.9 %own_kernel.4.own = bf16[192,3456]{1,0:T(8,128)(2,1)S(1)} custom-call(bf16[192,1152]{1,0:T(8,128)(2,1)S(1)} %bitcast.53, bf16[1152,3456]{1,0:T(8,128)(2,1)S(1)} %bitcast.47), custom_call_target="tpu_custom_call" | custom-call | flops 1528823808 | bytes 8404992 | tf_op jit(solution)/shard_map/own_kernel/pallas_call | solution.py:400
  45.6 0.0 collective-permute-done.5
  45.7 2.3 %temporal_kernel.2 = bf16[192,1152]{1,0:T(8,128)(2,1)S(1)} custom-call(bf16[192,3456]{1,0:T(8,128)(2,1)S(1)} %own_kernel.4.own, bf16[192,1152]{1,0:T(8,128)(2,1)S(1)} %bitcast.57, bf16[1152,3456]{1,0:T(8,128)(2,1)S(1)} %bitcast.47), custom_call_target="tpu_custom_call" | custom-call | flops 1019215872 | bytes 9732096 | tf_op jit(solution)/shard_map/temporal_kernel/pallas_call | solution.py:400
  48.0 0.0 collective-permute-done.3.right
  48.0 0.0 collective-permute-done.2.left
  48.0 7.5 %edge_kernel.1.normed = bf16[96,1152]{1,0:T(8,128)(2,1)S(1)} custom-call(bf16[3,12,40,1152]{3,2,1,0:T(8,128)(2,1)S(1)} %bitcast.52, bf16[1,12,40,128]{3,2,1,0:T(8,128)(2,1)S(1)} %broadcast_in_dim.21.keep, bf16[1,3,40,2432]{3,2,1,0:T(8,128)(2,1)S(1)} %collective-permute-done.above, bf16[1,3,40,2432]{3,2,1,0:T(8,128)(2,1)S(1)} %collective-permute-done.1.below, ...), custom_call_target="tpu_custom_call" | custom-call | flops 1000000000 | bytes 8902656 | tf_op jit(solution)/shard_map/edge_kernel/pallas_call | solution.py:400
  55.6 2.0 %collective-permute-start.4 = (bf16[96,1152]{1,0:T(8,128)(2,1)S(1)}, bf16[96,1152]{1,0:T(8,128)(2,1)S(1)}, u32[]{:S(2)}, u32[]{:S(2)}) collective-permute-start(bf16[96,1152]{1,0:T(8,128)(2,1)S(1)} %edge_kernel.1.normed), channel_id=1, source_target_pairs={{0,16},{16,0},{1,17},{17,1},{2,18},{18,2},{3,19},{19,3},{4,20},{20... | collective-permute-start | bytes 663560 | tf_op jit(solution)/shard_map/ppermute | solution.py:468
  57.5 1.9 %own_kernel.5.own = bf16[192,3456]{1,0:T(8,128)(2,1)S(1)} custom-call(bf16[192,1152]{1,0:T(8,128)(2,1)S(1)} %bitcast.55, bf16[1152,3456]{1,0:T(8,128)(2,1)S(1)} %bitcast.47), custom_call_target="tpu_custom_call" | custom-call | flops 1528823808 | bytes 8404992 | tf_op jit(solution)/shard_map/own_kernel/pallas_call | solution.py:400
  59.5 1.3 %own_kernel.3.own = bf16[96,3456]{1,0:T(8,128)(2,1)S(1)} custom-call(bf16[96,1152]{1,0:T(8,128)(2,1)S(1)} %edge_kernel.1.normed, bf16[1152,3456]{1,0:T(8,128)(2,1)S(1)} %bitcast.47), custom_call_target="tpu_custom_call" | custom-call | flops 764411904 | bytes 8183808 | tf_op jit(solution)/shard_map/own_kernel/pallas_call | solution.py:400
  60.8 0.0 collective-permute-done.6
  60.8 2.3 %temporal_kernel.3 = bf16[192,1152]{1,0:T(8,128)(2,1)S(1)} custom-call(bf16[192,3456]{1,0:T(8,128)(2,1)S(1)} %own_kernel.5.own, bf16[192,1152]{1,0:T(8,128)(2,1)S(1)} %bitcast.58, bf16[1152,3456]{1,0:T(8,128)(2,1)S(1)} %bitcast.47), custom_call_target="tpu_custom_call" | custom-call | flops 1019215872 | bytes 9732096 | tf_op jit(solution)/shard_map/temporal_kernel/pallas_call | solution.py:400
  63.2 0.2 collective-permute-done.4.other
  63.4 2.9 %last_kernel.1 = bf16[1,12,40,1152]{3,2,1,0:T(8,128)(2,1)} custom-call(bf16[96,3456]{1,0:T(8,128)(2,1)S(1)} %own_kernel.3.own, bf16[96,1152]{1,0:T(8,128)(2,1)S(1)} %collective-permute-done.4.other, bf16[1152,3456]{1,0:T(8,128)(2,1)S(1)} %bitcast.47, bf16[4,48,1152]{2,1,0:T(8,128)(2,1)S(1)} %bitcast.54, bf16[4,48,1152]{2,1,0:T(8,128)(2,1)S(1)} %bitcast.56), custom_call_target="tpu_custom_call" | custom-call | flops 509607936 | bytes 9732096 | tf_op jit(solution)/shard_map/last_kernel/pallas_call | solution.py:400
  (10 shorter events, 0.1 us)
Async XLA Ops:
  0.0 1.5 %copy-start.5 = (s32[1,12,40]{2,0,1:T(1,128)S(1)}, s32[1,12,40]{2,0,1:T(1,128)}, u32[]{:S(2)}) copy-start(s32[1,12,40]{2,0,1:T(1,128)} %param.8) | copy-start | bytes 5764
  0.0 6.5 %copy-start = (bf16[3,1,12,40,1152]{4,3,2,1,0:T(8,128)(2,1)S(1)}, bf16[3,1,12,40,1152]{4,3,2,1,0:T(8,128)(2,1)}, u32[]{:S(2)}) copy-start(bf16[3,1,12,40,1152]{4,3,2,1,0:T(8,128)(2,1)} %param.7) | copy-start | bytes 9953284
  1.6 4.9 %copy-start.3 = (bf16[1,12,40,1152]{3,2,1,0:T(8,128)(2,1)S(1)}, bf16[1,12,40,1152]{3,2,1,0:T(8,128)(2,1)}, u32[]{:S(2)}) copy-start(bf16[1,12,40,1152]{3,2,1,0:T(8,128)(2,1)} %resid.5) | copy-start | bytes 3317764
  1.6 4.9 %copy-start.4 = (f32[2,1152]{1,0:T(2,128)S(1)}, f32[2,1152]{1,0:T(2,128)}, u32[]{:S(2)}) copy-start(f32[2,1152]{1,0:T(2,128)} %modulation.5) | copy-start | bytes 27652
  1.7 19.3 %collective-permute-start.1 = (bf16[1,3,40,2432]{3,2,1,0:T(8,128)(2,1)S(1)}, bf16[1,3,40,2432]{3,2,1,0:T(8,128)(2,1)S(1)}, u32[]{:S(2)}, u32[]{:S(2)}) collective-permute-start(bf16[1,3,40,2432]{3,2,1,0:T(8,128)(2,1)S(1)} %maximum_bitcast_fusion.1), channel_id=1, source_target_pairs={{4,0},{8,4},{12,8},{5,1},{9,5},{13,9},{6,2},{10,6},{14,10},{7,3},{... | collective-permute-start | bytes 1751048 | tf_op jit(solution)/shard_map/ppermute | solution.py:427
  3.3 17.8 %collective-permute-start = (bf16[1,3,40,2432]{3,2,1,0:T(8,128)(2,1)S(1)}, bf16[1,3,40,2432]{3,2,1,0:T(8,128)(2,1)S(1)}, u32[]{:S(2)}, u32[]{:S(2)}) collective-permute-start(bf16[1,3,40,2432]{3,2,1,0:T(8,128)(2,1)S(1)} %maximum_bitcast_fusion), channel_id=1, source_target_pairs={{0,4},{4,8},{8,12},{1,5},{5,9},{9,13},{2,6},{6,10},{10,14},{3,7},{... | collective-permute-start | bytes 1751048 | tf_op jit(solution)/shard_map/ppermute | solution.py:426
  6.5 1.8 %copy-start.1 = (bf16[1152,1152]{1,0:T(8,128)(2,1)S(1)}, bf16[1152,1152]{1,0:T(8,128)(2,1)}, u32[]{:S(2)}) copy-start(bf16[1152,1152]{1,0:T(8,128)(2,1)} %w_out.5) | copy-start | bytes 7962628
  8.3 35.5 %slice-start = ((s8[7962624]{0:T(1024)(128)(4,1)}), s8[4194304]{0:T(1024)(128)(4,1)S(1)}, s32[]{:S(2)}) async-start(s8[7962624]{0:T(1024)(128)(4,1)} %bitcast.46), calls=%async_computation | async-start | bytes 8388608
  17.7 28.0 %collective-permute-start.5 = (bf16[4,48,1152]{2,1,0:T(8,128)(2,1)S(1)}, bf16[4,48,1152]{2,1,0:T(8,128)(2,1)S(1)}, u32[]{:S(2)}, u32[]{:S(2)}) collective-permute-start(bf16[4,48,1152]{2,1,0:T(8,128)(2,1)S(1)} %inner_kernel.1), channel_id=1, source_target_pairs={{0,16},{16,0},{1,17},{17,1},{2,18},{18,2},{3,19},{19,3},{4,20},{20... | collective-permute-start | bytes 1327112 | tf_op jit(solution)/shard_map/ppermute | solution.py:437
  20.8 7.1 %copy-start.2 = (bf16[1152,1152]{1,0:T(8,128)(2,1)S(1)}, bf16[1152,1152]{1,0:T(8,128)(2,1)}, u32[]{:S(2)}) copy-start(bf16[1152,1152]{1,0:T(8,128)(2,1)} %w_out.5) | copy-start | bytes 7962628
  21.1 22.6 %slice-start.1 = ((s8[7962624]{0:T(1024)(128)(4,1)}), s8[3768320]{0:T(1024)(128)(4,1)S(1)}, s32[]{:S(2)}) async-start(s8[7962624]{0:T(1024)(128)(4,1)} %bitcast.46), calls=%async_computation.1 | async-start | bytes 7536640
  21.3 26.7 %collective-permute-start.3 = (bf16[1,18,3,2432]{3,2,1,0:T(4,128)(2,1)S(1)}, bf16[1,18,3,2432]{3,2,1,0:T(4,128)(2,1)S(1)}, u32[]{:S(2)}, u32[]{:S(2)}) collective-permute-start(bf16[1,18,3,2432]{3,2,1,0:T(4,128)(2,1)S(1)} %maximum_bitcast_fusion.3), channel_id=1, source_target_pairs={{1,0},{2,1},{3,2},{5,4},{6,5},{7,6},{9,8},{10,9},{11,10},{13,12},{... | collective-permute-start | bytes 787976 | tf_op jit(solution)/shard_map/ppermute | solution.py:444
  23.1 24.9 %collective-permute-start.2 = (bf16[1,18,3,2432]{3,2,1,0:T(4,128)(2,1)S(1)}, bf16[1,18,3,2432]{3,2,1,0:T(4,128)(2,1)S(1)}, u32[]{:S(2)}, u32[]{:S(2)}) collective-permute-start(bf16[1,18,3,2432]{3,2,1,0:T(4,128)(2,1)S(1)} %maximum_bitcast_fusion.2), channel_id=1, source_target_pairs={{0,1},{1,2},{2,3},{4,5},{5,6},{6,7},{8,9},{9,10},{10,11},{12,13},{... | collective-permute-start | bytes 787976 | tf_op jit(solution)/shard_map/ppermute | solution.py:443
  43.5 17.3 %collective-permute-start.6 = (bf16[4,48,1152]{2,1,0:T(8,128)(2,1)S(1)}, bf16[4,48,1152]{2,1,0:T(8,128)(2,1)S(1)}, u32[]{:S(2)}, u32[]{:S(2)}) collective-permute-start(bf16[4,48,1152]{2,1,0:T(8,128)(2,1)S(1)} %rim_kernel.1), channel_id=1, source_target_pairs={{0,16},{16,0},{1,17},{17,1},{2,18},{18,2},{3,19},{19,3},{4,20},{20... | collective-permute-start | bytes 1327112 | tf_op jit(solution)/shard_map/ppermute | solution.py:454
  55.6 7.8 %collective-permute-start.4 = (bf16[96,1152]{1,0:T(8,128)(2,1)S(1)}, bf16[96,1152]{1,0:T(8,128)(2,1)S(1)}, u32[]{:S(2)}, u32[]{:S(2)}) collective-permute-start(bf16[96,1152]{1,0:T(8,128)(2,1)S(1)} %edge_kernel.1.normed), channel_id=1, source_target_pairs={{0,16},{16,0},{1,17},{17,1},{2,18},{18,2},{3,19},{19,3},{4,20},{20... | collective-permute-start | bytes 663560 | tf_op jit(solution)/shard_map/ppermute | solution.py:468

commit v2 on v1

--- a/solution.py
+++ b/solution.py
@@ -130,45 +130,51 @@
     return lax.broadcasted_iota(jnp.int32, shape, dim)
 
 
-def tile_attend(queries, keys, values, bias):
-    count, width = queries.shape
+def attend(tiles):
+    width = tiles[0][0].shape[1]
     head = width // HEADS
     factor = head ** (-0.5) * math.log2(math.e)
     lane = iota((1, 2 * LANES), 1)
-    bias_two = jnp.concatenate([bias, bias], axis=0)
-    pairs = []
+    spans = []
     for pair in range(HEADS // 2):
         start = LANES * pair
         low = 2 * head * pair - start
-        mid, high = low + head, low + 2 * head
-        window = queries[:, start : start + 2 * LANES]
-        first = jnp.where((lane >= low) & (lane < mid), window, 0.0)
-        second = jnp.where((lane >= mid) & (lane < high), window, 0.0)
-        both = jnp.concatenate([first, second], axis=0).astype(jnp.bfloat16)
-        scores = lax.dot_general(
-            both,
-            keys[:, start : start + 2 * LANES],
-            (((1,), (1,)), ((), ())),
-            preferred_element_type=jnp.float32,
-        )
-        scores = scores + bias_two
-        top = jnp.max(scores, -1, keepdims=True)
-        weights = jnp.exp2((scores - top) * factor)
-        total = jnp.sum(weights, -1, keepdims=True)
-        mixed = jnp.dot(
-            weights.astype(jnp.bfloat16),
-            values[:, start : start + 2 * LANES],
-            preferred_element_type=jnp.float32,
-        )
-        mixed = mixed / total
-        pairs.append(jnp.where(lane < mid, mixed[:count], mixed[count:]))
-    lane = iota((1, LANES), 1)
-    blocks = [pairs[0][:, :LANES]]
-    for pair in range(1, HEADS // 2):
-        cut = 2 * head * pair - LANES * pair
-        blocks.append(jnp.where(lane < cut, pairs[pair - 1][:, LANES:], pairs[pair][:, :LANES]))
-    blocks.append(pairs[-1][:, LANES:])
-    return jnp.concatenate(blocks, axis=1)
+        spans.append((slice(start, start + 2 * LANES), low, low + head, low + 2 * head))
+    scores = []
+    for queries, keys, values, bias in tiles:
+        for span, low, mid, high in spans:
+            first = jnp.where((lane >= low) & (lane < mid), queries[:, span], 0.0)
+            second = jnp.where((lane >= mid) & (lane < high), queries[:, span], 0.0)
+            both = jnp.concatenate([first, second], axis=0).astype(jnp.bfloat16)
+            scores.append(
+                lax.dot_general(
+                    both, keys[:, span], (((1,), (1,)), ((), ())), preferred_element_type=jnp.float32
+                )
+            )
+    weights = []
+    for index, (queries, keys, values, bias) in enumerate(tiles):
+        bias_two = jnp.concatenate([bias, bias], axis=0)
+        for pair in range(len(spans)):
+            score = scores[index * len(spans) + pair] + bias_two
+            top = jnp.max(score, -1, keepdims=True)
+            weight = jnp.exp2((score - top) * factor)
+            weights.append((weight.astype(jnp.bfloat16), 1.0 / jnp.sum(weight, -1, keepdims=True)))
+    results = []
+    edge_lane = iota((1, LANES), 1)
+    for index, (queries, keys, values, bias) in enumerate(tiles):
+        count = queries.shape[0]
+        pairs = []
+        for pair, (span, low, mid, high) in enumerate(spans):
+            weight, inverse = weights[index * len(spans) + pair]
+            mixed = jnp.dot(weight, values[:, span], preferred_element_type=jnp.float32) * inverse
+            pairs.append(jnp.where(lane < mid, mixed[:count], mixed[count:]))
+        blocks = [pairs[0][:, :LANES]]
+        for pair in range(1, len(spans)):
+            cut = spans[pair][1]
+            blocks.append(jnp.where(edge_lane < cut, pairs[pair - 1][:, LANES:], pairs[pair][:, :LANES]))
+        blocks.append(pairs[-1][:, LANES:])
+        results.append(jnp.concatenate(blocks, axis=1))
+    return results
 
 
 def keep_row(count, keep):
@@ -213,29 +219,53 @@
     return found.reshape(found.shape[0] * STRIP, found.shape[2])
 
 
+INNER_ROWS = 6
+INNER_BATCH = 4
+RIM_BATCH = 4
+EDGE_BATCH = 3
+
+
+def batched(tiles, size):
+    found = []
+    for start in range(0, len(tiles), size):
+        found += attend(tiles[start : start + size])
+    return found
+
+
 def inner_kernel(qkv, keep, resid, w_out, modulation, out, heads):
     tile_rows, tile_cols, width = resid.shape[1:]
     rows = tile_rows - 2 * RADIUS
     strips = tile_cols // STRIP - 1
     every = pl.ds(0, tile_rows)
     mine = pl.ds(RADIUS, rows)
+    step = INNER_ROWS
+    tiles = []
     for strip in range(strips):
-        bias = strip_bias(rows, window(keep, 0, every, strip))
-        mixed = tile_attend(
-            middle(qkv, 0, mine, strip), window(qkv, 1, every, strip), window(qkv, 2, every, strip), bias
-        )
-        heads[strip] = mixed.astype(jnp.bfloat16)
-        stream = finish(heads[strip], middle(resid, 0, mine, strip), w_out[...], modulation[...])
-        out[strip] = stream
+        queries = middle(qkv, 0, mine, strip)
+        keys, values, flags = (window(ref, plane, every, strip) for ref, plane in ((qkv, 1), (qkv, 2), (keep, 0)))
+        for start in range(0, rows, step):
+            span = slice(start * 2 * STRIP, (start + step + 2 * RADIUS) * 2 * STRIP)
+            tiles.append(
+                (
+                    queries[start * STRIP : (start + step) * STRIP],
+                    keys[span],
+                    values[span],
+                    strip_bias(step, flags[span]),
+                )
+            )
+    mixed = batched(tiles, INNER_BATCH * rows // step)
+    heads[...] = jnp.concatenate(mixed, axis=0).astype(jnp.bfloat16)
+    source = jnp.concatenate([middle(resid, 0, mine, strip) for strip in range(strips)], axis=0)
+    out[...] = finish(heads[...], source, w_out[...], modulation[...]).reshape(out.shape)
 
 
 def rim_kernel(qkv, keep, above, below, resid, w_out, modulation, out, heads):
     tile_rows, tile_cols, width = resid.shape[1:]
     strips = tile_cols // STRIP - 1
     near = 2 * RADIUS
+    tiles = []
+    sources = []
     for strip in range(strips):
-        halves = []
-        sources = []
         for side in range(2):
             inner = pl.ds(0 if side == 0 else tile_rows - near, near)
             mine = pl.ds(0 if side == 0 else tile_rows - RADIUS, RADIUS)
@@ -250,10 +280,10 @@
                 far = halo[:, at : at + local.shape[1]]
                 parts.append(jnp.concatenate([far, local] if side == 0 else [local, far], axis=0))
             bias = strip_bias(RADIUS, parts[2])
-            halves.append(tile_attend(middle(qkv, 0, mine, strip), parts[0], parts[1], bias))
+            tiles.append((middle(qkv, 0, mine, strip), parts[0], parts[1], bias))
             sources.append(middle(resid, 0, mine, strip))
-        heads[strip] = jnp.concatenate(halves, axis=0).astype(jnp.bfloat16)
-        out[strip] = finish(heads[strip], jnp.concatenate(sources, axis=0), w_out[...], modulation[...])
+    heads[...] = jnp.concatenate(batched(tiles, RIM_BATCH), axis=0).astype(jnp.bfloat16)
+    out[...] = finish(heads[...], jnp.concatenate(sources, axis=0), w_out[...], modulation[...]).reshape(out.shape)
 
 
 def edge_columns(ref, plane, row):
@@ -261,7 +291,7 @@
     return found[:STRIP], found[found.shape[0] - STRIP :]
 
 
-def edge_kernel(qkv, keep, above, below, left, right, resid, w_out, modulation, out, far, ends, mine):
+def edge_kernel(qkv, keep, above, below, left, right, resid, w_out, modulation, out, heads, far, ends, mine):
     tile_rows, tile_cols, width = resid.shape[1:]
     pad_rows = tile_rows + 2 * RADIUS
     far[...] = jnp.zeros_like(far)
@@ -286,6 +316,7 @@
             target[row, EDGE:STRIP] = tail[EDGE:]
     rows = 4
     span = 3 * STRIP
+    tiles = []
     for start in range(0, tile_rows, rows):
         count, keys = rows * STRIP, (rows + 2 * RADIUS) * span
         found = far[start : start + rows + 2 * RADIUS].reshape(keys, 2 * width + LANES).astype(jnp.bfloat16)
@@ -313,12 +344,13 @@
         bias = make_bias(
             q // STRIP + RADIUS, q_col, k // span, k_col, keep_row(count, found[:, 2 * width :])
         )
-        mixed = tile_attend(
-            ends[start : start + rows].reshape(count, width), found[:, :width], found[:, width : 2 * width], bias
+        tiles.append(
+            (ends[start : start + rows].reshape(count, width), found[:, :width], found[:, width : 2 * width], bias)
         )
-        out[start * STRIP : (start + rows) * STRIP] = finish(
-            mixed.astype(jnp.bfloat16), mine[start : start + rows].reshape(count, width), w_out[...], modulation[...]
-        )
+    mixed = batched(tiles, EDGE_BATCH)
+    source = mine[...].reshape(tile_rows * STRIP, width)
+    heads[...] = jnp.concatenate(mixed, axis=0).astype(jnp.bfloat16)
+    out[...] = finish(heads[...], source, w_out[...], modulation[...])
 
 
 def own_kernel(normed, w_qkv, out):
@@ -431,7 +463,7 @@
         inner_kernel,
         jax.ShapeDtypeStruct((strips, half, width), bf16),
         (qkv, keep, resid, w_spatial_out, modulation),
-        [pltpu.VMEM((strips, half, width), bf16)],
+        [pltpu.VMEM((strips * half, width), bf16)],
         flops=10**9,
     )
     inner_other = lax.ppermute(inner, "tm", swap)
@@ -448,7 +480,7 @@
         rim_kernel,
         jax.ShapeDtypeStruct((strips, rim_half, width), bf16),
         (qkv, keep, above, below, resid, w_spatial_out, modulation),
-        [pltpu.VMEM((strips, rim_half, width), bf16)],
+        [pltpu.VMEM((strips * rim_half, width), bf16)],
         flops=10**9,
     )
     rim_other = lax.ppermute(rim, "tm", swap)
@@ -459,6 +491,7 @@
         jax.ShapeDtypeStruct((edge_count, width), bf16),
         (qkv, keep, above, below, left, right, resid, w_spatial_out, modulation),
         [
+            pltpu.VMEM((edge_count, width), bf16),
             pltpu.VMEM((tile_rows + 2 * RADIUS, 3 * STRIP, 2 * width + LANES), jnp.float32),
             pltpu.VMEM((tile_rows, STRIP, width), jnp.float32),
             pltpu.VMEM((tile_rows, STRIP, width), jnp.float32),

time: 66.5 us -> 45.7 us (0.69)
  Pallas kernels: 45.4 us -> 22.3 us
  waiting for transfers between devices: 0.24 us -> 2.43 us
    pallas_call x9, Pallas kernels: 45.4 us -> 22.3 us  [call(): pl.pallas_call(body, out_shape=out_shape, in_specs=[VMEM] * len(operands)...]
    ppermute x1, waiting for transfers between devices: 0.22 us -> 1.72 us  [fast_device(): edge_other = lax.ppermute(edge, 'tm', swap)]
    ppermute x1, waiting for transfers between devices: 0.01 us -> 0.7 us  [fast_device(): rim_other = lax.ppermute(rim, 'tm', swap)]
  transfers between devices with their start and end apart: 7 -> 7, of which waited for: 1 -> 2; matrix products, arithmetic and copies ran while one was open for 2% -> 2% of each run, Pallas kernels for 64% -> 43%
where the time goes in v2:
time: 45.7 us; the launch traced here: 45.5 us
  Pallas kernels  22.3 us (49%)
  starting transfers between devices  16 us (35%)
  local copies, waits for them, and re-layouts  4.02 us (9%)
  waiting for transfers between devices  2.43 us (5%)
    pallas_call x9, Pallas kernels, call(): pl.pallas_call(body, out_shape=out_shape, in_specs=[VMEM] * len(operands)...  22.3 us
    ppermute x1, starting transfers between devices, fast_device(): lax.ppermute(side(slice(tile_cols - RADIUS, None)), 'col', rising(col_cou...  4.75 us
    ppermute x1, starting transfers between devices, fast_device(): lax.ppermute(border(slice(tile_rows - RADIUS, None)), 'row', rising(row_c...  3.07 us
    ppermute x1, starting transfers between devices, fast_device(): inner_other = lax.ppermute(inner, 'tm', swap)  3 us
    ppermute x1, starting transfers between devices, fast_device(): edge_other = lax.ppermute(edge, 'tm', swap)  1.99 us
    unnamed x18, local copies, waits for them, and re-layouts  1.79 us
    ppermute x1, waiting for transfers between devices, fast_device(): edge_other = lax.ppermute(edge, 'tm', swap)  1.72 us
    ppermute x1, starting transfers between devices, fast_device(): right = lax.ppermute(side(slice(0, RADIUS)), 'col', falling(col_count))  1.56 us
  transfers between devices with their start and end apart: 7, of which 2 were waited for; matrix products, arithmetic and copies ran while one was open for 2% of the time, Pallas kernels for 43%

profile of v2, /device:TPU:0, one launch (start us, length us, event | category | flops | bytes accessed | tf_op | source)
XLA Modules:
  0.0 45.5 jit_solution(14711131485446096581)
XLA Ops:
  0.0 0.0 copy-start.5
  0.0 1.4 %slice_bitcast_fusion.1 = (bf16[3,40,1152]{2,1,0:T(8,128)(2,1)S(1)}, bf16[3,40,1152]{2,1,0:T(8,128)(2,1)S(1)}, bf16[3,40,1152]{2,1,0:T(8,128)(2,1)S(1)}, bf16[3,40,1152]{2,1,0:T(8,128)(2,1)S(1)}) fusion(bf16[3,12,40,1152]{3,2,1,0:T(8,128)(2,1)} %bitcast.48), kind=kLoop, calls=%fused_computation.5 | loop fusion | bytes 2211840 | tf_op jit(solution)/shard_map/squeeze | solution.py:456
  1.5 0.0 copy-done.5
  1.5 0.1 squeeze.57
  1.6 0.0 copy-start.3
  1.6 0.0 copy-start.4
  1.7 1.4 %collective-permute-start.1 = (bf16[1,3,40,2432]{3,2,1,0:T(8,128)(2,1)S(1)}, bf16[1,3,40,2432]{3,2,1,0:T(8,128)(2,1)S(1)}, u32[]{:S(2)}, u32[]{:S(2)}) collective-permute-start(bf16[1,3,40,2432]{3,2,1,0:T(8,128)(2,1)S(1)} %maximum_bitcast_fusion.1), channel_id=1, source_target_pairs={{4,0},{8,4},{12,8},{5,1},{9,5},{13,9},{6,2},{10,6},{14,10},{7,3},{... | collective-permute-start | bytes 1751048 | tf_op jit(solution)/shard_map/ppermute | solution.py:459
  3.1 0.1 squeeze.54
  3.3 3.1 %collective-permute-start = (bf16[1,3,40,2432]{3,2,1,0:T(8,128)(2,1)S(1)}, bf16[1,3,40,2432]{3,2,1,0:T(8,128)(2,1)S(1)}, u32[]{:S(2)}, u32[]{:S(2)}) collective-permute-start(bf16[1,3,40,2432]{3,2,1,0:T(8,128)(2,1)S(1)} %maximum_bitcast_fusion), channel_id=1, source_target_pairs={{0,4},{4,8},{8,12},{1,5},{5,9},{9,13},{2,6},{6,10},{10,14},{3,7},{... | collective-permute-start | bytes 1751048 | tf_op jit(solution)/shard_map/ppermute | solution.py:458
  6.3 0.1 broadcast_in_dim.21.keep
  6.5 0.0 copy-done
  6.5 0.0 copy-done.3
  6.5 0.0 copy-done.4
  6.5 0.0 copy-start.1
  6.5 1.7 %copy-done.1 = bf16[1152,1152]{1,0:T(8,128)(2,1)S(1)} copy-done((bf16[1152,1152]{1,0:T(8,128)(2,1)S(1)}, bf16[1152,1152]{1,0:T(8,128)(2,1)}, u32[]{:S(2)}) %copy-start.1) | copy-done | bytes 2654232
  8.3 3.0 %inner_kernel.1 = bf16[4,48,1152]{2,1,0:T(8,128)(2,1)S(1)} custom-call(bf16[3,12,40,1152]{3,2,1,0:T(8,128)(2,1)S(1)} %bitcast.49, bf16[1,12,40,128]{3,2,1,0:T(8,128)(2,1)S(1)} %broadcast_in_dim.21.keep, bf16[1,12,40,1152]{3,2,1,0:T(8,128)(2,1)S(1)} %copy-done.3, bf16[1152,1152]{1,0:T(8,128)(2,1)S(1)} %copy-done.1, f32[2,1152]{1,0:T(2,128)S(1)} %copy-done.4), custom_call_target="tpu_custom_call" | custom-call | flops 1000000000 | bytes 7209984 | tf_op jit(solution)/shard_map/inner_kernel/pallas_call | solution.py:432
  11.3 3.0 %collective-permute-start.5 = (bf16[4,48,1152]{2,1,0:T(8,128)(2,1)S(1)}, bf16[4,48,1152]{2,1,0:T(8,128)(2,1)S(1)}, u32[]{:S(2)}, u32[]{:S(2)}) collective-permute-start(bf16[4,48,1152]{2,1,0:T(8,128)(2,1)S(1)} %inner_kernel.1), channel_id=1, source_target_pairs={{0,16},{16,0},{1,17},{17,1},{2,18},{18,2},{3,19},{19,3},{4,20},{20... | collective-permute-start | bytes 1327112 | tf_op jit(solution)/shard_map/ppermute | solution.py:469
  14.3 0.1 fusion.1
  14.4 0.2 slice_bitcast_fusion.5
  14.5 0.0 collective-permute-done.1.below
  14.6 0.1 slice_bitcast_fusion.8
  14.6 0.0 collective-permute-done.above
  14.6 0.1 slice_bitcast_fusion.9
  14.7 0.1 squeeze.66
  14.8 0.0 slice-start.1
  14.8 0.2 maximum_bitcast_fusion.3
  14.9 1.6 %collective-permute-start.3 = (bf16[1,18,3,2432]{3,2,1,0:T(4,128)(2,1)S(1)}, bf16[1,18,3,2432]{3,2,1,0:T(4,128)(2,1)S(1)}, u32[]{:S(2)}, u32[]{:S(2)}) collective-permute-start(bf16[1,18,3,2432]{3,2,1,0:T(4,128)(2,1)S(1)} %maximum_bitcast_fusion.3), channel_id=1, source_target_pairs={{1,0},{2,1},{3,2},{5,4},{6,5},{7,6},{9,8},{10,9},{11,10},{13,12},{... | collective-permute-start | bytes 787976 | tf_op jit(solution)/shard_map/ppermute | solution.py:476
  16.5 0.1 squeeze.61
  16.6 0.2 maximum_bitcast_fusion.2
  16.7 4.7 %collective-permute-start.2 = (bf16[1,18,3,2432]{3,2,1,0:T(4,128)(2,1)S(1)}, bf16[1,18,3,2432]{3,2,1,0:T(4,128)(2,1)S(1)}, u32[]{:S(2)}, u32[]{:S(2)}) collective-permute-start(bf16[1,18,3,2432]{3,2,1,0:T(4,128)(2,1)S(1)} %maximum_bitcast_fusion.2), channel_id=1, source_target_pairs={{0,1},{1,2},{2,3},{4,5},{5,6},{6,7},{8,9},{9,10},{10,11},{12,13},{... | collective-permute-start | bytes 787976 | tf_op jit(solution)/shard_map/ppermute | solution.py:475
  21.5 0.0 copy-done.2
  21.5 3.7 %rim_kernel.1 = bf16[4,48,1152]{2,1,0:T(8,128)(2,1)S(1)} custom-call(bf16[3,12,40,1152]{3,2,1,0:T(8,128)(2,1)S(1)} %bitcast.51, bf16[1,12,40,128]{3,2,1,0:T(8,128)(2,1)S(1)} %broadcast_in_dim.21.keep, bf16[1,3,40,2432]{3,2,1,0:T(8,128)(2,1)S(1)} %collective-permute-done.above, bf16[1,3,40,2432]{3,2,1,0:T(8,128)(2,1)S(1)} %collective-permute-done.1.below, ...), custom_call_target="tpu_custom_call" | custom-call | flops 1000000000 | bytes 8377344 | tf_op jit(solution)/shard_map/rim_kernel/pallas_call | solution.py:432
  25.2 0.2 collective-permute-start.6
  25.4 0.0 slice-done
  25.4 0.0 slice-done.1
  25.4 1.9 %own_kernel.4.own = bf16[192,3456]{1,0:T(8,128)(2,1)S(1)} custom-call(bf16[192,1152]{1,0:T(8,128)(2,1)S(1)} %bitcast.53, bf16[1152,3456]{1,0:T(8,128)(2,1)S(1)} %bitcast.47), custom_call_target="tpu_custom_call" | custom-call | flops 1528823808 | bytes 8404992 | tf_op jit(solution)/shard_map/own_kernel/pallas_call | solution.py:432
  27.3 0.0 collective-permute-done.5
  27.3 2.3 %temporal_kernel.2 = bf16[192,1152]{1,0:T(8,128)(2,1)S(1)} custom-call(bf16[192,3456]{1,0:T(8,128)(2,1)S(1)} %own_kernel.4.own, bf16[192,1152]{1,0:T(8,128)(2,1)S(1)} %bitcast.57, bf16[1152,3456]{1,0:T(8,128)(2,1)S(1)} %bitcast.47), custom_call_target="tpu_custom_call" | custom-call | flops 1019215872 | bytes 9732096 | tf_op jit(solution)/shard_map/temporal_kernel/pallas_call | solution.py:432
  29.6 0.0 collective-permute-done.3.right
  29.6 0.0 collective-permute-done.2.left
  29.7 2.6 %edge_kernel.1.normed = bf16[96,1152]{1,0:T(8,128)(2,1)S(1)} custom-call(bf16[3,12,40,1152]{3,2,1,0:T(8,128)(2,1)S(1)} %bitcast.52, bf16[1,12,40,128]{3,2,1,0:T(8,128)(2,1)S(1)} %broadcast_in_dim.21.keep, bf16[1,3,40,2432]{3,2,1,0:T(8,128)(2,1)S(1)} %collective-permute-done.above, bf16[1,3,40,2432]{3,2,1,0:T(8,128)(2,1)S(1)} %collective-permute-done.1.below, ...), custom_call_target="tpu_custom_call" | custom-call | flops 1000000000 | bytes 8902656 | tf_op jit(solution)/shard_map/edge_kernel/pallas_call | solution.py:432
  32.3 2.0 %collective-permute-start.4 = (bf16[96,1152]{1,0:T(8,128)(2,1)S(1)}, bf16[96,1152]{1,0:T(8,128)(2,1)S(1)}, u32[]{:S(2)}, u32[]{:S(2)}) collective-permute-start(bf16[96,1152]{1,0:T(8,128)(2,1)S(1)} %edge_kernel.1.normed), channel_id=1, source_target_pairs={{0,16},{16,0},{1,17},{17,1},{2,18},{18,2},{3,19},{19,3},{4,20},{20... | collective-permute-start | bytes 663560 | tf_op jit(solution)/shard_map/ppermute | solution.py:501
  34.3 1.9 %own_kernel.5.own = bf16[192,3456]{1,0:T(8,128)(2,1)S(1)} custom-call(bf16[192,1152]{1,0:T(8,128)(2,1)S(1)} %bitcast.55, bf16[1152,3456]{1,0:T(8,128)(2,1)S(1)} %bitcast.47), custom_call_target="tpu_custom_call" | custom-call | flops 1528823808 | bytes 8404992 | tf_op jit(solution)/shard_map/own_kernel/pallas_call | solution.py:432
  36.2 1.3 %own_kernel.3.own = bf16[96,3456]{1,0:T(8,128)(2,1)S(1)} custom-call(bf16[96,1152]{1,0:T(8,128)(2,1)S(1)} %edge_kernel.1.normed, bf16[1152,3456]{1,0:T(8,128)(2,1)S(1)} %bitcast.47), custom_call_target="tpu_custom_call" | custom-call | flops 764411904 | bytes 8183808 | tf_op jit(solution)/shard_map/own_kernel/pallas_call | solution.py:432
  37.5 0.7 %collective-permute-done.6 = bf16[4,48,1152]{2,1,0:T(8,128)(2,1)S(1)} collective-permute-done((bf16[4,48,1152]{2,1,0:T(8,128)(2,1)S(1)}, bf16[4,48,1152]{2,1,0:T(8,128)(2,1)S(1)}, u32[]{:S(2)}, u32[]{:S(2)}) %collective-permute-start.6) | collective-permute-done | bytes 442400 | tf_op jit(solution)/shard_map/ppermute | solution.py:486
  38.2 2.6 %temporal_kernel.3 = bf16[192,1152]{1,0:T(8,128)(2,1)S(1)} custom-call(bf16[192,3456]{1,0:T(8,128)(2,1)S(1)} %own_kernel.5.own, bf16[192,1152]{1,0:T(8,128)(2,1)S(1)} %bitcast.58, bf16[1152,3456]{1,0:T(8,128)(2,1)S(1)} %bitcast.47), custom_call_target="tpu_custom_call" | custom-call | flops 1019215872 | bytes 9732096 | tf_op jit(solution)/shard_map/temporal_kernel/pallas_call | solution.py:432
  40.8 1.7 %collective-permute-done.4.other = bf16[96,1152]{1,0:T(8,128)(2,1)S(1)} collective-permute-done((bf16[96,1152]{1,0:T(8,128)(2,1)S(1)}, bf16[96,1152]{1,0:T(8,128)(2,1)S(1)}, u32[]{:S(2)}, u32[]{:S(2)}) %collective-permute-start.4) | collective-permute-done | bytes 221216 | tf_op jit(solution)/shard_map/ppermute | solution.py:501
  42.5 3.0 %last_kernel.1 = bf16[1,12,40,1152]{3,2,1,0:T(8,128)(2,1)} custom-call(bf16[96,3456]{1,0:T(8,128)(2,1)S(1)} %own_kernel.3.own, bf16[96,1152]{1,0:T(8,128)(2,1)S(1)} %collective-permute-done.4.other, bf16[1152,3456]{1,0:T(8,128)(2,1)S(1)} %bitcast.47, bf16[4,48,1152]{2,1,0:T(8,128)(2,1)S(1)} %bitcast.54, bf16[4,48,1152]{2,1,0:T(8,128)(2,1)S(1)} %bitcast.56), custom_call_target="tpu_custom_call" | custom-call | flops 509607936 | bytes 9732096 | tf_op jit(solution)/shard_map/last_kernel/pallas_call | solution.py:432
  (10 shorter events, 0.1 us)
Async XLA Ops:
  0.0 1.5 %copy-start.5 = (s32[1,12,40]{2,0,1:T(1,128)S(1)}, s32[1,12,40]{2,0,1:T(1,128)}, u32[]{:S(2)}) copy-start(s32[1,12,40]{2,0,1:T(1,128)} %param.8) | copy-start | bytes 5764
  0.0 6.5 %copy-start = (bf16[3,1,12,40,1152]{4,3,2,1,0:T(8,128)(2,1)S(1)}, bf16[3,1,12,40,1152]{4,3,2,1,0:T(8,128)(2,1)}, u32[]{:S(2)}) copy-start(bf16[3,1,12,40,1152]{4,3,2,1,0:T(8,128)(2,1)} %param.7) | copy-start | bytes 9953284
  1.6 4.9 %copy-start.3 = (bf16[1,12,40,1152]{3,2,1,0:T(8,128)(2,1)S(1)}, bf16[1,12,40,1152]{3,2,1,0:T(8,128)(2,1)}, u32[]{:S(2)}) copy-start(bf16[1,12,40,1152]{3,2,1,0:T(8,128)(2,1)} %resid.5) | copy-start | bytes 3317764
  1.6 4.9 %copy-start.4 = (f32[2,1152]{1,0:T(2,128)S(1)}, f32[2,1152]{1,0:T(2,128)}, u32[]{:S(2)}) copy-start(f32[2,1152]{1,0:T(2,128)} %modulation.5) | copy-start | bytes 27652
  1.7 12.9 %collective-permute-start.1 = (bf16[1,3,40,2432]{3,2,1,0:T(8,128)(2,1)S(1)}, bf16[1,3,40,2432]{3,2,1,0:T(8,128)(2,1)S(1)}, u32[]{:S(2)}, u32[]{:S(2)}) collective-permute-start(bf16[1,3,40,2432]{3,2,1,0:T(8,128)(2,1)S(1)} %maximum_bitcast_fusion.1), channel_id=1, source_target_pairs={{4,0},{8,4},{12,8},{5,1},{9,5},{13,9},{6,2},{10,6},{14,10},{7,3},{... | collective-permute-start | bytes 1751048 | tf_op jit(solution)/shard_map/ppermute | solution.py:459
  3.3 11.4 %collective-permute-start = (bf16[1,3,40,2432]{3,2,1,0:T(8,128)(2,1)S(1)}, bf16[1,3,40,2432]{3,2,1,0:T(8,128)(2,1)S(1)}, u32[]{:S(2)}, u32[]{:S(2)}) collective-permute-start(bf16[1,3,40,2432]{3,2,1,0:T(8,128)(2,1)S(1)} %maximum_bitcast_fusion), channel_id=1, source_target_pairs={{0,4},{4,8},{8,12},{1,5},{5,9},{9,13},{2,6},{6,10},{10,14},{3,7},{... | collective-permute-start | bytes 1751048 | tf_op jit(solution)/shard_map/ppermute | solution.py:458
  6.5 1.8 %copy-start.1 = (bf16[1152,1152]{1,0:T(8,128)(2,1)S(1)}, bf16[1152,1152]{1,0:T(8,128)(2,1)}, u32[]{:S(2)}) copy-start(bf16[1152,1152]{1,0:T(8,128)(2,1)} %w_out.5) | copy-start | bytes 7962628
  8.3 17.1 %slice-start = ((s8[7962624]{0:T(1024)(128)(4,1)}), s8[4194304]{0:T(1024)(128)(4,1)S(1)}, s32[]{:S(2)}) async-start(s8[7962624]{0:T(1024)(128)(4,1)} %bitcast.46), calls=%async_computation | async-start | bytes 8388608
  11.3 16.0 %collective-permute-start.5 = (bf16[4,48,1152]{2,1,0:T(8,128)(2,1)S(1)}, bf16[4,48,1152]{2,1,0:T(8,128)(2,1)S(1)}, u32[]{:S(2)}, u32[]{:S(2)}) collective-permute-start(bf16[4,48,1152]{2,1,0:T(8,128)(2,1)S(1)} %inner_kernel.1), channel_id=1, source_target_pairs={{0,16},{16,0},{1,17},{17,1},{2,18},{18,2},{3,19},{19,3},{4,20},{20... | collective-permute-start | bytes 1327112 | tf_op jit(solution)/shard_map/ppermute | solution.py:469
  14.4 7.1 %copy-start.2 = (bf16[1152,1152]{1,0:T(8,128)(2,1)S(1)}, bf16[1152,1152]{1,0:T(8,128)(2,1)}, u32[]{:S(2)}) copy-start(bf16[1152,1152]{1,0:T(8,128)(2,1)} %w_out.5) | copy-start | bytes 7962628
  14.8 10.6 %slice-start.1 = ((s8[7962624]{0:T(1024)(128)(4,1)}), s8[3768320]{0:T(1024)(128)(4,1)S(1)}, s32[]{:S(2)}) async-start(s8[7962624]{0:T(1024)(128)(4,1)} %bitcast.46), calls=%async_computation.1 | async-start | bytes 7536640
  14.9 14.7 %collective-permute-start.3 = (bf16[1,18,3,2432]{3,2,1,0:T(4,128)(2,1)S(1)}, bf16[1,18,3,2432]{3,2,1,0:T(4,128)(2,1)S(1)}, u32[]{:S(2)}, u32[]{:S(2)}) collective-permute-start(bf16[1,18,3,2432]{3,2,1,0:T(4,128)(2,1)S(1)} %maximum_bitcast_fusion.3), channel_id=1, source_target_pairs={{1,0},{2,1},{3,2},{5,4},{6,5},{7,6},{9,8},{10,9},{11,10},{13,12},{... | collective-permute-start | bytes 787976 | tf_op jit(solution)/shard_map/ppermute | solution.py:476
  16.7 12.9 %collective-permute-start.2 = (bf16[1,18,3,2432]{3,2,1,0:T(4,128)(2,1)S(1)}, bf16[1,18,3,2432]{3,2,1,0:T(4,128)(2,1)S(1)}, u32[]{:S(2)}, u32[]{:S(2)}) collective-permute-start(bf16[1,18,3,2432]{3,2,1,0:T(4,128)(2,1)S(1)} %maximum_bitcast_fusion.2), channel_id=1, source_target_pairs={{0,1},{1,2},{2,3},{4,5},{5,6},{6,7},{8,9},{9,10},{10,11},{12,13},{... | collective-permute-start | bytes 787976 | tf_op jit(solution)/shard_map/ppermute | solution.py:475
  25.2 13.0 %collective-permute-start.6 = (bf16[4,48,1152]{2,1,0:T(8,128)(2,1)S(1)}, bf16[4,48,1152]{2,1,0:T(8,128)(2,1)S(1)}, u32[]{:S(2)}, u32[]{:S(2)}) collective-permute-start(bf16[4,48,1152]{2,1,0:T(8,128)(2,1)S(1)} %rim_kernel.1), channel_id=1, source_target_pairs={{0,16},{16,0},{1,17},{17,1},{2,18},{18,2},{3,19},{19,3},{4,20},{20... | collective-permute-start | bytes 1327112 | tf_op jit(solution)/shard_map/ppermute | solution.py:486
  32.3 10.2 %collective-permute-start.4 = (bf16[96,1152]{1,0:T(8,128)(2,1)S(1)}, bf16[96,1152]{1,0:T(8,128)(2,1)S(1)}, u32[]{:S(2)}, u32[]{:S(2)}) collective-permute-start(bf16[96,1152]{1,0:T(8,128)(2,1)S(1)} %edge_kernel.1.normed), channel_id=1, source_target_pairs={{0,16},{16,0},{1,17},{17,1},{2,18},{18,2},{3,19},{19,3},{4,20},{20... | collective-permute-start | bytes 663560 | tf_op jit(solution)/shard_map/ppermute | solution.py:501

commit v3 on v2

--- a/solution.py
+++ b/solution.py
@@ -3,6 +3,7 @@
 
 import jax
 import jax.numpy as jnp
+import numpy as np
 from jax import lax
 from jax.experimental import pallas as pl
 from jax.experimental.pallas import tpu as pltpu
@@ -232,7 +233,13 @@
     return found
 
 
-def inner_kernel(qkv, keep, resid, w_out, modulation, out, heads):
+def inner_kernel(qkv, keep, resid_hbm, w_hbm, modulation, out, resid, w_out, heads, arrived):
+    copies = [
+        pltpu.make_async_copy(resid_hbm, resid, arrived.at[0]),
+        pltpu.make_async_copy(w_hbm, w_out, arrived.at[1]),
+    ]
+    for copy in copies:
+        copy.start()
     tile_rows, tile_cols, width = resid.shape[1:]
     rows = tile_rows - 2 * RADIUS
     strips = tile_cols // STRIP - 1
@@ -255,35 +262,88 @@
             )
     mixed = batched(tiles, INNER_BATCH * rows // step)
     heads[...] = jnp.concatenate(mixed, axis=0).astype(jnp.bfloat16)
+    for copy in copies:
+        copy.wait()
     source = jnp.concatenate([middle(resid, 0, mine, strip) for strip in range(strips)], axis=0)
     out[...] = finish(heads[...], source, w_out[...], modulation[...]).reshape(out.shape)
 
 
-def rim_kernel(qkv, keep, above, below, resid, w_out, modulation, out, heads):
+def rim_kernel(odd, qkv, keep, first, second, resid, w_out, modulation, out, halo, heads, arrived):
     tile_rows, tile_cols, width = resid.shape[1:]
     strips = tile_cols // STRIP - 1
     near = 2 * RADIUS
+    above = jnp.where(odd[0] == 1, 0, 1)
+    copies = [
+        pltpu.make_async_copy(first, halo.at[pl.ds(above, 1)], arrived.at[0]),
+        pltpu.make_async_copy(second, halo.at[pl.ds(1 - above, 1)], arrived.at[1]),
+    ]
+    for copy in copies:
+        copy.start()
+    cases = [(strip, side) for strip in range(strips) for side in range(2)]
+    locals_ = []
+    for strip, side in cases:
+        inner = pl.ds(0 if side == 0 else tile_rows - near, near)
+        locals_.append([window(ref, plane, inner, strip) for ref, plane in ((qkv, 1), (qkv, 2), (keep, 0))])
+    for copy in copies:
+        copy.wait()
     tiles = []
     sources = []
-    for strip in range(strips):
-        for side in range(2):
-            inner = pl.ds(0 if side == 0 else tile_rows - near, near)
-            mine = pl.ds(0 if side == 0 else tile_rows - RADIUS, RADIUS)
-            halo_ref = above if side == 0 else below
-            halo = window(halo_ref, 0, pl.ds(0, RADIUS), strip)
-            parts = []
-            for at, local in (
-                (0, window(qkv, 1, inner, strip)),
-                (width, window(qkv, 2, inner, strip)),
-                (2 * width, window(keep, 0, inner, strip)),
-            ):
-                far = halo[:, at : at + local.shape[1]]
-                parts.append(jnp.concatenate([far, local] if side == 0 else [local, far], axis=0))
-            bias = strip_bias(RADIUS, parts[2])
-            tiles.append((middle(qkv, 0, mine, strip), parts[0], parts[1], bias))
-            sources.append(middle(resid, 0, mine, strip))
+    for (strip, side), parts in zip(cases, locals_):
+        mine = pl.ds(0 if side == 0 else tile_rows - RADIUS, RADIUS)
+        far = window(halo, side, pl.ds(0, RADIUS), strip)
+        joined = []
+        for at, local in zip((0, width, 2 * width), parts):
+            piece = far[:, at : at + local.shape[1]]
+            joined.append(jnp.concatenate([piece, local] if side == 0 else [local, piece], axis=0))
+        bias = strip_bias(RADIUS, joined[2])
+        tiles.append((middle(qkv, 0, mine, strip), joined[0], joined[1], bias))
+        sources.append(middle(resid, 0, mine, strip))
     heads[...] = jnp.concatenate(batched(tiles, RIM_BATCH), axis=0).astype(jnp.bfloat16)
     out[...] = finish(heads[...], jnp.concatenate(sources, axis=0), w_out[...], modulation[...]).reshape(out.shape)
+
+
+def load_kernel(odd, qkv_hbm, keep_hbm, one, two, qkv, keep, flags, arrived):
+    tile_rows, tile_cols, width = qkv.shape[1:]
+    last = tile_rows - RADIUS
+    starts = (jnp.where(odd[0] == 1, 0, last), jnp.where(odd[0] == 1, last, 0))
+    copies = [pltpu.make_async_copy(keep_hbm, flags, arrived.at[0])]
+    for out, start in zip((one, two), starts):
+        for plane in (1, 2):
+            copies.append(
+                pltpu.make_async_copy(
+                    qkv_hbm.at[plane, pl.ds(start, RADIUS)],
+                    out.at[0, :, :, pl.ds((plane - 1) * width, width)],
+                    arrived.at[len(copies)],
+                )
+            )
+    copies.append(pltpu.make_async_copy(qkv_hbm, qkv, arrived.at[len(copies)]))
+    for copy in copies:
+        copy.start()
+    copies[0].wait()
+    for row in range(tile_rows):
+        spread = jnp.broadcast_to(flags[row].astype(jnp.float32), (LANES, tile_cols))
+        keep[0, row] = spread.T.astype(jnp.bfloat16)
+    for out, start in zip((one, two), starts):
+        out[0, :, :, 2 * width :] = keep[0, pl.ds(start, RADIUS)]
+    for copy in copies[1:]:
+        copy.wait()
+
+
+def columns_kernel(odd, qkv, keep, halo, one, two):
+    tile_rows, tile_cols, width = qkv.shape[1:]
+    even = odd[1] == 0
+    body = slice(RADIUS, RADIUS + tile_rows)
+    for ref, plane, rows, lane, lanes in (
+        (qkv, 1, body, 0, width),
+        (qkv, 2, body, width, width),
+        (keep, 0, body, 2 * width, LANES),
+        (halo, 0, slice(0, RADIUS), 0, 2 * width + LANES),
+        (halo, 1, slice(RADIUS + tile_rows, 2 * RADIUS + tile_rows), 0, 2 * width + LANES),
+    ):
+        head = ref[plane, :, 0:STRIP, :].astype(jnp.float32)[:, :RADIUS]
+        tail = ref[plane, :, tile_cols - STRIP : tile_cols, :].astype(jnp.float32)[:, STRIP - RADIUS :]
+        one[0, rows, :, lane : lane + lanes] = jnp.where(even, tail, head).astype(jnp.bfloat16)
+        two[0, rows, :, lane : lane + lanes] = jnp.where(even, head, tail).astype(jnp.bfloat16)
 
 
 def edge_columns(ref, plane, row):
@@ -291,7 +351,7 @@
     return found[:STRIP], found[found.shape[0] - STRIP :]
 
 
-def edge_kernel(qkv, keep, above, below, left, right, resid, w_out, modulation, out, heads, far, ends, mine):
+def edge_kernel(odd, qkv, keep, halo, side_one, side_two, resid, w_out, modulation, out, heads, far, ends, mine):
     tile_rows, tile_cols, width = resid.shape[1:]
     pad_rows = tile_rows + 2 * RADIUS
     far[...] = jnp.zeros_like(far)
@@ -300,15 +360,18 @@
         if 0 <= local < tile_rows:
             sources = ((qkv, 1, local, 0, width), (qkv, 2, local, width, width), (keep, 0, local, 2 * width, LANES))
         elif local < 0:
-            sources = ((above, 0, row, 0, 2 * width + LANES),)
+            sources = ((halo, 0, row, 0, 2 * width + LANES),)
         else:
-            sources = ((below, 0, local - tile_rows, 0, 2 * width + LANES),)
+            sources = ((halo, 1, local - tile_rows, 0, 2 * width + LANES),)
         for ref, plane, at, lane, lanes in sources:
             head, tail = edge_columns(ref, plane, at)
             far[row, 0:STRIP, lane : lane + lanes] = head
             far[row, STRIP : 2 * STRIP, lane : lane + lanes] = tail
-        far[row, 2 * STRIP : 2 * STRIP + RADIUS, :] = left[0, row].astype(jnp.float32)
-        far[row, 2 * STRIP + RADIUS : 2 * STRIP + 2 * RADIUS, :] = right[0, row].astype(jnp.float32)
+        far[row, 2 * STRIP : 2 * STRIP + RADIUS, :] = side_one[0, row].astype(jnp.float32)
+        far[row, 2 * STRIP + RADIUS : 2 * STRIP + 2 * RADIUS, :] = side_two[0, row].astype(jnp.float32)
+    one_left = odd[1] == 1
+    one_col = jnp.where(one_left, -RADIUS, tile_cols)
+    two_col = jnp.where(one_left, tile_cols, -RADIUS)
     for row in range(tile_rows):
         for ref, plane, target in ((qkv, 0, ends), (resid, 0, mine)):
             head, tail = edge_columns(ref, plane, row)
@@ -332,10 +395,10 @@
                 k_col + tile_cols - 2 * STRIP,
                 jnp.where(
                     k_col < 2 * STRIP + RADIUS,
-                    k_col - 2 * STRIP - RADIUS,
+                    k_col - 2 * STRIP + one_col,
                     jnp.where(
                         k_col < 2 * STRIP + 2 * RADIUS,
-                        k_col - 2 * STRIP - RADIUS + tile_cols,
+                        k_col - 2 * STRIP - RADIUS + two_col,
                         -100 * tile_cols,
                     ),
                 ),
@@ -353,20 +416,33 @@
     out[...] = finish(heads[...], source, w_out[...], modulation[...])
 
 
-def own_kernel(normed, w_qkv, out):
-    out[...] = jnp.dot(normed[...], w_qkv[...], preferred_element_type=jnp.float32).astype(jnp.bfloat16)
+def project(normed, w_qkv, plane):
+    width = normed.shape[1]
+    return jnp.dot(normed, w_qkv[:, plane * width : (plane + 1) * width], preferred_element_type=jnp.float32)
+
+
+def own_kernel(*refs):
+    half = (len(refs) - 1) // 2
+    w_qkv = refs[half]
+    width = w_qkv.shape[0]
+    normed = jnp.concatenate([ref[...] for ref in refs[:half]], axis=0)
+    for plane in range(3):
+        found = project(normed, w_qkv, plane).astype(jnp.bfloat16)
+        start = 0
+        for ref in refs[half + 1 :]:
+            count = ref.shape[0]
+            ref[:, plane * width : (plane + 1) * width] = found[start : start + count]
+            start += count
 
 
 def head_marks(width):
-    feature, lane = iota((width, LANES), 0), iota((width, LANES), 1)
-    head = width // HEADS
-    return jnp.where((feature >= lane * head) & (feature < lane * head + head), 1.0, 0.0).astype(jnp.bfloat16)
+    feature, lane = np.arange(width)[:, None], np.arange(LANES)[None, :]
+    return jnp.asarray(feature // (width // HEADS) == lane % HEADS, jnp.bfloat16)
 
 
 def mark_heads(width):
-    row, feature = iota((2 * LANES, width), 0) % LANES, iota((2 * LANES, width), 1)
-    head = width // HEADS
-    return jnp.where((feature >= row * head) & (feature < row * head + head), 1.0, 0.0).astype(jnp.bfloat16)
+    row, feature = np.arange(LANES)[:, None], np.arange(width)[None, :]
+    return jnp.asarray((feature // (width // HEADS) == row % HEADS) & (row < 2 * HEADS), jnp.bfloat16)
 
 
 def halves_of(values):
@@ -375,13 +451,12 @@
     return high, low
 
 
-def temporal(own, other_kv):
-    width = own.shape[1] // 3
+def temporal(own, other_key, other_value, marks, spread):
+    width = other_key.shape[1]
     scale = (width // HEADS) ** (-0.5)
-    query = own[:, :width].astype(jnp.float32)
-    key_gap = other_kv[:, :width].astype(jnp.float32) - own[:, width : 2 * width].astype(jnp.float32)
-    high, low = halves_of(query * key_gap)
-    marks = head_marks(width)
+    lane = iota((1, LANES), 1)
+    key_gap = other_key.astype(jnp.float32) - own[:, width : 2 * width].astype(jnp.float32)
+    high, low = halves_of(own[:, :width].astype(jnp.float32) * key_gap)
     gap = (
         jnp.dot(high, marks, preferred_element_type=jnp.float32)
         + jnp.dot(low, marks, preferred_element_type=jnp.float32)
@@ -389,28 +464,33 @@
     own_weight = jnp.exp(jnp.minimum(-gap, 0.0))
     other_weight = jnp.exp(jnp.minimum(gap, 0.0))
     inverse = 1.0 / (own_weight + other_weight)
-    spread = mark_heads(width)
 
     def share(weight):
         part = weight.astype(jnp.bfloat16).astype(jnp.float32) * inverse
-        return jnp.dot(jnp.concatenate(halves_of(part), axis=1), spread, preferred_element_type=jnp.float32)
-
-    mixed = share(own_weight) * own[:, 2 * width :].astype(jnp.float32) + share(other_weight) * other_kv[
-        :, width:
-    ].astype(jnp.float32)
-    return mixed
-
-
-def temporal_kernel(own, other, w_qkv, out):
-    width = other.shape[1]
-    other_kv = jnp.dot(other[...], w_qkv[:, width:], preferred_element_type=jnp.float32).astype(jnp.bfloat16)
-    out[...] = temporal(own[...], other_kv).astype(jnp.bfloat16)
-
-
-def last_kernel(own, other, w_qkv, inner, rim, out, mixed_ref):
+        high, low = halves_of(part)
+        packed = jnp.where(lane < HEADS, high.astype(jnp.float32), low.astype(jnp.float32)).astype(jnp.bfloat16)
+        return jnp.dot(packed, spread, preferred_element_type=jnp.float32)
+
+    return share(own_weight) * own[:, 2 * width :].astype(jnp.float32) + share(other_weight) * other_value.astype(
+        jnp.float32
+    )
+
+
+def middle_kernel(inner_own, rim_own, inner_other, rim_other, edge, w_qkv, marks, spread, inner, rim, edge_own):
+    width = edge.shape[1]
+    first, second = inner.shape[0], inner.shape[0] + rim.shape[0]
+    stacked = jnp.concatenate([inner_other[...], rim_other[...], edge[...]], axis=0)
+    edge_own[:, :width] = project(edge[...], w_qkv, 0).astype(jnp.bfloat16)
+    keys = project(stacked, w_qkv, 1).astype(jnp.bfloat16)
+    values = project(stacked, w_qkv, 2).astype(jnp.bfloat16)
+    edge_own[:, width : 2 * width] = keys[second:]
+    edge_own[:, 2 * width :] = values[second:]
+    for own, out, rows in ((inner_own, inner, slice(0, first)), (rim_own, rim, slice(first, second))):
+        out[...] = temporal(own[...], keys[rows], values[rows], marks[...], spread[...]).astype(jnp.bfloat16)
+
+
+def last_kernel(own, other, w_qkv, marks, spread, inner, rim, out, mixed_ref):
     tile_rows, tile_cols, width = out.shape[1:]
-    other_kv = jnp.dot(other[...], w_qkv[:, width:], preferred_element_type=jnp.float32).astype(jnp.bfloat16)
-    edge = temporal(own[...], other_kv)
     strips = tile_cols // STRIP - 1
     for row in range(tile_rows):
         if row < RADIUS:
@@ -419,21 +499,30 @@
             source, at = inner, row - RADIUS
         else:
             source, at = rim, row - tile_rows + 2 * RADIUS
+        rows = tile_rows - 2 * RADIUS if source is inner else 2 * RADIUS
+        for strip in range(strips):
+            start = (strip * rows + at) * STRIP
+            piece = source[start : start + STRIP, :].astype(jnp.float32)
+            mixed_ref[row, EDGE + STRIP * strip : EDGE + STRIP * strip + STRIP] = piece
+    keys = project(other[...], w_qkv, 1).astype(jnp.bfloat16)
+    values = project(other[...], w_qkv, 2).astype(jnp.bfloat16)
+    edge = temporal(own[...], keys, values, marks[...], spread[...])
+    for row in range(tile_rows):
         mixed_ref[row, 0:EDGE] = edge[STRIP * row : STRIP * row + EDGE]
         mixed_ref[row, tile_cols - EDGE :] = edge[STRIP * row + EDGE : STRIP * row + STRIP]
-        for strip in range(strips):
-            piece = source[strip, STRIP * at : STRIP * at + STRIP, :].astype(jnp.float32)
-            mixed_ref[row, EDGE + STRIP * strip : EDGE + STRIP * strip + STRIP] = piece
     out[0] = mixed_ref[...].astype(jnp.bfloat16)
 
 
-def call(body, out_shape, operands, scratch=(), flops=0, limit=32):
-    size = sum(x.size * x.dtype.itemsize for x in operands)
+def call(body, out_shape, operands, scratch=(), flops=0, limit=24, specs=()):
+    size = sum(math.prod(x.shape) * x.dtype.itemsize for x in operands)
+    in_specs = [VMEM] * len(operands)
+    for index, spec in specs:
+        in_specs[index] = spec
     return pl.pallas_call(
         body,
         out_shape=out_shape,
-        in_specs=[VMEM] * len(operands),
-        out_specs=VMEM,
+        in_specs=in_specs,
+        out_specs=[VMEM] * len(out_shape) if isinstance(out_shape, list) else VMEM,
         scratch_shapes=list(scratch),
         cost_estimate=pl.CostEstimate(flops=flops, bytes_accessed=size, transcendentals=0),
         compiler_params=pltpu.CompilerParams(vmem_limit_bytes=limit * MIB),
@@ -441,91 +530,103 @@
     )(*operands)
 
 
+def exchanges(count):
+    found = []
+    for start in (0, 1):
+        pairs = [(i, i + 1) for i in range(start, count - 1, 2)]
+        found.append(pairs + [(j, i) for i, j in pairs])
+    return found
+
+
 def fast_device(resid, spatial_qkv, key_keep, w_spatial_out, modulation, w_temporal_qkv):
     frame_count, tile_rows, tile_cols, width = resid.shape
-    qkv = spatial_qkv[:, 0]
-    keep = jnp.broadcast_to(key_keep.astype(jnp.bfloat16)[..., None], key_keep.shape + (LANES,))
     strips = tile_cols // STRIP - 1
-    row_count, col_count = lax.axis_size("row"), lax.axis_size("col")
-    rising = lambda count: [(i, i + 1) for i in range(count - 1)]
-    falling = lambda count: [(i + 1, i) for i in range(count - 1)]
+    odd = jnp.stack([lax.axis_index("row") % 2, lax.axis_index("col") % 2]).astype(jnp.int32)
     swap = [(0, 1), (1, 0)]
     bf16 = jnp.bfloat16
-
-    def border(rows):
-        return jnp.concatenate([qkv[1, rows], qkv[2, rows], keep[0, rows]], axis=-1)[None]
-
-    above = lax.ppermute(border(slice(tile_rows - RADIUS, None)), "row", rising(row_count))
-    below = lax.ppermute(border(slice(0, RADIUS)), "row", falling(row_count))
-
-    half = (tile_rows - 2 * RADIUS) * STRIP
-    inner = call(
+    struct = lambda *shape: jax.ShapeDtypeStruct(shape, bf16)
+    held = lambda *shape: pltpu.VMEM(shape, bf16)
+    stay = lambda x: pltpu.with_memory_space_constraint(x, pltpu.HBM)
+    smem = pl.BlockSpec(memory_space=pltpu.SMEM)
+    hbm = pl.BlockSpec(memory_space=pltpu.HBM)
+    marks, spread = head_marks(width), mark_heads(width)
+    lanes = 2 * width + LANES
+    pad_rows = tile_rows + 2 * RADIUS
+    edge_count = tile_rows * STRIP
+
+    one, two, qkv, keep = call(
+        load_kernel,
+        [struct(1, RADIUS, tile_cols, lanes)] * 2
+        + [held(3, tile_rows, tile_cols, width), held(1, tile_rows, tile_cols, LANES)],
+        (odd, stay(spatial_qkv[:, 0]), stay(key_keep.reshape(tile_rows, 1, tile_cols))),
+        [pltpu.VMEM((tile_rows, 1, tile_cols), jnp.int32), pltpu.SemaphoreType.DMA((6,))],
+        specs=[(0, smem), (1, hbm), (2, hbm)],
+    )
+    pairs_one, pairs_two = exchanges(lax.axis_size("row"))
+    first = lax.ppermute(one, "row", pairs_one)
+    second = lax.ppermute(two, "row", pairs_two)
+
+    inner_count = strips * (tile_rows - 2 * RADIUS) * STRIP
+    inner, resid, w_spatial_out = call(
         inner_kernel,
-        jax.ShapeDtypeStruct((strips, half, width), bf16),
-        (qkv, keep, resid, w_spatial_out, modulation),
-        [pltpu.VMEM((strips * half, width), bf16)],
+        [struct(inner_count, width), held(*resid.shape), held(width, width)],
+        (qkv, keep, stay(resid), stay(w_spatial_out), modulation),
+        [held(inner_count, width), pltpu.SemaphoreType.DMA((2,))],
         flops=10**9,
+        specs=[(2, hbm), (3, hbm)],
     )
     inner_other = lax.ppermute(inner, "tm", swap)
 
-    def side(cols):
-        local = jnp.concatenate([qkv[1, :, cols], qkv[2, :, cols], keep[0, :, cols]], axis=-1)
-        return jnp.concatenate([above[0, :, cols], local, below[0, :, cols]], axis=0)[None]
-
-    left = lax.ppermute(side(slice(tile_cols - RADIUS, None)), "col", rising(col_count))
-    right = lax.ppermute(side(slice(0, RADIUS)), "col", falling(col_count))
-
-    rim_half = 2 * RADIUS * STRIP
-    rim = call(
+    rim_count = strips * 2 * RADIUS * STRIP
+    rim, halo = call(
         rim_kernel,
-        jax.ShapeDtypeStruct((strips, rim_half, width), bf16),
-        (qkv, keep, above, below, resid, w_spatial_out, modulation),
-        [pltpu.VMEM((strips * rim_half, width), bf16)],
+        [struct(rim_count, width), held(2, RADIUS, tile_cols, lanes)],
+        (odd, qkv, keep, first, second, resid, w_spatial_out, modulation),
+        [held(rim_count, width), pltpu.SemaphoreType.DMA((2,))],
         flops=10**9,
+        specs=[(0, smem)],
     )
     rim_other = lax.ppermute(rim, "tm", swap)
 
-    edge_count = tile_rows * STRIP
+    one, two = call(
+        columns_kernel, [struct(1, pad_rows, RADIUS, lanes)] * 2, (odd, qkv, keep, halo), specs=[(0, smem)]
+    )
+    pairs_one, pairs_two = exchanges(lax.axis_size("col"))
+    side_one = lax.ppermute(one, "col", pairs_one)
+    side_two = lax.ppermute(two, "col", pairs_two)
+
+    inner_own, rim_own = call(
+        own_kernel,
+        [struct(inner_count, 3 * width), struct(rim_count, 3 * width)],
+        (inner, rim, w_temporal_qkv),
+        flops=(inner_count + rim_count) * width * width * 6,
+    )
+
     edge = call(
         edge_kernel,
-        jax.ShapeDtypeStruct((edge_count, width), bf16),
-        (qkv, keep, above, below, left, right, resid, w_spatial_out, modulation),
+        struct(edge_count, width),
+        (odd, qkv, keep, halo, side_one, side_two, resid, w_spatial_out, modulation),
         [
-            pltpu.VMEM((edge_count, width), bf16),
-            pltpu.VMEM((tile_rows + 2 * RADIUS, 3 * STRIP, 2 * width + LANES), jnp.float32),
+            held(edge_count, width),
+            pltpu.VMEM((pad_rows, 3 * STRIP, lanes), jnp.float32),
             pltpu.VMEM((tile_rows, STRIP, width), jnp.float32),
             pltpu.VMEM((tile_rows, STRIP, width), jnp.float32),
         ],
         flops=10**9,
+        specs=[(0, smem)],
     )
     edge_other = lax.ppermute(edge, "tm", swap)
 
-    def own(normed):
-        count = normed.shape[0]
-        return call(
-            own_kernel,
-            jax.ShapeDtypeStruct((count, 3 * width), bf16),
-            (normed, w_temporal_qkv),
-            flops=count * width * width * 6,
-        )
-
-    def attend(own_qkv, other):
-        count = other.shape[0]
-        return call(
-            temporal_kernel,
-            jax.ShapeDtypeStruct((count, width), bf16),
-            (own_qkv, other, w_temporal_qkv),
-            flops=count * width * width * 4,
-        )
-
-    flat = lambda x: x.reshape(-1, width)
-    inner_own, rim_own, edge_own = own(flat(inner)), own(flat(rim)), own(edge)
-    inner_done = attend(inner_own, flat(inner_other)).reshape(inner.shape)
-    rim_done = attend(rim_own, flat(rim_other)).reshape(rim.shape)
+    inner_done, rim_done, edge_own = call(
+        middle_kernel,
+        [struct(inner_count, width), struct(rim_count, width), struct(edge_count, 3 * width)],
+        (inner_own, rim_own, inner_other, rim_other, edge, w_temporal_qkv, marks, spread),
+        flops=(inner_count + rim_count + edge_count) * width * width * 4,
+    )
     return call(
         last_kernel,
-        jax.ShapeDtypeStruct(resid.shape, bf16),
-        (edge_own, edge_other, w_temporal_qkv, inner_done, rim_done),
+        jax.ShapeDtypeStruct((frame_count, tile_rows, tile_cols, width), bf16),
+        (edge_own, edge_other, w_temporal_qkv, marks, spread, inner_done, rim_done),
         [pltpu.VMEM((tile_rows, tile_cols, width), jnp.float32)],
         flops=edge_count * width * width * 4,
     )

time: 45.7 us -> 44.6 us (0.976)
  the two profiles are of different devices: /device:TPU:0 before, /device:TPU:20 now
where the time goes in v3:
time: 44.6 us; the launch traced here: 44.5 us
  Pallas kernels  27.4 us (61%)
  starting transfers between devices  10 us (22%)
  waiting for transfers between devices  6.76 us (15%)
    pallas_call x8, Pallas kernels, call(): pl.pallas_call(body, out_shape=out_shape, in_specs=in_specs, out_specs=[V...  27.4 us
    ppermute x1, waiting for transfers between devices, fast_device(): second = lax.ppermute(two, 'row', pairs_two)  3.61 us
    ppermute x1, waiting for transfers between devices, fast_device(): side_two = lax.ppermute(two, 'col', pairs_two)  3.07 us
    ppermute x1, starting transfers between devices, fast_device(): second = lax.ppermute(two, 'row', pairs_two)  2.5 us
    ppermute x1, starting transfers between devices, fast_device(): side_two = lax.ppermute(two, 'col', pairs_two)  2.09 us
    ppermute x1, starting transfers between devices, fast_device(): side_one = lax.ppermute(one, 'col', pairs_one)  1.64 us
    ppermute x1, starting transfers between devices, fast_device(): inner_other = lax.ppermute(inner, 'tm', swap)  1.56 us
    ppermute x1, starting transfers between devices, fast_device(): rim_other = lax.ppermute(rim, 'tm', swap)  1.55 us
  transfers between devices with their start and end apart: 7, of which 3 were waited for; matrix products, arithmetic and copies ran while one was open for 0% of the time, Pallas kernels for 49%

profile of v3, /device:TPU:20, one launch (start us, length us, event | category | flops | bytes accessed | tf_op | source)
XLA Modules:
  0.0 44.5 jit_solution(15988868423363149447)
XLA Ops:
  0.0 0.1 pad_add_fusion.odd
  0.1 0.0 copy-start.2
  0.1 2.9 %load_kernel.1 = (bf16[1,3,40,2432]{3,2,1,0:T(8,128)(2,1)S(1)}, bf16[1,3,40,2432]{3,2,1,0:T(8,128)(2,1)S(1)}, bf16[3,12,40,1152]{3,2,1,0:T(8,128)(2,1)S(1)}, bf16[1,12,40,128]{3,2,1,0:T(8,128)(2,1)S(1)}) custom-call(s32[2]{0:T(128)S(1)} %pad_add_fusion.odd, bf16[3,12,40,1152]{3,2,1,0:T(8,128)(2,1)} %bitcast.6, s32[12,1,40]{2,1,0:T(1,128)} %bitcast.7), custom_call_target="tpu_custom_call" | custom-call | bytes 3319688 | tf_op jit(solution)/shard_map/load_kernel/pallas_call | solution.py:521
  3.0 0.1 collective-permute-start
  3.1 2.5 %collective-permute-start.1 = (bf16[1,3,40,2432]{3,2,1,0:T(8,128)(2,1)S(1)}, bf16[1,3,40,2432]{3,2,1,0:T(8,128)(2,1)S(1)}, u32[]{:S(2)}, u32[]{:S(2)}) collective-permute-start(bf16[1,3,40,2432]{3,2,1,0:T(8,128)(2,1)S(1)} %get-tuple-element.25), channel_id=1, source_target_pairs={{4,8},{8,4},{5,9},{9,5},{6,10},{10,6},{7,11},{11,7},{20,24},{24,20... | collective-permute-start | bytes 1751048 | tf_op jit(solution)/shard_map/ppermute | solution.py:567
  5.6 0.0 copy-done.2
  5.6 0.0 slice-start
  5.6 3.4 %inner_kernel.1 = (bf16[192,1152]{1,0:T(8,128)(2,1)S(1)}, bf16[1,12,40,1152]{3,2,1,0:T(8,128)(2,1)S(1)}, bf16[1152,1152]{1,0:T(8,128)(2,1)S(1)}) custom-call(bf16[3,12,40,1152]{3,2,1,0:T(8,128)(2,1)S(1)} %get-tuple-element.21.qkv, bf16[1,12,40,128]{3,2,1,0:T(8,128)(2,1)S(1)} %get-tuple-element.22.keep, bf16[1,12,40,1152]{3,2,1,0:T(8,128)(2,1)} %resid_hbm.1, ...), custom_call_target="tpu_custom_call" | custom-call | flops 1000000000 | bytes 7209984 | tf_op jit(solution)/shard_map/inner_kernel/pallas_call | solution.py:521
  9.0 1.6 %collective-permute-start.2 = (bf16[192,1152]{1,0:T(8,128)(2,1)S(1)}, bf16[192,1152]{1,0:T(8,128)(2,1)S(1)}, u32[]{:S(2)}, u32[]{:S(2)}) collective-permute-start(bf16[192,1152]{1,0:T(8,128)(2,1)S(1)} %get-tuple-element.23.refs_0_), channel_id=1, source_target_pairs={{0,16},{16,0},{1,17},{17,1},{2,18},{18,2},{3,19},{19,3},{4,20},{20... | collective-permute-start | bytes 1327112 | tf_op jit(solution)/shard_map/ppermute | solution.py:578
  10.6 0.0 collective-permute-done.first
  10.6 3.6 %collective-permute-done.1.second = bf16[1,3,40,2432]{3,2,1,0:T(8,128)(2,1)S(1)} collective-permute-done((bf16[1,3,40,2432]{3,2,1,0:T(8,128)(2,1)S(1)}, bf16[1,3,40,2432]{3,2,1,0:T(8,128)(2,1)S(1)}, u32[]{:S(2)}, u32[]{:S(2)}) %collective-permute-start.1) | collective-permute-done | bytes 583712 | tf_op jit(solution)/shard_map/ppermute | solution.py:567
  14.2 0.0 slice-start.1
  14.2 4.8 %rim_kernel.1 = (bf16[192,1152]{1,0:T(8,128)(2,1)S(1)}, bf16[2,3,40,2432]{3,2,1,0:T(8,128)(2,1)S(1)}) custom-call(s32[2]{0:T(128)S(1)} %pad_add_fusion.odd, bf16[3,12,40,1152]{3,2,1,0:T(8,128)(2,1)S(1)} %get-tuple-element.21.qkv, bf16[1,12,40,128]{3,2,1,0:T(8,128)(2,1)S(1)} %get-tuple-element.22.keep, ...), custom_call_target="tpu_custom_call" | custom-call | flops 1000000000 | bytes 8377352 | tf_op jit(solution)/shard_map/rim_kernel/pallas_call | solution.py:521
  19.0 1.6 %collective-permute-start.3 = (bf16[192,1152]{1,0:T(8,128)(2,1)S(1)}, bf16[192,1152]{1,0:T(8,128)(2,1)S(1)}, u32[]{:S(2)}, u32[]{:S(2)}) collective-permute-start(bf16[192,1152]{1,0:T(8,128)(2,1)S(1)} %get-tuple-element.28.refs_1_), channel_id=1, source_target_pairs={{0,16},{16,0},{1,17},{17,1},{2,18},{18,2},{3,19},{19,3},{4,20},{20... | collective-permute-start | bytes 1327112 | tf_op jit(solution)/shard_map/ppermute | solution.py:589
  20.6 1.2 %columns_kernel.1 = (bf16[1,18,3,2432]{3,2,1,0:T(4,128)(2,1)S(1)}, bf16[1,18,3,2432]{3,2,1,0:T(4,128)(2,1)S(1)}) custom-call(s32[2]{0:T(128)S(1)} %pad_add_fusion.odd, bf16[3,12,40,1152]{3,2,1,0:T(8,128)(2,1)S(1)} %get-tuple-element.21.qkv, bf16[1,12,40,128]{3,2,1,0:T(8,128)(2,1)S(1)} %get-tuple-element.22.keep, ...), custom_call_target="tpu_custom_call" | custom-call | bytes 4608008 | tf_op jit(solution)/shard_map/columns_kernel/pallas_call | solution.py:521
  21.7 1.6 %collective-permute-start.4 = (bf16[1,18,3,2432]{3,2,1,0:T(4,128)(2,1)S(1)}, bf16[1,18,3,2432]{3,2,1,0:T(4,128)(2,1)S(1)}, u32[]{:S(2)}, u32[]{:S(2)}) collective-permute-start(bf16[1,18,3,2432]{3,2,1,0:T(4,128)(2,1)S(1)} %get-tuple-element.32), channel_id=1, source_target_pairs={{0,1},{2,3},{1,0},{3,2},{4,5},{6,7},{5,4},{7,6},{8,9},{10,11},{9,8... | collective-permute-start | bytes 787976 | tf_op jit(solution)/shard_map/ppermute | solution.py:595
  23.4 2.1 %collective-permute-start.5 = (bf16[1,18,3,2432]{3,2,1,0:T(4,128)(2,1)S(1)}, bf16[1,18,3,2432]{3,2,1,0:T(4,128)(2,1)S(1)}, u32[]{:S(2)}, u32[]{:S(2)}) collective-permute-start(bf16[1,18,3,2432]{3,2,1,0:T(4,128)(2,1)S(1)} %get-tuple-element.33), channel_id=1, source_target_pairs={{1,2},{2,1},{5,6},{6,5},{9,10},{10,9},{13,14},{14,13},{17,18},{18,... | collective-permute-start | bytes 787976 | tf_op jit(solution)/shard_map/ppermute | solution.py:596
  25.5 0.0 slice-done
  25.5 0.0 slice-done.1
  25.5 4.0 %own_kernel.1 = (bf16[192,3456]{1,0:T(8,128)(2,1)S(1)}, bf16[192,3456]{1,0:T(8,128)(2,1)S(1)}) custom-call(bf16[192,1152]{1,0:T(8,128)(2,1)S(1)} %get-tuple-element.23.refs_0_, bf16[192,1152]{1,0:T(8,128)(2,1)S(1)} %get-tuple-element.28.refs_1_, bf16[1152,3456]{1,0:T(8,128)(2,1)S(1)} %bitcast.5), custom_call_target="tpu_custom_call" | custom-call | flops 3057647616 | bytes 8847360 | tf_op jit(solution)/shard_map/own_kernel/pallas_call | solution.py:521
  29.5 0.0 copy-start
  29.5 0.0 copy-start.1
  29.5 0.0 collective-permute-done.4.side_one
  29.5 3.1 %collective-permute-done.5.side_two = bf16[1,18,3,2432]{3,2,1,0:T(4,128)(2,1)S(1)} collective-permute-done((bf16[1,18,3,2432]{3,2,1,0:T(4,128)(2,1)S(1)}, bf16[1,18,3,2432]{3,2,1,0:T(4,128)(2,1)S(1)}, u32[]{:S(2)}, u32[]{:S(2)}) %collective-permute-start.5) | collective-permute-done | bytes 262688 | tf_op jit(solution)/shard_map/ppermute | solution.py:596
  32.6 3.2 %edge_kernel.1.edge = bf16[96,1152]{1,0:T(8,128)(2,1)S(1)} custom-call(s32[2]{0:T(128)S(1)} %pad_add_fusion.odd, bf16[3,12,40,1152]{3,2,1,0:T(8,128)(2,1)S(1)} %get-tuple-element.21.qkv, bf16[1,12,40,128]{3,2,1,0:T(8,128)(2,1)S(1)} %get-tuple-element.22.keep, bf16[2,3,40,2432]{3,2,1,0:T(8,128)(2,1)S(1)} %get-tuple-element.31.halo, ...), custom_call_target="tpu_custom_call" | custom-call | flops 1000000000 | bytes 8902664 | tf_op jit(solution)/shard_map/edge_kernel/pallas_call | solution.py:521
  35.8 0.6 %collective-permute-start.6 = (bf16[96,1152]{1,0:T(8,128)(2,1)S(1)}, bf16[96,1152]{1,0:T(8,128)(2,1)S(1)}, u32[]{:S(2)}, u32[]{:S(2)}) collective-permute-start(bf16[96,1152]{1,0:T(8,128)(2,1)S(1)} %edge_kernel.1.edge), channel_id=1, source_target_pairs={{0,16},{16,0},{1,17},{17,1},{2,18},{18,2},{3,19},{19,3},{4,20},{20... | collective-permute-start | bytes 663560 | tf_op jit(solution)/shard_map/ppermute | solution.py:618
  36.4 0.0 collective-permute-done.2.inner_other
  36.4 0.0 collective-permute-done.3.rim_other
  36.4 0.0 copy-done
  36.4 0.0 copy-done.1
  36.4 5.3 %middle_kernel.1 = (bf16[192,1152]{1,0:T(8,128)(2,1)S(1)}, bf16[192,1152]{1,0:T(8,128)(2,1)S(1)}, bf16[96,3456]{1,0:T(8,128)(2,1)S(1)}) custom-call(bf16[192,3456]{1,0:T(8,128)(2,1)S(1)} %get-tuple-element.29.inner_own, bf16[192,3456]{1,0:T(8,128)(2,1)S(1)} %get-tuple-element.30.rim_own, bf16[192,1152]{1,0:T(8,128)(2,1)S(1)} %collective-permute-done.2.inner_other, ...), custom_call_target="tpu_custom_call" | custom-call | flops 2548039680 | bytes 12312576 | tf_op jit(solution)/shard_map/middle_kernel/pallas_call | solution.py:521
  41.7 0.1 collective-permute-done.6.other
  41.8 2.7 %last_kernel.1 = bf16[1,12,40,1152]{3,2,1,0:T(8,128)(2,1)} custom-call(bf16[96,3456]{1,0:T(8,128)(2,1)S(1)} %get-tuple-element.34.own, bf16[96,1152]{1,0:T(8,128)(2,1)S(1)} %collective-permute-done.6.other, bf16[1152,3456]{1,0:T(8,128)(2,1)S(1)} %bitcast.5, bf16[1152,128]{1,0:T(8,128)(2,1)S(1)} %copy-done, bf16[128,1152]{1,0:T(8,128)(2,1)S(1)} %copy-done.1, ...), custom_call_target="tpu_custom_call" | custom-call | flops 509607936 | bytes 10321920 | tf_op jit(solution)/shard_map/last_kernel/pallas_call | solution.py:521
  (1 shorter events, 0.0 us)
Async XLA Ops:
  0.1 5.5 %copy-start.2 = (f32[2,1152]{1,0:T(2,128)S(1)}, f32[2,1152]{1,0:T(2,128)}, u32[]{:S(2)}) copy-start(f32[2,1152]{1,0:T(2,128)} %modulation.5) | copy-start | bytes 27652
  3.0 7.6 %collective-permute-start = (bf16[1,3,40,2432]{3,2,1,0:T(8,128)(2,1)S(1)}, bf16[1,3,40,2432]{3,2,1,0:T(8,128)(2,1)S(1)}, u32[]{:S(2)}, u32[]{:S(2)}) collective-permute-start(bf16[1,3,40,2432]{3,2,1,0:T(8,128)(2,1)S(1)} %get-tuple-element.24), channel_id=1, source_target_pairs={{0,4},{8,12},{4,0},{12,8},{1,5},{9,13},{5,1},{13,9},{2,6},{10,14},... | collective-permute-start | bytes 1751048 | tf_op jit(solution)/shard_map/ppermute | solution.py:566
  3.1 11.1 %collective-permute-start.1 = (bf16[1,3,40,2432]{3,2,1,0:T(8,128)(2,1)S(1)}, bf16[1,3,40,2432]{3,2,1,0:T(8,128)(2,1)S(1)}, u32[]{:S(2)}, u32[]{:S(2)}) collective-permute-start(bf16[1,3,40,2432]{3,2,1,0:T(8,128)(2,1)S(1)} %get-tuple-element.25), channel_id=1, source_target_pairs={{4,8},{8,4},{5,9},{9,5},{6,10},{10,6},{7,11},{11,7},{20,24},{24,20... | collective-permute-start | bytes 1751048 | tf_op jit(solution)/shard_map/ppermute | solution.py:567
  5.6 19.9 %slice-start = ((s8[7962624]{0:T(1024)(128)(4,1)}), s8[4194304]{0:T(1024)(128)(4,1)S(1)}, s32[]{:S(2)}) async-start(s8[7962624]{0:T(1024)(128)(4,1)} %bitcast.4), calls=%async_computation | async-start | bytes 8388608
  9.0 27.4 %collective-permute-start.2 = (bf16[192,1152]{1,0:T(8,128)(2,1)S(1)}, bf16[192,1152]{1,0:T(8,128)(2,1)S(1)}, u32[]{:S(2)}, u32[]{:S(2)}) collective-permute-start(bf16[192,1152]{1,0:T(8,128)(2,1)S(1)} %get-tuple-element.23.refs_0_), channel_id=1, source_target_pairs={{0,16},{16,0},{1,17},{17,1},{2,18},{18,2},{3,19},{19,3},{4,20},{20... | collective-permute-start | bytes 1327112 | tf_op jit(solution)/shard_map/ppermute | solution.py:578
  14.2 11.3 %slice-start.1 = ((s8[7962624]{0:T(1024)(128)(4,1)}), s8[3768320]{0:T(1024)(128)(4,1)S(1)}, s32[]{:S(2)}) async-start(s8[7962624]{0:T(1024)(128)(4,1)} %bitcast.4), calls=%async_computation.1 | async-start | bytes 7536640
  19.0 17.4 %collective-permute-start.3 = (bf16[192,1152]{1,0:T(8,128)(2,1)S(1)}, bf16[192,1152]{1,0:T(8,128)(2,1)S(1)}, u32[]{:S(2)}, u32[]{:S(2)}) collective-permute-start(bf16[192,1152]{1,0:T(8,128)(2,1)S(1)} %get-tuple-element.28.refs_1_), channel_id=1, source_target_pairs={{0,16},{16,0},{1,17},{17,1},{2,18},{18,2},{3,19},{19,3},{4,20},{20... | collective-permute-start | bytes 1327112 | tf_op jit(solution)/shard_map/ppermute | solution.py:589
  21.7 7.8 %collective-permute-start.4 = (bf16[1,18,3,2432]{3,2,1,0:T(4,128)(2,1)S(1)}, bf16[1,18,3,2432]{3,2,1,0:T(4,128)(2,1)S(1)}, u32[]{:S(2)}, u32[]{:S(2)}) collective-permute-start(bf16[1,18,3,2432]{3,2,1,0:T(4,128)(2,1)S(1)} %get-tuple-element.32), channel_id=1, source_target_pairs={{0,1},{2,3},{1,0},{3,2},{4,5},{6,7},{5,4},{7,6},{8,9},{10,11},{9,8... | collective-permute-start | bytes 787976 | tf_op jit(solution)/shard_map/ppermute | solution.py:595
  23.4 9.2 %collective-permute-start.5 = (bf16[1,18,3,2432]{3,2,1,0:T(4,128)(2,1)S(1)}, bf16[1,18,3,2432]{3,2,1,0:T(4,128)(2,1)S(1)}, u32[]{:S(2)}, u32[]{:S(2)}) collective-permute-start(bf16[1,18,3,2432]{3,2,1,0:T(4,128)(2,1)S(1)} %get-tuple-element.33), channel_id=1, source_target_pairs={{1,2},{2,1},{5,6},{6,5},{9,10},{10,9},{13,14},{14,13},{17,18},{18,... | collective-permute-start | bytes 787976 | tf_op jit(solution)/shard_map/ppermute | solution.py:596
  29.5 6.9 %copy-start = (bf16[1152,128]{1,0:T(8,128)(2,1)S(1)}, bf16[1152,128]{1,0:T(8,128)(2,1)}, u32[]{:S(2)}) copy-start(bf16[1152,128]{1,0:T(8,128)(2,1)} %constant.28.clone.marks) | copy-start | bytes 884740
  29.5 6.9 %copy-start.1 = (bf16[128,1152]{1,0:T(8,128)(2,1)S(1)}, bf16[128,1152]{1,0:T(8,128)(2,1)}, u32[]{:S(2)}) copy-start(bf16[128,1152]{1,0:T(8,128)(2,1)} %constant.29.clone.spread) | copy-start | bytes 884740
  35.8 6.0 %collective-permute-start.6 = (bf16[96,1152]{1,0:T(8,128)(2,1)S(1)}, bf16[96,1152]{1,0:T(8,128)(2,1)S(1)}, u32[]{:S(2)}, u32[]{:S(2)}) collective-permute-start(bf16[96,1152]{1,0:T(8,128)(2,1)S(1)} %edge_kernel.1.edge), channel_id=1, source_target_pairs={{0,16},{16,0},{1,17},{17,1},{2,18},{18,2},{3,19},{19,3},{4,20},{20... | collective-permute-start | bytes 663560 | tf_op jit(solution)/shard_map/ppermute | solution.py:618

commit v4 on v3

--- a/solution.py
+++ b/solution.py
@@ -192,11 +192,12 @@
     return jnp.where(near & ((keep > 0.5) | itself), 0.0, NEG_FILL)
 
 
-def strip_bias(rows, keep):
-    count, keys = rows * STRIP, (rows + 2 * RADIUS) * 2 * STRIP
+def strip_bias(rows, keep, strips=1):
+    columns, key_columns = strips * STRIP, (strips + 1) * STRIP
+    count, keys = rows * columns, (rows + 2 * RADIUS) * key_columns
     q, k = iota((count, keys), 0), iota((count, keys), 1)
     return make_bias(
-        q // STRIP + RADIUS, q % STRIP + EDGE, k // (2 * STRIP), k % (2 * STRIP), keep_row(count, keep)
+        q // columns + RADIUS, q % columns + EDGE, k // key_columns, k % key_columns, keep_row(count, keep)
     )
 
 
@@ -209,20 +210,25 @@
     return (scaled * (1.0 + modulation[1:2]) + modulation[0:1]).astype(jnp.bfloat16)
 
 
+def wide(ref, plane, rows, strip, strips=1):
+    found = ref[plane, rows, pl.ds(STRIP * strip, (strips + 1) * STRIP), :].astype(jnp.float32)
+    return found.reshape(found.shape[0] * found.shape[1], found.shape[2])
+
+
 def window(ref, plane, rows, strip):
-    found = ref[plane, rows, pl.ds(STRIP * strip, 2 * STRIP), :].astype(jnp.float32)
-    return found.reshape(found.shape[0] * found.shape[1], found.shape[2]).astype(jnp.bfloat16)
-
-
-def middle(ref, plane, rows, strip):
-    found = ref[plane, rows, pl.ds(STRIP * strip, 2 * STRIP), :].astype(jnp.float32)
-    found = found[:, EDGE : EDGE + STRIP]
-    return found.reshape(found.shape[0] * STRIP, found.shape[2])
+    return wide(ref, plane, rows, strip).astype(jnp.bfloat16)
+
+
+def middle(ref, plane, rows, strip, strips=1):
+    found = ref[plane, rows, pl.ds(STRIP * strip, (strips + 1) * STRIP), :].astype(jnp.float32)
+    found = found[:, EDGE : EDGE + strips * STRIP]
+    return found.reshape(found.shape[0] * found.shape[1], found.shape[2])
 
 
 INNER_ROWS = 6
 INNER_BATCH = 4
 RIM_BATCH = 4
+RIM_STRIPS = 2
 EDGE_BATCH = 3
 
 
@@ -268,46 +274,36 @@
     out[...] = finish(heads[...], source, w_out[...], modulation[...]).reshape(out.shape)
 
 
-def rim_kernel(odd, qkv, keep, first, second, resid, w_out, modulation, out, halo, heads, arrived):
+def rim_kernel(qkv, keep, halo, resid, w_out, modulation, out, heads):
     tile_rows, tile_cols, width = resid.shape[1:]
     strips = tile_cols // STRIP - 1
     near = 2 * RADIUS
-    above = jnp.where(odd[0] == 1, 0, 1)
-    copies = [
-        pltpu.make_async_copy(first, halo.at[pl.ds(above, 1)], arrived.at[0]),
-        pltpu.make_async_copy(second, halo.at[pl.ds(1 - above, 1)], arrived.at[1]),
-    ]
-    for copy in copies:
-        copy.start()
-    cases = [(strip, side) for strip in range(strips) for side in range(2)]
-    locals_ = []
-    for strip, side in cases:
-        inner = pl.ds(0 if side == 0 else tile_rows - near, near)
-        locals_.append([window(ref, plane, inner, strip) for ref, plane in ((qkv, 1), (qkv, 2), (keep, 0))])
-    for copy in copies:
-        copy.wait()
     tiles = []
     sources = []
-    for (strip, side), parts in zip(cases, locals_):
-        mine = pl.ds(0 if side == 0 else tile_rows - RADIUS, RADIUS)
-        far = window(halo, side, pl.ds(0, RADIUS), strip)
-        joined = []
-        for at, local in zip((0, width, 2 * width), parts):
-            piece = far[:, at : at + local.shape[1]]
-            joined.append(jnp.concatenate([piece, local] if side == 0 else [local, piece], axis=0))
-        bias = strip_bias(RADIUS, joined[2])
-        tiles.append((middle(qkv, 0, mine, strip), joined[0], joined[1], bias))
-        sources.append(middle(resid, 0, mine, strip))
+    for strip in range(0, strips, RIM_STRIPS):
+        for side in range(2):
+            inner = pl.ds(0 if side == 0 else tile_rows - near, near)
+            mine = pl.ds(0 if side == 0 else tile_rows - RADIUS, RADIUS)
+            far = wide(halo, side, pl.ds(0, RADIUS), strip, RIM_STRIPS)
+            joined = []
+            for at, (ref, plane) in zip((0, width, 2 * width), ((qkv, 1), (qkv, 2), (keep, 0))):
+                local = wide(ref, plane, inner, strip, RIM_STRIPS)
+                piece = far[:, at : at + local.shape[1]]
+                both = jnp.concatenate([piece, local] if side == 0 else [local, piece], axis=0)
+                joined.append(both.astype(jnp.bfloat16))
+            bias = strip_bias(RADIUS, joined[2], RIM_STRIPS)
+            tiles.append((middle(qkv, 0, mine, strip, RIM_STRIPS), joined[0], joined[1], bias))
+            sources.append(middle(resid, 0, mine, strip, RIM_STRIPS))
     heads[...] = jnp.concatenate(batched(tiles, RIM_BATCH), axis=0).astype(jnp.bfloat16)
     out[...] = finish(heads[...], jnp.concatenate(sources, axis=0), w_out[...], modulation[...]).reshape(out.shape)
 
 
-def load_kernel(odd, qkv_hbm, keep_hbm, one, two, qkv, keep, flags, arrived):
+def load_kernel(odd, qkv_hbm, keep_hbm, one, two, qkv, keep, flags, packed, arrived):
     tile_rows, tile_cols, width = qkv.shape[1:]
     last = tile_rows - RADIUS
     starts = (jnp.where(odd[0] == 1, 0, last), jnp.where(odd[0] == 1, last, 0))
     copies = [pltpu.make_async_copy(keep_hbm, flags, arrived.at[0])]
-    for out, start in zip((one, two), starts):
+    for out, start in zip((two, one), starts[::-1]):
         for plane in (1, 2):
             copies.append(
                 pltpu.make_async_copy(
@@ -320,16 +316,27 @@
     for copy in copies:
         copy.start()
     copies[0].wait()
+    packed[...] = jnp.zeros_like(packed)
     for row in range(tile_rows):
-        spread = jnp.broadcast_to(flags[row].astype(jnp.float32), (LANES, tile_cols))
-        keep[0, row] = spread.T.astype(jnp.bfloat16)
+        packed[row : row + 1, :tile_cols] = flags[row].astype(jnp.float32)
+    turned = packed[...].T
+    for row in range(tile_rows):
+        column = jnp.broadcast_to(turned[:tile_cols, row : row + 1], (tile_cols, LANES))
+        keep[0, row] = column.astype(jnp.bfloat16)
     for out, start in zip((one, two), starts):
         out[0, :, :, 2 * width :] = keep[0, pl.ds(start, RADIUS)]
     for copy in copies[1:]:
         copy.wait()
 
 
-def columns_kernel(odd, qkv, keep, halo, one, two):
+def columns_kernel(odd, qkv, keep, first, second, after, one, two, halo, arrived):
+    above = jnp.where(odd[0] == 1, 0, 1)
+    copies = [
+        pltpu.make_async_copy(first, halo.at[pl.ds(above, 1)], arrived.at[0]),
+        pltpu.make_async_copy(second, halo.at[pl.ds(1 - above, 1)], arrived.at[1]),
+    ]
+    for copy in copies:
+        copy.start()
     tile_rows, tile_cols, width = qkv.shape[1:]
     even = odd[1] == 0
     body = slice(RADIUS, RADIUS + tile_rows)
@@ -340,6 +347,9 @@
         (halo, 0, slice(0, RADIUS), 0, 2 * width + LANES),
         (halo, 1, slice(RADIUS + tile_rows, 2 * RADIUS + tile_rows), 0, 2 * width + LANES),
     ):
+        if ref is halo and plane == 0:
+            for copy in copies:
+                copy.wait()
         head = ref[plane, :, 0:STRIP, :].astype(jnp.float32)[:, :RADIUS]
         tail = ref[plane, :, tile_cols - STRIP : tile_cols, :].astype(jnp.float32)[:, STRIP - RADIUS :]
         one[0, rows, :, lane : lane + lanes] = jnp.where(even, tail, head).astype(jnp.bfloat16)
@@ -351,10 +361,10 @@
     return found[:STRIP], found[found.shape[0] - STRIP :]
 
 
-def edge_kernel(odd, qkv, keep, halo, side_one, side_two, resid, w_out, modulation, out, heads, far, ends, mine):
+def edge_kernel(odd, qkv, keep, halo, side_one, side_two, resid, w_out, modulation, after, out, heads, far, ends, mine):
     tile_rows, tile_cols, width = resid.shape[1:]
     pad_rows = tile_rows + 2 * RADIUS
-    far[...] = jnp.zeros_like(far)
+    far[:, 2 * STRIP :, :] = jnp.zeros((pad_rows, STRIP, far.shape[2]), jnp.float32)
     for row in range(pad_rows):
         local = row - RADIUS
         if 0 <= local < tile_rows:
@@ -421,18 +431,8 @@
     return jnp.dot(normed, w_qkv[:, plane * width : (plane + 1) * width], preferred_element_type=jnp.float32)
 
 
-def own_kernel(*refs):
-    half = (len(refs) - 1) // 2
-    w_qkv = refs[half]
-    width = w_qkv.shape[0]
-    normed = jnp.concatenate([ref[...] for ref in refs[:half]], axis=0)
-    for plane in range(3):
-        found = project(normed, w_qkv, plane).astype(jnp.bfloat16)
-        start = 0
-        for ref in refs[half + 1 :]:
-            count = ref.shape[0]
-            ref[:, plane * width : (plane + 1) * width] = found[start : start + count]
-            start += count
+def own_kernel(normed, w_qkv, out):
+    out[...] = jnp.dot(normed[...], w_qkv[...], preferred_element_type=jnp.float32).astype(jnp.bfloat16)
 
 
 def head_marks(width):
@@ -476,45 +476,67 @@
     )
 
 
-def middle_kernel(inner_own, rim_own, inner_other, rim_other, edge, w_qkv, marks, spread, inner, rim, edge_own):
-    width = edge.shape[1]
-    first, second = inner.shape[0], inner.shape[0] + rim.shape[0]
-    stacked = jnp.concatenate([inner_other[...], rim_other[...], edge[...]], axis=0)
-    edge_own[:, :width] = project(edge[...], w_qkv, 0).astype(jnp.bfloat16)
+def middle_kernel(own, other, fresh, w_qkv, marks, spread, out, fresh_own):
+    count, width = other.shape
+    stacked = jnp.concatenate([other[...], fresh[...]], axis=0)
+    fresh_own[:, :width] = project(fresh[...], w_qkv, 0).astype(jnp.bfloat16)
     keys = project(stacked, w_qkv, 1).astype(jnp.bfloat16)
     values = project(stacked, w_qkv, 2).astype(jnp.bfloat16)
-    edge_own[:, width : 2 * width] = keys[second:]
-    edge_own[:, 2 * width :] = values[second:]
-    for own, out, rows in ((inner_own, inner, slice(0, first)), (rim_own, rim, slice(first, second))):
-        out[...] = temporal(own[...], keys[rows], values[rows], marks[...], spread[...]).astype(jnp.bfloat16)
-
-
-def last_kernel(own, other, w_qkv, marks, spread, inner, rim, out, mixed_ref):
+    fresh_own[:, width : 2 * width] = keys[count:]
+    fresh_own[:, 2 * width :] = values[count:]
+    out[...] = temporal(own[...], keys[:count], values[:count], marks[...], spread[...]).astype(jnp.bfloat16)
+
+
+def joining_kernel(own, other, fresh, inner, w_qkv, marks, spread, out, ends, fresh_own, rim, mixed):
     tile_rows, tile_cols, width = out.shape[1:]
     strips = tile_cols // STRIP - 1
+    middle_kernel(own, other, fresh, w_qkv, marks, spread, rim, fresh_own)
     for row in range(tile_rows):
-        if row < RADIUS:
-            source, at = rim, row
-        elif row < tile_rows - RADIUS:
-            source, at = inner, row - RADIUS
-        else:
-            source, at = rim, row - tile_rows + 2 * RADIUS
-        rows = tile_rows - 2 * RADIUS if source is inner else 2 * RADIUS
-        for strip in range(strips):
-            start = (strip * rows + at) * STRIP
-            piece = source[start : start + STRIP, :].astype(jnp.float32)
-            mixed_ref[row, EDGE + STRIP * strip : EDGE + STRIP * strip + STRIP] = piece
+        if RADIUS <= row < tile_rows - RADIUS:
+            for strip in range(strips):
+                start = (strip * (tile_rows - 2 * RADIUS) + row - RADIUS) * STRIP
+                piece = inner[start : start + STRIP, :].astype(jnp.float32)
+                mixed[row, EDGE + STRIP * strip : EDGE + STRIP * strip + STRIP] = piece
+            continue
+        at = row if row < RADIUS else row - tile_rows + 2 * RADIUS
+        columns = RIM_STRIPS * STRIP
+        for part in range(0, strips, RIM_STRIPS):
+            start = part // RIM_STRIPS * 2 * RADIUS * columns + at * columns
+            piece = rim[start : start + columns, :].astype(jnp.float32)
+            mixed[row, EDGE + STRIP * part : EDGE + STRIP * part + columns] = piece
+    mixed[:, 0:EDGE] = jnp.zeros((tile_rows, EDGE, width), jnp.float32)
+    mixed[:, tile_cols - EDGE :] = jnp.zeros((tile_rows, EDGE, width), jnp.float32)
+    out[0] = mixed[...].astype(jnp.bfloat16)
+    ends[:, 0:STRIP] = mixed[:, 0:STRIP]
+    ends[:, STRIP:] = mixed[:, tile_cols - STRIP :]
+
+
+def last_kernel(own, other, w_qkv, marks, spread, ready, ends, out, mixed, left, right, arrived):
+    tile_rows, tile_cols, width = ready.shape[1:]
+    whole = pltpu.make_async_copy(ready, out, arrived.at[0])
+    whole.start()
     keys = project(other[...], w_qkv, 1).astype(jnp.bfloat16)
     values = project(other[...], w_qkv, 2).astype(jnp.bfloat16)
     edge = temporal(own[...], keys, values, marks[...], spread[...])
-    for row in range(tile_rows):
-        mixed_ref[row, 0:EDGE] = edge[STRIP * row : STRIP * row + EDGE]
-        mixed_ref[row, tile_cols - EDGE :] = edge[STRIP * row + EDGE : STRIP * row + STRIP]
-    out[0] = mixed_ref[...].astype(jnp.bfloat16)
-
-
-def call(body, out_shape, operands, scratch=(), flops=0, limit=24, specs=()):
-    size = sum(math.prod(x.shape) * x.dtype.itemsize for x in operands)
+    edge = edge.reshape(tile_rows, STRIP, width)
+    mixed[:, 0:STRIP] = ends[:, 0:STRIP]
+    mixed[:, STRIP:] = ends[:, STRIP:]
+    mixed[:, 0:EDGE] = edge[:, :EDGE]
+    mixed[:, STRIP + EDGE :] = edge[:, EDGE:]
+    left[...] = mixed[:, :STRIP].astype(jnp.bfloat16)
+    right[...] = mixed[:, STRIP:].astype(jnp.bfloat16)
+    whole.wait()
+    copies = [
+        pltpu.make_async_copy(left, out.at[0, :, pl.ds(0, STRIP)], arrived.at[1]),
+        pltpu.make_async_copy(right, out.at[0, :, pl.ds(tile_cols - STRIP, STRIP)], arrived.at[2]),
+    ]
+    for copy in copies:
+        copy.start()
+    for copy in copies:
+        copy.wait()
+
+
+def call(body, out_shape, operands, scratch=(), flops=0, limit=24, specs=(), out_spec=VMEM):
     in_specs = [VMEM] * len(operands)
     for index, spec in specs:
         in_specs[index] = spec
@@ -522,9 +544,9 @@
         body,
         out_shape=out_shape,
         in_specs=in_specs,
-        out_specs=[VMEM] * len(out_shape) if isinstance(out_shape, list) else VMEM,
+        out_specs=[VMEM] * len(out_shape) if isinstance(out_shape, list) else out_spec,
         scratch_shapes=list(scratch),
-        cost_estimate=pl.CostEstimate(flops=flops, bytes_accessed=size, transcendentals=0),
+        cost_estimate=pl.CostEstimate(flops=flops, bytes_accessed=0, transcendentals=0),
         compiler_params=pltpu.CompilerParams(vmem_limit_bytes=limit * MIB),
         name=body.__name__,
     )(*operands)
@@ -549,6 +571,7 @@
     stay = lambda x: pltpu.with_memory_space_constraint(x, pltpu.HBM)
     smem = pl.BlockSpec(memory_space=pltpu.SMEM)
     hbm = pl.BlockSpec(memory_space=pltpu.HBM)
+    anywhere = pl.BlockSpec(memory_space=pl.ANY)
     marks, spread = head_marks(width), mark_heads(width)
     lanes = 2 * width + LANES
     pad_rows = tile_rows + 2 * RADIUS
@@ -559,7 +582,11 @@
         [struct(1, RADIUS, tile_cols, lanes)] * 2
         + [held(3, tile_rows, tile_cols, width), held(1, tile_rows, tile_cols, LANES)],
         (odd, stay(spatial_qkv[:, 0]), stay(key_keep.reshape(tile_rows, 1, tile_cols))),
-        [pltpu.VMEM((tile_rows, 1, tile_cols), jnp.int32), pltpu.SemaphoreType.DMA((6,))],
+        [
+            pltpu.VMEM((tile_rows, 1, tile_cols), jnp.int32),
+            pltpu.VMEM((LANES, LANES), jnp.float32),
+            pltpu.SemaphoreType.DMA((6,)),
+        ],
         specs=[(0, smem), (1, hbm), (2, hbm)],
     )
     pairs_one, pairs_two = exchanges(lax.axis_size("row"))
@@ -572,63 +599,69 @@
         [struct(inner_count, width), held(*resid.shape), held(width, width)],
         (qkv, keep, stay(resid), stay(w_spatial_out), modulation),
         [held(inner_count, width), pltpu.SemaphoreType.DMA((2,))],
-        flops=10**9,
         specs=[(2, hbm), (3, hbm)],
     )
     inner_other = lax.ppermute(inner, "tm", swap)
-
-    rim_count = strips * 2 * RADIUS * STRIP
-    rim, halo = call(
-        rim_kernel,
-        [struct(rim_count, width), held(2, RADIUS, tile_cols, lanes)],
-        (odd, qkv, keep, first, second, resid, w_spatial_out, modulation),
-        [held(rim_count, width), pltpu.SemaphoreType.DMA((2,))],
-        flops=10**9,
-        specs=[(0, smem)],
-    )
-    rim_other = lax.ppermute(rim, "tm", swap)
-
-    one, two = call(
-        columns_kernel, [struct(1, pad_rows, RADIUS, lanes)] * 2, (odd, qkv, keep, halo), specs=[(0, smem)]
+    inner_own = call(own_kernel, struct(inner_count, 3 * width), (inner, w_temporal_qkv))
+
+    one, two, halo = call(
+        columns_kernel,
+        [struct(1, pad_rows, RADIUS, lanes)] * 2 + [held(2, RADIUS, tile_cols, lanes)],
+        (odd, qkv, keep, first, second, inner_own),
+        [pltpu.SemaphoreType.DMA((2,))],
+        specs=[(0, smem), (5, anywhere)],
     )
     pairs_one, pairs_two = exchanges(lax.axis_size("col"))
     side_one = lax.ppermute(one, "col", pairs_one)
     side_two = lax.ppermute(two, "col", pairs_two)
 
-    inner_own, rim_own = call(
-        own_kernel,
-        [struct(inner_count, 3 * width), struct(rim_count, 3 * width)],
-        (inner, rim, w_temporal_qkv),
-        flops=(inner_count + rim_count) * width * width * 6,
+    rim_count = strips * 2 * RADIUS * STRIP
+    rim = call(
+        rim_kernel,
+        struct(rim_count, width),
+        (qkv, keep, halo, resid, w_spatial_out, modulation),
+        [held(rim_count, width)],
+    )
+    rim_other = lax.ppermute(rim, "tm", swap)
+
+    inner_done, rim_own = call(
+        middle_kernel,
+        [struct(inner_count, width), struct(rim_count, 3 * width)],
+        (inner_own, inner_other, rim, w_temporal_qkv, marks, spread),
     )
 
     edge = call(
         edge_kernel,
         struct(edge_count, width),
-        (odd, qkv, keep, halo, side_one, side_two, resid, w_spatial_out, modulation),
+        (odd, qkv, keep, halo, side_one, side_two, resid, w_spatial_out, modulation, inner_done),
         [
             held(edge_count, width),
             pltpu.VMEM((pad_rows, 3 * STRIP, lanes), jnp.float32),
             pltpu.VMEM((tile_rows, STRIP, width), jnp.float32),
             pltpu.VMEM((tile_rows, STRIP, width), jnp.float32),
         ],
-        flops=10**9,
-        specs=[(0, smem)],
+        specs=[(0, smem), (9, anywhere)],
     )
     edge_other = lax.ppermute(edge, "tm", swap)
 
-    inner_done, rim_done, edge_own = call(
-        middle_kernel,
-        [struct(inner_count, width), struct(rim_count, width), struct(edge_count, 3 * width)],
-        (inner_own, rim_own, inner_other, rim_other, edge, w_temporal_qkv, marks, spread),
-        flops=(inner_count + rim_count + edge_count) * width * width * 4,
+    out = (frame_count, tile_rows, tile_cols, width)
+    ready, ends, edge_own = call(
+        joining_kernel,
+        [struct(*out), pltpu.VMEM((tile_rows, 2 * STRIP, width), jnp.float32), struct(edge_count, 3 * width)],
+        (rim_own, rim_other, edge, inner_done, w_temporal_qkv, marks, spread),
+        [held(rim_count, width), pltpu.VMEM((tile_rows, tile_cols, width), jnp.float32)],
     )
     return call(
         last_kernel,
-        jax.ShapeDtypeStruct((frame_count, tile_rows, tile_cols, width), bf16),
-        (edge_own, edge_other, w_temporal_qkv, marks, spread, inner_done, rim_done),
-        [pltpu.VMEM((tile_rows, tile_cols, width), jnp.float32)],
-        flops=edge_count * width * width * 4,
+        struct(*out),
+        (edge_own, edge_other, w_temporal_qkv, marks, spread, ready, ends),
+        [
+            pltpu.VMEM((tile_rows, 2 * STRIP, width), jnp.float32),
+            held(tile_rows, STRIP, width),
+            held(tile_rows, STRIP, width),
+            pltpu.SemaphoreType.DMA((3,)),
+        ],
+        out_spec=hbm,
     )
 
 
@@ -638,6 +671,7 @@
         frame_count == 1
         and lax.axis_size("tm") == 2
         and width == 9 * LANES
+        and (tile_cols // STRIP - 1) % RIM_STRIPS == 0
         and tile_cols % STRIP == 0
         and tile_cols >= 2 * STRIP
         and tile_rows % 4 == 0

time: 44.6 us -> 42.2 us (0.946)
  the two profiles are of different devices: /device:TPU:20 before, /device:TPU:9 now
where the time goes in v4:
time: 42.2 us; the launch traced here: 42.1 us
  Pallas kernels  26.3 us (62%)
  starting transfers between devices  11.5 us (27%)
  waiting for transfers between devices  3.85 us (9%)
    pallas_call x9, Pallas kernels, call(): pl.pallas_call(body, out_shape=out_shape, in_specs=in_specs, out_specs=[V...  26.3 us
    ppermute x1, starting transfers between devices, fast_device(): side_two = lax.ppermute(two, 'col', pairs_two)  4.66 us
    ppermute x1, starting transfers between devices, fast_device(): second = lax.ppermute(two, 'row', pairs_two)  3.18 us
    ppermute x1, waiting for transfers between devices, fast_device(): rim_other = lax.ppermute(rim, 'tm', swap)  2.25 us
    ppermute x1, waiting for transfers between devices, fast_device(): second = lax.ppermute(two, 'row', pairs_two)  1.59 us
    ppermute x1, starting transfers between devices, fast_device(): inner_other = lax.ppermute(inner, 'tm', swap)  1.28 us
    ppermute x1, starting transfers between devices, fast_device(): rim_other = lax.ppermute(rim, 'tm', swap)  1.27 us
  transfers between devices with their start and end apart: 7, of which 2 were waited for; matrix products, arithmetic and copies ran while one was open for 0% of the time, Pallas kernels for 50%

profile of v4, /device:TPU:9, one launch (start us, length us, event | category | flops | bytes accessed | tf_op | source)
XLA Modules:
  0.0 42.1 jit_solution(4582201684726609478)
XLA Ops:
  0.0 0.0 copy-start.3
  0.0 0.1 pad_add_fusion.odd
  0.1 0.0 copy-start
  0.1 3.1 %load_kernel.1 = (bf16[1,3,40,2432]{3,2,1,0:T(8,128)(2,1)S(1)}, bf16[1,3,40,2432]{3,2,1,0:T(8,128)(2,1)S(1)}, bf16[3,12,40,1152]{3,2,1,0:T(8,128)(2,1)S(1)}, bf16[1,12,40,128]{3,2,1,0:T(8,128)(2,1)S(1)}) custom-call(s32[2]{0:T(128)S(1)} %pad_add_fusion.odd, bf16[3,12,40,1152]{3,2,1,0:T(8,128)(2,1)} %bitcast.4, s32[12,1,40]{2,1,0:T(1,128)} %bitcast.5), custom_call_target="tpu_custom_call" | custom-call | tf_op jit(solution)/shard_map/load_kernel/pallas_call | solution.py:543
  3.2 0.7 %collective-permute-start.1 = (bf16[1,3,40,2432]{3,2,1,0:T(8,128)(2,1)S(1)}, bf16[1,3,40,2432]{3,2,1,0:T(8,128)(2,1)S(1)}, u32[]{:S(2)}, u32[]{:S(2)}) collective-permute-start(bf16[1,3,40,2432]{3,2,1,0:T(8,128)(2,1)S(1)} %get-tuple-element.23), channel_id=1, source_target_pairs={{0,4},{8,12},{4,0},{12,8},{1,5},{9,13},{5,1},{13,9},{2,6},{10,14},... | collective-permute-start | bytes 1751048 | tf_op jit(solution)/shard_map/ppermute | solution.py:593
  3.9 3.2 %collective-permute-start.2 = (bf16[1,3,40,2432]{3,2,1,0:T(8,128)(2,1)S(1)}, bf16[1,3,40,2432]{3,2,1,0:T(8,128)(2,1)S(1)}, u32[]{:S(2)}, u32[]{:S(2)}) collective-permute-start(bf16[1,3,40,2432]{3,2,1,0:T(8,128)(2,1)S(1)} %get-tuple-element.24), channel_id=1, source_target_pairs={{4,8},{8,4},{5,9},{9,5},{6,10},{10,6},{7,11},{11,7},{20,24},{24,20... | collective-permute-start | bytes 1751048 | tf_op jit(solution)/shard_map/ppermute | solution.py:594
  7.1 0.0 copy-done.3
  7.1 3.3 %inner_kernel.1 = (bf16[192,1152]{1,0:T(8,128)(2,1)S(1)}, bf16[1,12,40,1152]{3,2,1,0:T(8,128)(2,1)S(1)}, bf16[1152,1152]{1,0:T(8,128)(2,1)S(1)}) custom-call(bf16[3,12,40,1152]{3,2,1,0:T(8,128)(2,1)S(1)} %get-tuple-element.20.qkv, bf16[1,12,40,128]{3,2,1,0:T(8,128)(2,1)S(1)} %get-tuple-element.21.keep, bf16[1,12,40,1152]{3,2,1,0:T(8,128)(2,1)} %resid_hbm.1, ...), custom_call_target="tpu_custom_call" | custom-call | tf_op jit(solution)/shard_map/inner_kernel/pallas_call | solution.py:543
  10.5 1.3 %collective-permute-start = (bf16[192,1152]{1,0:T(8,128)(2,1)S(1)}, bf16[192,1152]{1,0:T(8,128)(2,1)S(1)}, u32[]{:S(2)}, u32[]{:S(2)}) collective-permute-start(bf16[192,1152]{1,0:T(8,128)(2,1)S(1)} %get-tuple-element.22.normed), channel_id=1, source_target_pairs={{0,16},{16,0},{1,17},{17,1},{2,18},{18,2},{3,19},{19,3},{4,20},{20... | collective-permute-start | bytes 1327112 | tf_op jit(solution)/shard_map/ppermute | solution.py:604
  11.8 0.0 copy-done
  11.8 2.0 %own_kernel.1.after.own = bf16[192,3456]{1,0:T(8,128)(2,1)S(1)} custom-call(bf16[192,1152]{1,0:T(8,128)(2,1)S(1)} %get-tuple-element.22.normed, bf16[1152,3456]{1,0:T(8,128)(2,1)S(1)} %copy-done), custom_call_target="tpu_custom_call" | custom-call | tf_op jit(solution)/shard_map/own_kernel/pallas_call | solution.py:543
  13.8 0.0 collective-permute-done.1.first
  13.8 1.6 %collective-permute-done.2.second = bf16[1,3,40,2432]{3,2,1,0:T(8,128)(2,1)S(1)} collective-permute-done((bf16[1,3,40,2432]{3,2,1,0:T(8,128)(2,1)S(1)}, bf16[1,3,40,2432]{3,2,1,0:T(8,128)(2,1)S(1)}, u32[]{:S(2)}, u32[]{:S(2)}) %collective-permute-start.2) | collective-permute-done | bytes 583712 | tf_op jit(solution)/shard_map/ppermute | solution.py:594
  15.4 1.4 %columns_kernel.1 = (bf16[1,18,3,2432]{3,2,1,0:T(4,128)(2,1)S(1)}, bf16[1,18,3,2432]{3,2,1,0:T(4,128)(2,1)S(1)}, bf16[2,3,40,2432]{3,2,1,0:T(8,128)(2,1)S(1)}) custom-call(s32[2]{0:T(128)S(1)} %pad_add_fusion.odd, bf16[3,12,40,1152]{3,2,1,0:T(8,128)(2,1)S(1)} %get-tuple-element.20.qkv, bf16[1,12,40,128]{3,2,1,0:T(8,128)(2,1)S(1)} %get-tuple-element.21.keep, ...), custom_call_target="tpu_custom_call" | custom-call | tf_op jit(solution)/shard_map/columns_kernel/pallas_call | solution.py:543
  16.8 0.1 collective-permute-start.4
  16.9 4.7 %collective-permute-start.5 = (bf16[1,18,3,2432]{3,2,1,0:T(4,128)(2,1)S(1)}, bf16[1,18,3,2432]{3,2,1,0:T(4,128)(2,1)S(1)}, u32[]{:S(2)}, u32[]{:S(2)}) collective-permute-start(bf16[1,18,3,2432]{3,2,1,0:T(4,128)(2,1)S(1)} %get-tuple-element.30), channel_id=1, source_target_pairs={{1,2},{2,1},{5,6},{6,5},{9,10},{10,9},{13,14},{14,13},{17,18},{18,... | collective-permute-start | bytes 787976 | tf_op jit(solution)/shard_map/ppermute | solution.py:616
  21.5 0.0 copy-start.1
  21.5 0.0 copy-start.2
  21.5 3.2 %rim_kernel.1.fresh = bf16[192,1152]{1,0:T(8,128)(2,1)S(1)} custom-call(bf16[3,12,40,1152]{3,2,1,0:T(8,128)(2,1)S(1)} %get-tuple-element.20.qkv, bf16[1,12,40,128]{3,2,1,0:T(8,128)(2,1)S(1)} %get-tuple-element.21.keep, bf16[2,3,40,2432]{3,2,1,0:T(8,128)(2,1)S(1)} %get-tuple-element.25.halo, bf16[1,12,40,1152]{3,2,1,0:T(8,128)(2,1)S(1)} %get-tuple-element.26.resid, ...), custom_call_target="tpu_custom_call" | custom-call | tf_op jit(solution)/shard_map/rim_kernel/pallas_call | solution.py:543
  24.7 1.3 %collective-permute-start.3 = (bf16[192,1152]{1,0:T(8,128)(2,1)S(1)}, bf16[192,1152]{1,0:T(8,128)(2,1)S(1)}, u32[]{:S(2)}, u32[]{:S(2)}) collective-permute-start(bf16[192,1152]{1,0:T(8,128)(2,1)S(1)} %rim_kernel.1.fresh), channel_id=1, source_target_pairs={{0,16},{16,0},{1,17},{17,1},{2,18},{18,2},{3,19},{19,3},{4,20},{20... | collective-permute-start | bytes 1327112 | tf_op jit(solution)/shard_map/ppermute | solution.py:625
  26.0 0.0 collective-permute-done.other
  26.0 0.0 copy-done.1
  26.0 0.0 copy-done.2
  26.0 4.1 %middle_kernel.1 = (bf16[192,1152]{1,0:T(8,128)(2,1)S(1)}, bf16[192,3456]{1,0:T(8,128)(2,1)S(1)}) custom-call(bf16[192,3456]{1,0:T(8,128)(2,1)S(1)} %own_kernel.1.after.own, bf16[192,1152]{1,0:T(8,128)(2,1)S(1)} %collective-permute-done.other, bf16[192,1152]{1,0:T(8,128)(2,1)S(1)} %rim_kernel.1.fresh, bf16[1152,3456]{1,0:T(8,128)(2,1)S(1)} %copy-done, ...), custom_call_target="tpu_custom_call" | custom-call | tf_op jit(solution)/shard_map/middle_kernel/pallas_call | solution.py:543
  30.1 0.0 collective-permute-done.4.side_one
  30.1 0.0 collective-permute-done.5.side_two
  30.1 3.2 %edge_kernel.1.fresh = bf16[96,1152]{1,0:T(8,128)(2,1)S(1)} custom-call(s32[2]{0:T(128)S(1)} %pad_add_fusion.odd, bf16[3,12,40,1152]{3,2,1,0:T(8,128)(2,1)S(1)} %get-tuple-element.20.qkv, bf16[1,12,40,128]{3,2,1,0:T(8,128)(2,1)S(1)} %get-tuple-element.21.keep, bf16[2,3,40,2432]{3,2,1,0:T(8,128)(2,1)S(1)} %get-tuple-element.25.halo, ...), custom_call_target="tpu_custom_call" | custom-call | tf_op jit(solution)/shard_map/edge_kernel/pallas_call | solution.py:543
  33.3 0.3 collective-permute-start.6
  33.6 2.2 %collective-permute-done.3.other = bf16[192,1152]{1,0:T(8,128)(2,1)S(1)} collective-permute-done((bf16[192,1152]{1,0:T(8,128)(2,1)S(1)}, bf16[192,1152]{1,0:T(8,128)(2,1)S(1)}, u32[]{:S(2)}, u32[]{:S(2)}) %collective-permute-start.3) | collective-permute-done | bytes 442400 | tf_op jit(solution)/shard_map/ppermute | solution.py:625
  35.9 3.7 %joining_kernel.1 = (bf16[1,12,40,1152]{3,2,1,0:T(8,128)(2,1)S(1)}, f32[12,16,1152]{2,1,0:T(8,128)S(1)}, bf16[96,3456]{1,0:T(8,128)(2,1)S(1)}) custom-call(bf16[192,3456]{1,0:T(8,128)(2,1)S(1)} %get-tuple-element.28.own, bf16[192,1152]{1,0:T(8,128)(2,1)S(1)} %collective-permute-done.3.other, bf16[96,1152]{1,0:T(8,128)(2,1)S(1)} %edge_kernel.1.fresh, ...), custom_call_target="tpu_custom_call" | custom-call | tf_op jit(solution)/shard_map/joining_kernel/pallas_call | solution.py:543
  39.6 0.0 collective-permute-done.6.other
  39.6 2.4 %last_kernel.1 = bf16[1,12,40,1152]{3,2,1,0:T(8,128)(2,1)} custom-call(bf16[96,3456]{1,0:T(8,128)(2,1)S(1)} %get-tuple-element.32.own, bf16[96,1152]{1,0:T(8,128)(2,1)S(1)} %collective-permute-done.6.other, bf16[1152,3456]{1,0:T(8,128)(2,1)S(1)} %copy-done, bf16[1152,128]{1,0:T(8,128)(2,1)S(1)} %copy-done.2, bf16[128,1152]{1,0:T(8,128)(2,1)S(1)} %copy-done.1, ...), custom_call_target="tpu_custom_call" | custom-call | tf_op jit(solution)/shard_map/last_kernel/pallas_call | solution.py:543
Async XLA Ops:
  0.0 7.1 %copy-start.3 = (f32[2,1152]{1,0:T(2,128)S(1)}, f32[2,1152]{1,0:T(2,128)}, u32[]{:S(2)}) copy-start(f32[2,1152]{1,0:T(2,128)} %modulation.5) | copy-start | bytes 27652
  0.1 11.7 %copy-start = (bf16[1152,3456]{1,0:T(8,128)(2,1)S(1)}, bf16[1152,3456]{1,0:T(8,128)(2,1)}, u32[]{:S(2)}) copy-start(bf16[1152,3456]{1,0:T(8,128)(2,1)} %w_qkv.7) | copy-start | bytes 23887876
  3.2 10.6 %collective-permute-start.1 = (bf16[1,3,40,2432]{3,2,1,0:T(8,128)(2,1)S(1)}, bf16[1,3,40,2432]{3,2,1,0:T(8,128)(2,1)S(1)}, u32[]{:S(2)}, u32[]{:S(2)}) collective-permute-start(bf16[1,3,40,2432]{3,2,1,0:T(8,128)(2,1)S(1)} %get-tuple-element.23), channel_id=1, source_target_pairs={{0,4},{8,12},{4,0},{12,8},{1,5},{9,13},{5,1},{13,9},{2,6},{10,14},... | collective-permute-start | bytes 1751048 | tf_op jit(solution)/shard_map/ppermute | solution.py:593
  3.9 11.4 %collective-permute-start.2 = (bf16[1,3,40,2432]{3,2,1,0:T(8,128)(2,1)S(1)}, bf16[1,3,40,2432]{3,2,1,0:T(8,128)(2,1)S(1)}, u32[]{:S(2)}, u32[]{:S(2)}) collective-permute-start(bf16[1,3,40,2432]{3,2,1,0:T(8,128)(2,1)S(1)} %get-tuple-element.24), channel_id=1, source_target_pairs={{4,8},{8,4},{5,9},{9,5},{6,10},{10,6},{7,11},{11,7},{20,24},{24,20... | collective-permute-start | bytes 1751048 | tf_op jit(solution)/shard_map/ppermute | solution.py:594
  10.5 15.5 %collective-permute-start = (bf16[192,1152]{1,0:T(8,128)(2,1)S(1)}, bf16[192,1152]{1,0:T(8,128)(2,1)S(1)}, u32[]{:S(2)}, u32[]{:S(2)}) collective-permute-start(bf16[192,1152]{1,0:T(8,128)(2,1)S(1)} %get-tuple-element.22.normed), channel_id=1, source_target_pairs={{0,16},{16,0},{1,17},{17,1},{2,18},{18,2},{3,19},{19,3},{4,20},{20... | collective-permute-start | bytes 1327112 | tf_op jit(solution)/shard_map/ppermute | solution.py:604
  16.8 13.3 %collective-permute-start.4 = (bf16[1,18,3,2432]{3,2,1,0:T(4,128)(2,1)S(1)}, bf16[1,18,3,2432]{3,2,1,0:T(4,128)(2,1)S(1)}, u32[]{:S(2)}, u32[]{:S(2)}) collective-permute-start(bf16[1,18,3,2432]{3,2,1,0:T(4,128)(2,1)S(1)} %get-tuple-element.29), channel_id=1, source_target_pairs={{0,1},{2,3},{1,0},{3,2},{4,5},{6,7},{5,4},{7,6},{8,9},{10,11},{9,8... | collective-permute-start | bytes 787976 | tf_op jit(solution)/shard_map/ppermute | solution.py:615
  16.9 13.2 %collective-permute-start.5 = (bf16[1,18,3,2432]{3,2,1,0:T(4,128)(2,1)S(1)}, bf16[1,18,3,2432]{3,2,1,0:T(4,128)(2,1)S(1)}, u32[]{:S(2)}, u32[]{:S(2)}) collective-permute-start(bf16[1,18,3,2432]{3,2,1,0:T(4,128)(2,1)S(1)} %get-tuple-element.30), channel_id=1, source_target_pairs={{1,2},{2,1},{5,6},{6,5},{9,10},{10,9},{13,14},{14,13},{17,18},{18,... | collective-permute-start | bytes 787976 | tf_op jit(solution)/shard_map/ppermute | solution.py:616
  21.5 4.5 %copy-start.1 = (bf16[128,1152]{1,0:T(8,128)(2,1)S(1)}, bf16[128,1152]{1,0:T(8,128)(2,1)}, u32[]{:S(2)}) copy-start(bf16[128,1152]{1,0:T(8,128)(2,1)} %constant.29.clone.spread) | copy-start | bytes 884740
  21.5 4.5 %copy-start.2 = (bf16[1152,128]{1,0:T(8,128)(2,1)S(1)}, bf16[1152,128]{1,0:T(8,128)(2,1)}, u32[]{:S(2)}) copy-start(bf16[1152,128]{1,0:T(8,128)(2,1)} %constant.28.clone.marks) | copy-start | bytes 884740
  24.7 11.1 %collective-permute-start.3 = (bf16[192,1152]{1,0:T(8,128)(2,1)S(1)}, bf16[192,1152]{1,0:T(8,128)(2,1)S(1)}, u32[]{:S(2)}, u32[]{:S(2)}) collective-permute-start(bf16[192,1152]{1,0:T(8,128)(2,1)S(1)} %rim_kernel.1.fresh), channel_id=1, source_target_pairs={{0,16},{16,0},{1,17},{17,1},{2,18},{18,2},{3,19},{19,3},{4,20},{20... | collective-permute-start | bytes 1327112 | tf_op jit(solution)/shard_map/ppermute | solution.py:625
  33.3 6.2 %collective-permute-start.6 = (bf16[96,1152]{1,0:T(8,128)(2,1)S(1)}, bf16[96,1152]{1,0:T(8,128)(2,1)S(1)}, u32[]{:S(2)}, u32[]{:S(2)}) collective-permute-start(bf16[96,1152]{1,0:T(8,128)(2,1)S(1)} %edge_kernel.1.fresh), channel_id=1, source_target_pairs={{0,16},{16,0},{1,17},{17,1},{2,18},{18,2},{3,19},{19,3},{4,20},{20... | collective-permute-start | bytes 663560 | tf_op jit(solution)/shard_map/ppermute | solution.py:645

commit v5 on v4

--- a/solution.py
+++ b/solution.py
@@ -329,31 +329,37 @@
         copy.wait()
 
 
-def columns_kernel(odd, qkv, keep, first, second, after, one, two, halo, arrived):
-    above = jnp.where(odd[0] == 1, 0, 1)
-    copies = [
-        pltpu.make_async_copy(first, halo.at[pl.ds(above, 1)], arrived.at[0]),
-        pltpu.make_async_copy(second, halo.at[pl.ds(1 - above, 1)], arrived.at[1]),
-    ]
-    for copy in copies:
-        copy.start()
-    tile_rows, tile_cols, width = qkv.shape[1:]
+def pack_columns(odd, sources, one, two):
     even = odd[1] == 0
-    body = slice(RADIUS, RADIUS + tile_rows)
-    for ref, plane, rows, lane, lanes in (
-        (qkv, 1, body, 0, width),
-        (qkv, 2, body, width, width),
-        (keep, 0, body, 2 * width, LANES),
-        (halo, 0, slice(0, RADIUS), 0, 2 * width + LANES),
-        (halo, 1, slice(RADIUS + tile_rows, 2 * RADIUS + tile_rows), 0, 2 * width + LANES),
-    ):
-        if ref is halo and plane == 0:
-            for copy in copies:
-                copy.wait()
+    for ref, plane, rows, lane in sources:
+        tile_cols, lanes = ref.shape[-2:]
         head = ref[plane, :, 0:STRIP, :].astype(jnp.float32)[:, :RADIUS]
         tail = ref[plane, :, tile_cols - STRIP : tile_cols, :].astype(jnp.float32)[:, STRIP - RADIUS :]
-        one[0, rows, :, lane : lane + lanes] = jnp.where(even, tail, head).astype(jnp.bfloat16)
-        two[0, rows, :, lane : lane + lanes] = jnp.where(even, head, tail).astype(jnp.bfloat16)
+        one[rows, :, lane : lane + lanes] = jnp.where(even, tail, head).astype(jnp.bfloat16)
+        two[rows, :, lane : lane + lanes] = jnp.where(even, head, tail).astype(jnp.bfloat16)
+
+
+def own_kernel(odd, normed, w_qkv, qkv, keep, out, one, two):
+    tile_rows, tile_cols, width = qkv.shape[1:]
+    rows = slice(0, tile_rows)
+    pack_columns(odd, ((qkv, 1, rows, 0), (qkv, 2, rows, width), (keep, 0, rows, 2 * width)), one, two)
+    out[...] = jnp.dot(normed[...], w_qkv[...], preferred_element_type=jnp.float32).astype(jnp.bfloat16)
+
+
+def columns_kernel(odd, first, second, one_body, two_body, one, two, halo):
+    tile_rows = one_body.shape[0]
+    for above in (0, 1):
+
+        @pl.when(odd[0] == 1 - above)
+        def _():
+            halo[above : above + 1] = first[...]
+            halo[1 - above : 2 - above] = second[...]
+
+    body = slice(RADIUS, RADIUS + tile_rows)
+    one[0, body] = one_body[...]
+    two[0, body] = two_body[...]
+    top, bottom = slice(0, RADIUS), slice(RADIUS + tile_rows, 2 * RADIUS + tile_rows)
+    pack_columns(odd, ((halo, 0, top, 0), (halo, 1, bottom, 0)), one.at[0], two.at[0])
 
 
 def edge_columns(ref, plane, row):
@@ -426,15 +432,6 @@
     out[...] = finish(heads[...], source, w_out[...], modulation[...])
 
 
-def project(normed, w_qkv, plane):
-    width = normed.shape[1]
-    return jnp.dot(normed, w_qkv[:, plane * width : (plane + 1) * width], preferred_element_type=jnp.float32)
-
-
-def own_kernel(normed, w_qkv, out):
-    out[...] = jnp.dot(normed[...], w_qkv[...], preferred_element_type=jnp.float32).astype(jnp.bfloat16)
-
-
 def head_marks(width):
     feature, lane = np.arange(width)[:, None], np.arange(LANES)[None, :]
     return jnp.asarray(feature // (width // HEADS) == lane % HEADS, jnp.bfloat16)
@@ -479,60 +476,81 @@
 def middle_kernel(own, other, fresh, w_qkv, marks, spread, out, fresh_own):
     count, width = other.shape
     stacked = jnp.concatenate([other[...], fresh[...]], axis=0)
-    fresh_own[:, :width] = project(fresh[...], w_qkv, 0).astype(jnp.bfloat16)
-    keys = project(stacked, w_qkv, 1).astype(jnp.bfloat16)
-    values = project(stacked, w_qkv, 2).astype(jnp.bfloat16)
-    fresh_own[:, width : 2 * width] = keys[count:]
-    fresh_own[:, 2 * width :] = values[count:]
-    out[...] = temporal(own[...], keys[:count], values[:count], marks[...], spread[...]).astype(jnp.bfloat16)
-
-
-def joining_kernel(own, other, fresh, inner, w_qkv, marks, spread, out, ends, fresh_own, rim, mixed):
-    tile_rows, tile_cols, width = out.shape[1:]
-    strips = tile_cols // STRIP - 1
-    middle_kernel(own, other, fresh, w_qkv, marks, spread, rim, fresh_own)
-    for row in range(tile_rows):
-        if RADIUS <= row < tile_rows - RADIUS:
-            for strip in range(strips):
-                start = (strip * (tile_rows - 2 * RADIUS) + row - RADIUS) * STRIP
-                piece = inner[start : start + STRIP, :].astype(jnp.float32)
-                mixed[row, EDGE + STRIP * strip : EDGE + STRIP * strip + STRIP] = piece
-            continue
-        at = row if row < RADIUS else row - tile_rows + 2 * RADIUS
-        columns = RIM_STRIPS * STRIP
-        for part in range(0, strips, RIM_STRIPS):
-            start = part // RIM_STRIPS * 2 * RADIUS * columns + at * columns
-            piece = rim[start : start + columns, :].astype(jnp.float32)
-            mixed[row, EDGE + STRIP * part : EDGE + STRIP * part + columns] = piece
-    mixed[:, 0:EDGE] = jnp.zeros((tile_rows, EDGE, width), jnp.float32)
-    mixed[:, tile_cols - EDGE :] = jnp.zeros((tile_rows, EDGE, width), jnp.float32)
-    out[0] = mixed[...].astype(jnp.bfloat16)
+    query = jnp.dot(fresh[...], w_qkv[:, :width], preferred_element_type=jnp.float32)
+    fresh_own[:, :width] = query.astype(jnp.bfloat16)
+    pairs = jnp.dot(stacked, w_qkv[:, width:], preferred_element_type=jnp.float32).astype(jnp.bfloat16)
+    fresh_own[:, width:] = pairs[count:]
+    mixed = temporal(own[...], pairs[:count, :width], pairs[:count, width:], marks[...], spread[...])
+    out[...] = mixed.astype(jnp.bfloat16)
+
+
+def place(pieces, ready, ends, mixed):
+    rows, tile_cols, width = mixed.shape
+    for row, column, source, start, count in pieces:
+        mixed[row, column : column + count] = source[start : start + count, :].astype(jnp.float32)
+    mixed[:, 0:EDGE] = jnp.zeros((rows, EDGE, width), jnp.float32)
+    mixed[:, tile_cols - EDGE :] = jnp.zeros((rows, EDGE, width), jnp.float32)
+    ready[...] = mixed[...].astype(jnp.bfloat16)
     ends[:, 0:STRIP] = mixed[:, 0:STRIP]
     ends[:, STRIP:] = mixed[:, tile_cols - STRIP :]
 
 
-def last_kernel(own, other, w_qkv, marks, spread, ready, ends, out, mixed, left, right, arrived):
-    tile_rows, tile_cols, width = ready.shape[1:]
-    whole = pltpu.make_async_copy(ready, out, arrived.at[0])
-    whole.start()
-    keys = project(other[...], w_qkv, 1).astype(jnp.bfloat16)
-    values = project(other[...], w_qkv, 2).astype(jnp.bfloat16)
-    edge = temporal(own[...], keys, values, marks[...], spread[...])
+def edge_own_kernel(edge, inner, w_qkv, out, ready, ends, mixed):
+    rows, tile_cols, width = mixed.shape
+    pieces = []
+    for row in range(rows):
+        for strip in range(tile_cols // STRIP - 1):
+            pieces.append((row, EDGE + STRIP * strip, inner, (strip * rows + row) * STRIP, STRIP))
+    place(pieces, ready, ends, mixed)
+    out[...] = jnp.dot(edge[...], w_qkv[...], preferred_element_type=jnp.float32).astype(jnp.bfloat16)
+
+
+def rim_done_kernel(own, other, w_qkv, marks, spread, ready, ends, rim, mixed):
+    rows, tile_cols, width = mixed.shape
+    pairs = jnp.dot(other[...], w_qkv[:, width:], preferred_element_type=jnp.float32).astype(jnp.bfloat16)
+    rim[...] = temporal(own[...], pairs[:, :width], pairs[:, width:], marks[...], spread[...])
+    columns = RIM_STRIPS * STRIP
+    pieces = []
+    for row in range(rows):
+        for part in range((tile_cols // STRIP - 1) // RIM_STRIPS):
+            pieces.append((row, EDGE + columns * part, rim, (part * rows + row) * columns, columns))
+    place(pieces, ready, ends, mixed)
+
+
+def last_kernel(own, other, w_qkv, marks, spread, inner, inner_ends, rim, rim_ends, out, mixed, left, right, arrived):
+    tile_rows, tile_cols, width = out.shape[1:]
+    low, high = RADIUS, tile_rows - RADIUS
+    parts = (
+        (slice(0, low), rim, rim_ends, slice(0, RADIUS)),
+        (slice(low, high), inner, inner_ends, slice(0, high - low)),
+        (slice(high, tile_rows), rim, rim_ends, slice(RADIUS, 2 * RADIUS)),
+    )
+    whole = []
+    for target, ready, ends, rows in parts:
+        size = rows.stop - rows.start
+        copy = pltpu.make_async_copy(
+            ready.at[pl.ds(rows.start, size), pl.ds(STRIP, tile_cols - 2 * STRIP)],
+            out.at[0, pl.ds(target.start, size), pl.ds(STRIP, tile_cols - 2 * STRIP)],
+            arrived.at[len(whole)],
+        )
+        copy.start()
+        whole.append(copy)
+    pairs = jnp.dot(other[...], w_qkv[:, width:], preferred_element_type=jnp.float32).astype(jnp.bfloat16)
+    edge = temporal(own[...], pairs[:, :width], pairs[:, width:], marks[...], spread[...])
     edge = edge.reshape(tile_rows, STRIP, width)
-    mixed[:, 0:STRIP] = ends[:, 0:STRIP]
-    mixed[:, STRIP:] = ends[:, STRIP:]
+    for target, ready, ends, rows in parts:
+        mixed[target] = ends[rows]
     mixed[:, 0:EDGE] = edge[:, :EDGE]
     mixed[:, STRIP + EDGE :] = edge[:, EDGE:]
     left[...] = mixed[:, :STRIP].astype(jnp.bfloat16)
     right[...] = mixed[:, STRIP:].astype(jnp.bfloat16)
-    whole.wait()
     copies = [
-        pltpu.make_async_copy(left, out.at[0, :, pl.ds(0, STRIP)], arrived.at[1]),
-        pltpu.make_async_copy(right, out.at[0, :, pl.ds(tile_cols - STRIP, STRIP)], arrived.at[2]),
+        pltpu.make_async_copy(left, out.at[0, :, pl.ds(0, STRIP)], arrived.at[3]),
+        pltpu.make_async_copy(right, out.at[0, :, pl.ds(tile_cols - STRIP, STRIP)], arrived.at[4]),
     ]
     for copy in copies:
         copy.start()
-    for copy in copies:
+    for copy in whole + copies:
         copy.wait()
 
 
@@ -602,14 +620,18 @@
         specs=[(2, hbm), (3, hbm)],
     )
     inner_other = lax.ppermute(inner, "tm", swap)
-    inner_own = call(own_kernel, struct(inner_count, 3 * width), (inner, w_temporal_qkv))
+    inner_own, one_body, two_body = call(
+        own_kernel,
+        [struct(inner_count, 3 * width)] + [held(tile_rows, RADIUS, lanes)] * 2,
+        (odd, inner, w_temporal_qkv, qkv, keep),
+        specs=[(0, smem)],
+    )
 
     one, two, halo = call(
         columns_kernel,
         [struct(1, pad_rows, RADIUS, lanes)] * 2 + [held(2, RADIUS, tile_cols, lanes)],
-        (odd, qkv, keep, first, second, inner_own),
-        [pltpu.SemaphoreType.DMA((2,))],
-        specs=[(0, smem), (5, anywhere)],
+        (odd, first, second, one_body, two_body),
+        specs=[(0, smem)],
     )
     pairs_one, pairs_two = exchanges(lax.axis_size("col"))
     side_one = lax.ppermute(one, "col", pairs_one)
@@ -644,22 +666,33 @@
     )
     edge_other = lax.ppermute(edge, "tm", swap)
 
-    out = (frame_count, tile_rows, tile_cols, width)
-    ready, ends, edge_own = call(
-        joining_kernel,
-        [struct(*out), pltpu.VMEM((tile_rows, 2 * STRIP, width), jnp.float32), struct(edge_count, 3 * width)],
-        (rim_own, rim_other, edge, inner_done, w_temporal_qkv, marks, spread),
-        [held(rim_count, width), pltpu.VMEM((tile_rows, tile_cols, width), jnp.float32)],
+    def rows_of(count):
+        whole, ends = (count, tile_cols, width), (count, 2 * STRIP, width)
+        return [held(*whole), pltpu.VMEM(ends, jnp.float32)], pltpu.VMEM(whole, jnp.float32)
+
+    shapes, scratch = rows_of(tile_rows - 2 * RADIUS)
+    edge_own, inner_ready, inner_ends = call(
+        edge_own_kernel,
+        [struct(edge_count, 3 * width)] + shapes,
+        (edge, inner_done, w_temporal_qkv),
+        [scratch],
+    )
+    shapes, scratch = rows_of(2 * RADIUS)
+    rim_ready, rim_ends = call(
+        rim_done_kernel,
+        shapes,
+        (rim_own, rim_other, w_temporal_qkv, marks, spread),
+        [pltpu.VMEM((rim_count, width), jnp.float32), scratch],
     )
     return call(
         last_kernel,
-        struct(*out),
-        (edge_own, edge_other, w_temporal_qkv, marks, spread, ready, ends),
+        struct(frame_count, tile_rows, tile_cols, width),
+        (edge_own, edge_other, w_temporal_qkv, marks, spread, inner_ready, inner_ends, rim_ready, rim_ends),
         [
             pltpu.VMEM((tile_rows, 2 * STRIP, width), jnp.float32),
             held(tile_rows, STRIP, width),
             held(tile_rows, STRIP, width),
-            pltpu.SemaphoreType.DMA((3,)),
+            pltpu.SemaphoreType.DMA((5,)),
         ],
         out_spec=hbm,
     )

time: 42.2 us -> 41.9 us (level)
  waiting for transfers between devices: 3.85 us -> 3.21 us
    ppermute x1, waiting for transfers between devices: 1.59 us -> 0.71 us  [fast_device(): second = lax.ppermute(two, 'row', pairs_two)]
    ppermute x1, waiting for transfers between devices: 0.01 us -> 0.56 us  [fast_device(): edge_other = lax.ppermute(edge, 'tm', swap)]
    pallas_call x9 -> x10, Pallas kernels: 26.3 us -> 26.6 us  [call(): pl.pallas_call(body, out_shape=out_shape, in_specs=in_specs, out_specs=[V...]
  transfers between devices with their start and end apart: 7 -> 7, of which waited for: 2 -> 3; matrix products, arithmetic and copies ran while one was open for 0% -> 0% of each run, Pallas kernels for 50% -> 51%
where the time goes in v5:
time: 41.9 us; the launch traced here: 41.7 us
  Pallas kernels  26.6 us (63%)
  starting transfers between devices  11.5 us (27%)
  waiting for transfers between devices  3.21 us (8%)
    pallas_call x10, Pallas kernels, call(): pl.pallas_call(body, out_shape=out_shape, in_specs=in_specs, out_specs=[V...  26.6 us
    ppermute x1, starting transfers between devices, fast_device(): side_two = lax.ppermute(two, 'col', pairs_two)  4.66 us
    ppermute x1, starting transfers between devices, fast_device(): second = lax.ppermute(two, 'row', pairs_two)  3.18 us
    ppermute x1, waiting for transfers between devices, fast_device(): rim_other = lax.ppermute(rim, 'tm', swap)  1.93 us
    ppermute x1, starting transfers between devices, fast_device(): inner_other = lax.ppermute(inner, 'tm', swap)  1.27 us
    ppermute x1, starting transfers between devices, fast_device(): rim_other = lax.ppermute(rim, 'tm', swap)  1.27 us
  transfers between devices with their start and end apart: 7, of which 3 were waited for; matrix products, arithmetic and copies ran while one was open for 0% of the time, Pallas kernels for 51%

profile of v5, /device:TPU:9, one launch (start us, length us, event | category | flops | bytes accessed | tf_op | source)
XLA Modules:
  0.0 41.7 jit_solution(4825297259658312669)
XLA Ops:
  0.0 0.0 copy-start.3
  0.0 0.1 pad_add_fusion.odd
  0.1 0.0 copy-start
  0.1 3.1 %load_kernel.1 = (bf16[1,3,40,2432]{3,2,1,0:T(8,128)(2,1)S(1)}, bf16[1,3,40,2432]{3,2,1,0:T(8,128)(2,1)S(1)}, bf16[3,12,40,1152]{3,2,1,0:T(8,128)(2,1)S(1)}, bf16[1,12,40,128]{3,2,1,0:T(8,128)(2,1)S(1)}) custom-call(s32[2]{0:T(128)S(1)} %pad_add_fusion.odd, bf16[3,12,40,1152]{3,2,1,0:T(8,128)(2,1)} %bitcast.4, s32[12,1,40]{2,1,0:T(1,128)} %bitcast.5), custom_call_target="tpu_custom_call" | custom-call | tf_op jit(solution)/shard_map/load_kernel/pallas_call | solution.py:561
  3.2 0.7 %collective-permute-start = (bf16[1,3,40,2432]{3,2,1,0:T(8,128)(2,1)S(1)}, bf16[1,3,40,2432]{3,2,1,0:T(8,128)(2,1)S(1)}, u32[]{:S(2)}, u32[]{:S(2)}) collective-permute-start(bf16[1,3,40,2432]{3,2,1,0:T(8,128)(2,1)S(1)} %get-tuple-element.27), channel_id=1, source_target_pairs={{0,4},{8,12},{4,0},{12,8},{1,5},{9,13},{5,1},{13,9},{2,6},{10,14},... | collective-permute-start | bytes 1751048 | tf_op jit(solution)/shard_map/ppermute | solution.py:611
  3.9 3.2 %collective-permute-start.1 = (bf16[1,3,40,2432]{3,2,1,0:T(8,128)(2,1)S(1)}, bf16[1,3,40,2432]{3,2,1,0:T(8,128)(2,1)S(1)}, u32[]{:S(2)}, u32[]{:S(2)}) collective-permute-start(bf16[1,3,40,2432]{3,2,1,0:T(8,128)(2,1)S(1)} %get-tuple-element.28), channel_id=1, source_target_pairs={{4,8},{8,4},{5,9},{9,5},{6,10},{10,6},{7,11},{11,7},{20,24},{24,20... | collective-permute-start | bytes 1751048 | tf_op jit(solution)/shard_map/ppermute | solution.py:612
  7.1 0.0 copy-done.3
  7.1 3.3 %inner_kernel.1 = (bf16[192,1152]{1,0:T(8,128)(2,1)S(1)}, bf16[1,12,40,1152]{3,2,1,0:T(8,128)(2,1)S(1)}, bf16[1152,1152]{1,0:T(8,128)(2,1)S(1)}) custom-call(bf16[3,12,40,1152]{3,2,1,0:T(8,128)(2,1)S(1)} %get-tuple-element.25.qkv, bf16[1,12,40,128]{3,2,1,0:T(8,128)(2,1)S(1)} %get-tuple-element.26.keep, bf16[1,12,40,1152]{3,2,1,0:T(8,128)(2,1)} %resid_hbm.1, ...), custom_call_target="tpu_custom_call" | custom-call | tf_op jit(solution)/shard_map/inner_kernel/pallas_call | solution.py:561
  10.4 1.3 %collective-permute-start.4 = (bf16[192,1152]{1,0:T(8,128)(2,1)S(1)}, bf16[192,1152]{1,0:T(8,128)(2,1)S(1)}, u32[]{:S(2)}, u32[]{:S(2)}) collective-permute-start(bf16[192,1152]{1,0:T(8,128)(2,1)S(1)} %get-tuple-element.29.normed), channel_id=1, source_target_pairs={{0,16},{16,0},{1,17},{17,1},{2,18},{18,2},{3,19},{19,3},{4,20},{20... | collective-permute-start | bytes 1327112 | tf_op jit(solution)/shard_map/ppermute | solution.py:622
  11.7 0.0 copy-done
  11.7 2.9 %own_kernel.1 = (bf16[192,3456]{1,0:T(8,128)(2,1)S(1)}, bf16[12,3,2432]{2,1,0:T(4,128)(2,1)S(1)}, bf16[12,3,2432]{2,1,0:T(4,128)(2,1)S(1)}) custom-call(s32[2]{0:T(128)S(1)} %pad_add_fusion.odd, bf16[192,1152]{1,0:T(8,128)(2,1)S(1)} %get-tuple-element.29.normed, bf16[1152,3456]{1,0:T(8,128)(2,1)S(1)} %copy-done, ...), custom_call_target="tpu_custom_call" | custom-call | tf_op jit(solution)/shard_map/own_kernel/pallas_call | solution.py:561
  14.6 0.0 collective-permute-done.first
  14.6 0.7 %collective-permute-done.1.second = bf16[1,3,40,2432]{3,2,1,0:T(8,128)(2,1)S(1)} collective-permute-done((bf16[1,3,40,2432]{3,2,1,0:T(8,128)(2,1)S(1)}, bf16[1,3,40,2432]{3,2,1,0:T(8,128)(2,1)S(1)}, u32[]{:S(2)}, u32[]{:S(2)}) %collective-permute-start.1) | collective-permute-done | bytes 583712 | tf_op jit(solution)/shard_map/ppermute | solution.py:612
  15.4 0.9 %columns_kernel.1 = (bf16[1,18,3,2432]{3,2,1,0:T(4,128)(2,1)S(1)}, bf16[1,18,3,2432]{3,2,1,0:T(4,128)(2,1)S(1)}, bf16[2,3,40,2432]{3,2,1,0:T(8,128)(2,1)S(1)}) custom-call(s32[2]{0:T(128)S(1)} %pad_add_fusion.odd, bf16[1,3,40,2432]{3,2,1,0:T(8,128)(2,1)S(1)} %collective-permute-done.first, bf16[1,3,40,2432]{3,2,1,0:T(8,128)(2,1)S(1)} %collective-permute-done.1.second, ...), custom_call_target="tpu_custom_call" | custom-call | tf_op jit(solution)/shard_map/columns_kernel/pallas_call | solution.py:561
  16.3 0.1 collective-permute-start.2
  16.3 4.7 %collective-permute-start.3 = (bf16[1,18,3,2432]{3,2,1,0:T(4,128)(2,1)S(1)}, bf16[1,18,3,2432]{3,2,1,0:T(4,128)(2,1)S(1)}, u32[]{:S(2)}, u32[]{:S(2)}) collective-permute-start(bf16[1,18,3,2432]{3,2,1,0:T(4,128)(2,1)S(1)} %get-tuple-element.34), channel_id=1, source_target_pairs={{1,2},{2,1},{5,6},{6,5},{9,10},{10,9},{13,14},{14,13},{17,18},{18,... | collective-permute-start | bytes 787976 | tf_op jit(solution)/shard_map/ppermute | solution.py:638
  21.0 0.0 copy-start.1
  21.0 0.0 copy-start.2
  21.0 3.2 %rim_kernel.1.fresh = bf16[192,1152]{1,0:T(8,128)(2,1)S(1)} custom-call(bf16[3,12,40,1152]{3,2,1,0:T(8,128)(2,1)S(1)} %get-tuple-element.25.qkv, bf16[1,12,40,128]{3,2,1,0:T(8,128)(2,1)S(1)} %get-tuple-element.26.keep, bf16[2,3,40,2432]{3,2,1,0:T(8,128)(2,1)S(1)} %get-tuple-element.32.halo, bf16[1,12,40,1152]{3,2,1,0:T(8,128)(2,1)S(1)} %get-tuple-element.35.resid, ...), custom_call_target="tpu_custom_call" | custom-call | tf_op jit(solution)/shard_map/rim_kernel/pallas_call | solution.py:561
  24.3 1.3 %collective-permute-start.6 = (bf16[192,1152]{1,0:T(8,128)(2,1)S(1)}, bf16[192,1152]{1,0:T(8,128)(2,1)S(1)}, u32[]{:S(2)}, u32[]{:S(2)}) collective-permute-start(bf16[192,1152]{1,0:T(8,128)(2,1)S(1)} %rim_kernel.1.fresh), channel_id=1, source_target_pairs={{0,16},{16,0},{1,17},{17,1},{2,18},{18,2},{3,19},{19,3},{4,20},{20... | collective-permute-start | bytes 1327112 | tf_op jit(solution)/shard_map/ppermute | solution.py:647
  25.6 0.0 collective-permute-done.4.other
  25.6 0.0 copy-done.1
  25.6 0.0 copy-done.2
  25.6 3.8 %middle_kernel.1 = (bf16[192,1152]{1,0:T(8,128)(2,1)S(1)}, bf16[192,3456]{1,0:T(8,128)(2,1)S(1)}) custom-call(bf16[192,3456]{1,0:T(8,128)(2,1)S(1)} %get-tuple-element.37.own, bf16[192,1152]{1,0:T(8,128)(2,1)S(1)} %collective-permute-done.4.other, bf16[192,1152]{1,0:T(8,128)(2,1)S(1)} %rim_kernel.1.fresh, bf16[1152,3456]{1,0:T(8,128)(2,1)S(1)} %copy-done, ...), custom_call_target="tpu_custom_call" | custom-call | tf_op jit(solution)/shard_map/middle_kernel/pallas_call | solution.py:561
  29.4 0.0 collective-permute-done.2.side_one
  29.4 0.0 collective-permute-done.3.side_two
  29.4 3.2 %edge_kernel.1.edge = bf16[96,1152]{1,0:T(8,128)(2,1)S(1)} custom-call(s32[2]{0:T(128)S(1)} %pad_add_fusion.odd, bf16[3,12,40,1152]{3,2,1,0:T(8,128)(2,1)S(1)} %get-tuple-element.25.qkv, bf16[1,12,40,128]{3,2,1,0:T(8,128)(2,1)S(1)} %get-tuple-element.26.keep, bf16[2,3,40,2432]{3,2,1,0:T(8,128)(2,1)S(1)} %get-tuple-element.32.halo, ...), custom_call_target="tpu_custom_call" | custom-call | tf_op jit(solution)/shard_map/edge_kernel/pallas_call | solution.py:561
  32.7 0.3 collective-permute-start.5
  33.0 1.6 %edge_own_kernel.1 = (bf16[96,3456]{1,0:T(8,128)(2,1)S(1)}, bf16[6,40,1152]{2,1,0:T(8,128)(2,1)S(1)}, f32[6,16,1152]{2,1,0:T(8,128)S(1)}) custom-call(bf16[96,1152]{1,0:T(8,128)(2,1)S(1)} %edge_kernel.1.edge, bf16[192,1152]{1,0:T(8,128)(2,1)S(1)} %get-tuple-element.38.after.inner, bf16[1152,3456]{1,0:T(8,128)(2,1)S(1)} %copy-done), custom_call_target="tpu_custom_call" | custom-call | tf_op jit(solution)/shard_map/edge_own_kernel/pallas_call | solution.py:561
  34.6 1.9 %collective-permute-done.6.other = bf16[192,1152]{1,0:T(8,128)(2,1)S(1)} collective-permute-done((bf16[192,1152]{1,0:T(8,128)(2,1)S(1)}, bf16[192,1152]{1,0:T(8,128)(2,1)S(1)}, u32[]{:S(2)}, u32[]{:S(2)}) %collective-permute-start.6) | collective-permute-done | bytes 442400 | tf_op jit(solution)/shard_map/ppermute | solution.py:647
  36.5 2.2 %rim_done_kernel.1 = (bf16[6,40,1152]{2,1,0:T(8,128)(2,1)S(1)}, f32[6,16,1152]{2,1,0:T(8,128)S(1)}) custom-call(bf16[192,3456]{1,0:T(8,128)(2,1)S(1)} %get-tuple-element.42.own, bf16[192,1152]{1,0:T(8,128)(2,1)S(1)} %collective-permute-done.6.other, bf16[1152,3456]{1,0:T(8,128)(2,1)S(1)} %copy-done, bf16[1152,128]{1,0:T(8,128)(2,1)S(1)} %copy-done.2, ...), custom_call_target="tpu_custom_call" | custom-call | tf_op jit(solution)/shard_map/rim_done_kernel/pallas_call | solution.py:561
  38.7 0.6 %collective-permute-done.5.other = bf16[96,1152]{1,0:T(8,128)(2,1)S(1)} collective-permute-done((bf16[96,1152]{1,0:T(8,128)(2,1)S(1)}, bf16[96,1152]{1,0:T(8,128)(2,1)S(1)}, u32[]{:S(2)}, u32[]{:S(2)}) %collective-permute-start.5) | collective-permute-done | bytes 221216 | tf_op jit(solution)/shard_map/ppermute | solution.py:667
  39.2 2.3 %last_kernel.1 = bf16[1,12,40,1152]{3,2,1,0:T(8,128)(2,1)} custom-call(bf16[96,3456]{1,0:T(8,128)(2,1)S(1)} %get-tuple-element.39.own, bf16[96,1152]{1,0:T(8,128)(2,1)S(1)} %collective-permute-done.5.other, bf16[1152,3456]{1,0:T(8,128)(2,1)S(1)} %copy-done, bf16[1152,128]{1,0:T(8,128)(2,1)S(1)} %copy-done.2, bf16[128,1152]{1,0:T(8,128)(2,1)S(1)} %copy-done.1, ...), custom_call_target="tpu_custom_call" | custom-call | tf_op jit(solution)/shard_map/last_kernel/pallas_call | solution.py:561
Async XLA Ops:
  0.0 7.1 %copy-start.3 = (f32[2,1152]{1,0:T(2,128)S(1)}, f32[2,1152]{1,0:T(2,128)}, u32[]{:S(2)}) copy-start(f32[2,1152]{1,0:T(2,128)} %modulation.5) | copy-start | bytes 27652
  0.1 11.6 %copy-start = (bf16[1152,3456]{1,0:T(8,128)(2,1)S(1)}, bf16[1152,3456]{1,0:T(8,128)(2,1)}, u32[]{:S(2)}) copy-start(bf16[1152,3456]{1,0:T(8,128)(2,1)} %w_qkv.9) | copy-start | bytes 23887876
  3.2 11.4 %collective-permute-start = (bf16[1,3,40,2432]{3,2,1,0:T(8,128)(2,1)S(1)}, bf16[1,3,40,2432]{3,2,1,0:T(8,128)(2,1)S(1)}, u32[]{:S(2)}, u32[]{:S(2)}) collective-permute-start(bf16[1,3,40,2432]{3,2,1,0:T(8,128)(2,1)S(1)} %get-tuple-element.27), channel_id=1, source_target_pairs={{0,4},{8,12},{4,0},{12,8},{1,5},{9,13},{5,1},{13,9},{2,6},{10,14},... | collective-permute-start | bytes 1751048 | tf_op jit(solution)/shard_map/ppermute | solution.py:611
  3.9 11.4 %collective-permute-start.1 = (bf16[1,3,40,2432]{3,2,1,0:T(8,128)(2,1)S(1)}, bf16[1,3,40,2432]{3,2,1,0:T(8,128)(2,1)S(1)}, u32[]{:S(2)}, u32[]{:S(2)}) collective-permute-start(bf16[1,3,40,2432]{3,2,1,0:T(8,128)(2,1)S(1)} %get-tuple-element.28), channel_id=1, source_target_pairs={{4,8},{8,4},{5,9},{9,5},{6,10},{10,6},{7,11},{11,7},{20,24},{24,20... | collective-permute-start | bytes 1751048 | tf_op jit(solution)/shard_map/ppermute | solution.py:612
  10.4 15.1 %collective-permute-start.4 = (bf16[192,1152]{1,0:T(8,128)(2,1)S(1)}, bf16[192,1152]{1,0:T(8,128)(2,1)S(1)}, u32[]{:S(2)}, u32[]{:S(2)}) collective-permute-start(bf16[192,1152]{1,0:T(8,128)(2,1)S(1)} %get-tuple-element.29.normed), channel_id=1, source_target_pairs={{0,16},{16,0},{1,17},{17,1},{2,18},{18,2},{3,19},{19,3},{4,20},{20... | collective-permute-start | bytes 1327112 | tf_op jit(solution)/shard_map/ppermute | solution.py:622
  16.3 13.1 %collective-permute-start.2 = (bf16[1,18,3,2432]{3,2,1,0:T(4,128)(2,1)S(1)}, bf16[1,18,3,2432]{3,2,1,0:T(4,128)(2,1)S(1)}, u32[]{:S(2)}, u32[]{:S(2)}) collective-permute-start(bf16[1,18,3,2432]{3,2,1,0:T(4,128)(2,1)S(1)} %get-tuple-element.33), channel_id=1, source_target_pairs={{0,1},{2,3},{1,0},{3,2},{4,5},{6,7},{5,4},{7,6},{8,9},{10,11},{9,8... | collective-permute-start | bytes 787976 | tf_op jit(solution)/shard_map/ppermute | solution.py:637
  16.3 13.1 %collective-permute-start.3 = (bf16[1,18,3,2432]{3,2,1,0:T(4,128)(2,1)S(1)}, bf16[1,18,3,2432]{3,2,1,0:T(4,128)(2,1)S(1)}, u32[]{:S(2)}, u32[]{:S(2)}) collective-permute-start(bf16[1,18,3,2432]{3,2,1,0:T(4,128)(2,1)S(1)} %get-tuple-element.34), channel_id=1, source_target_pairs={{1,2},{2,1},{5,6},{6,5},{9,10},{10,9},{13,14},{14,13},{17,18},{18,... | collective-permute-start | bytes 787976 | tf_op jit(solution)/shard_map/ppermute | solution.py:638
  21.0 4.6 %copy-start.1 = (bf16[128,1152]{1,0:T(8,128)(2,1)S(1)}, bf16[128,1152]{1,0:T(8,128)(2,1)}, u32[]{:S(2)}) copy-start(bf16[128,1152]{1,0:T(8,128)(2,1)} %constant.29.clone.spread) | copy-start | bytes 884740
  21.0 4.5 %copy-start.2 = (bf16[1152,128]{1,0:T(8,128)(2,1)S(1)}, bf16[1152,128]{1,0:T(8,128)(2,1)}, u32[]{:S(2)}) copy-start(bf16[1152,128]{1,0:T(8,128)(2,1)} %constant.28.clone.marks) | copy-start | bytes 884740
  24.3 12.2 %collective-permute-start.6 = (bf16[192,1152]{1,0:T(8,128)(2,1)S(1)}, bf16[192,1152]{1,0:T(8,128)(2,1)S(1)}, u32[]{:S(2)}, u32[]{:S(2)}) collective-permute-start(bf16[192,1152]{1,0:T(8,128)(2,1)S(1)} %rim_kernel.1.fresh), channel_id=1, source_target_pairs={{0,16},{16,0},{1,17},{17,1},{2,18},{18,2},{3,19},{19,3},{4,20},{20... | collective-permute-start | bytes 1327112 | tf_op jit(solution)/shard_map/ppermute | solution.py:647
  32.7 6.6 %collective-permute-start.5 = (bf16[96,1152]{1,0:T(8,128)(2,1)S(1)}, bf16[96,1152]{1,0:T(8,128)(2,1)S(1)}, u32[]{:S(2)}, u32[]{:S(2)}) collective-permute-start(bf16[96,1152]{1,0:T(8,128)(2,1)S(1)} %edge_kernel.1.edge), channel_id=1, source_target_pairs={{0,16},{16,0},{1,17},{17,1},{2,18},{18,2},{3,19},{19,3},{4,20},{20... | collective-permute-start | bytes 663560 | tf_op jit(solution)/shard_map/ppermute | solution.py:667

commit v6 on v5

--- a/solution.py
+++ b/solution.py
@@ -473,17 +473,6 @@
     )
 
 
-def middle_kernel(own, other, fresh, w_qkv, marks, spread, out, fresh_own):
-    count, width = other.shape
-    stacked = jnp.concatenate([other[...], fresh[...]], axis=0)
-    query = jnp.dot(fresh[...], w_qkv[:, :width], preferred_element_type=jnp.float32)
-    fresh_own[:, :width] = query.astype(jnp.bfloat16)
-    pairs = jnp.dot(stacked, w_qkv[:, width:], preferred_element_type=jnp.float32).astype(jnp.bfloat16)
-    fresh_own[:, width:] = pairs[count:]
-    mixed = temporal(own[...], pairs[:count, :width], pairs[:count, width:], marks[...], spread[...])
-    out[...] = mixed.astype(jnp.bfloat16)
-
-
 def place(pieces, ready, ends, mixed):
     rows, tile_cols, width = mixed.shape
     for row, column, source, start, count in pieces:
@@ -495,29 +484,41 @@
     ends[:, STRIP:] = mixed[:, tile_cols - STRIP :]
 
 
-def edge_own_kernel(edge, inner, w_qkv, out, ready, ends, mixed):
+def attend_frames(own, other, w_qkv, marks, spread):
+    width = other.shape[1]
+    pairs = jnp.dot(other[...], w_qkv[:, width:], preferred_element_type=jnp.float32).astype(jnp.bfloat16)
+    return temporal(own[...], pairs[:, :width], pairs[:, width:], marks[...], spread[...])
+
+
+def late_own_kernel(rim, edge, w_qkv, rim_own, edge_own):
+    both = jnp.concatenate([rim[...], edge[...]], axis=0)
+    found = jnp.dot(both, w_qkv[...], preferred_element_type=jnp.float32).astype(jnp.bfloat16)
+    rim_own[...] = found[: rim.shape[0]]
+    edge_own[...] = found[rim.shape[0] :]
+
+
+def inner_done_kernel(own, other, w_qkv, marks, spread, after, ready, ends, done, mixed):
     rows, tile_cols, width = mixed.shape
+    done[...] = attend_frames(own, other, w_qkv, marks, spread)
     pieces = []
     for row in range(rows):
         for strip in range(tile_cols // STRIP - 1):
-            pieces.append((row, EDGE + STRIP * strip, inner, (strip * rows + row) * STRIP, STRIP))
+            pieces.append((row, EDGE + STRIP * strip, done, (strip * rows + row) * STRIP, STRIP))
     place(pieces, ready, ends, mixed)
-    out[...] = jnp.dot(edge[...], w_qkv[...], preferred_element_type=jnp.float32).astype(jnp.bfloat16)
-
-
-def rim_done_kernel(own, other, w_qkv, marks, spread, ready, ends, rim, mixed):
+
+
+def rim_done_kernel(own, other, w_qkv, marks, spread, ready, ends, done, mixed):
     rows, tile_cols, width = mixed.shape
-    pairs = jnp.dot(other[...], w_qkv[:, width:], preferred_element_type=jnp.float32).astype(jnp.bfloat16)
-    rim[...] = temporal(own[...], pairs[:, :width], pairs[:, width:], marks[...], spread[...])
+    done[...] = attend_frames(own, other, w_qkv, marks, spread)
     columns = RIM_STRIPS * STRIP
     pieces = []
     for row in range(rows):
         for part in range((tile_cols // STRIP - 1) // RIM_STRIPS):
-            pieces.append((row, EDGE + columns * part, rim, (part * rows + row) * columns, columns))
+            pieces.append((row, EDGE + columns * part, done, (part * rows + row) * columns, columns))
     place(pieces, ready, ends, mixed)
 
 
-def last_kernel(own, other, w_qkv, marks, spread, inner, inner_ends, rim, rim_ends, out, mixed, left, right, arrived):
+def last_kernel(own, other, w_qkv, marks, spread, inner, inner_ends, rim, rim_ends, out, left, right, arrived):
     tile_rows, tile_cols, width = out.shape[1:]
     low, high = RADIUS, tile_rows - RADIUS
     parts = (
@@ -535,15 +536,12 @@
         )
         copy.start()
         whole.append(copy)
-    pairs = jnp.dot(other[...], w_qkv[:, width:], preferred_element_type=jnp.float32).astype(jnp.bfloat16)
-    edge = temporal(own[...], pairs[:, :width], pairs[:, width:], marks[...], spread[...])
+    edge = attend_frames(own, other, w_qkv, marks, spread)
     edge = edge.reshape(tile_rows, STRIP, width)
+    early = iota((1, STRIP, 1), 1) < EDGE
     for target, ready, ends, rows in parts:
-        mixed[target] = ends[rows]
-    mixed[:, 0:EDGE] = edge[:, :EDGE]
-    mixed[:, STRIP + EDGE :] = edge[:, EDGE:]
-    left[...] = mixed[:, :STRIP].astype(jnp.bfloat16)
-    right[...] = mixed[:, STRIP:].astype(jnp.bfloat16)
+        left[target] = jnp.where(early, edge[target], ends[rows, :STRIP]).astype(jnp.bfloat16)
+        right[target] = jnp.where(early, ends[rows, STRIP:], edge[target]).astype(jnp.bfloat16)
     copies = [
         pltpu.make_async_copy(left, out.at[0, :, pl.ds(0, STRIP)], arrived.at[3]),
         pltpu.make_async_copy(right, out.at[0, :, pl.ds(tile_cols - STRIP, STRIP)], arrived.at[4]),
@@ -646,16 +644,23 @@
     )
     rim_other = lax.ppermute(rim, "tm", swap)
 
-    inner_done, rim_own = call(
-        middle_kernel,
-        [struct(inner_count, width), struct(rim_count, 3 * width)],
-        (inner_own, inner_other, rim, w_temporal_qkv, marks, spread),
+    def rows_of(count):
+        whole, ends = (count, tile_cols, width), (count, 2 * STRIP, width)
+        return [held(*whole), pltpu.VMEM(ends, jnp.float32)], pltpu.VMEM(whole, jnp.float32)
+
+    shapes, scratch = rows_of(tile_rows - 2 * RADIUS)
+    inner_ready, inner_ends = call(
+        inner_done_kernel,
+        shapes,
+        (inner_own, inner_other, w_temporal_qkv, marks, spread, rim),
+        [pltpu.VMEM((inner_count, width), jnp.float32), scratch],
+        specs=[(5, anywhere)],
     )
 
     edge = call(
         edge_kernel,
         struct(edge_count, width),
-        (odd, qkv, keep, halo, side_one, side_two, resid, w_spatial_out, modulation, inner_done),
+        (odd, qkv, keep, halo, side_one, side_two, resid, w_spatial_out, modulation, inner_ready),
         [
             held(edge_count, width),
             pltpu.VMEM((pad_rows, 3 * STRIP, lanes), jnp.float32),
@@ -666,16 +671,10 @@
     )
     edge_other = lax.ppermute(edge, "tm", swap)
 
-    def rows_of(count):
-        whole, ends = (count, tile_cols, width), (count, 2 * STRIP, width)
-        return [held(*whole), pltpu.VMEM(ends, jnp.float32)], pltpu.VMEM(whole, jnp.float32)
-
-    shapes, scratch = rows_of(tile_rows - 2 * RADIUS)
-    edge_own, inner_ready, inner_ends = call(
-        edge_own_kernel,
-        [struct(edge_count, 3 * width)] + shapes,
-        (edge, inner_done, w_temporal_qkv),
-        [scratch],
+    rim_own, edge_own = call(
+        late_own_kernel,
+        [struct(rim_count, 3 * width), struct(edge_count, 3 * width)],
+        (rim, edge, w_temporal_qkv),
     )
     shapes, scratch = rows_of(2 * RADIUS)
     rim_ready, rim_ends = call(
@@ -689,7 +688,6 @@
         struct(frame_count, tile_rows, tile_cols, width),
         (edge_own, edge_other, w_temporal_qkv, marks, spread, inner_ready, inner_ends, rim_ready, rim_ends),
         [
-            pltpu.VMEM((tile_rows, 2 * STRIP, width), jnp.float32),
             held(tile_rows, STRIP, width),
             held(tile_rows, STRIP, width),
             pltpu.SemaphoreType.DMA((5,)),

time: 41.9 us -> 41.9 us (level)
  transfers between devices with their start and end apart: 7 -> 7, of which waited for: 3 -> 3; matrix products, arithmetic and copies ran while one was open for 0% -> 0% of each run, Pallas kernels for 51% -> 50%
where the time goes in v6:
time: 41.9 us; the launch traced here: 41.7 us
  Pallas kernels  26.3 us (63%)
  starting transfers between devices  11.5 us (27%)
  waiting for transfers between devices  3.52 us (8%)
    pallas_call x10, Pallas kernels, call(): pl.pallas_call(body, out_shape=out_shape, in_specs=in_specs, out_specs=[V...  26.3 us
    ppermute x1, starting transfers between devices, fast_device(): side_two = lax.ppermute(two, 'col', pairs_two)  4.66 us
    ppermute x1, starting transfers between devices, fast_device(): second = lax.ppermute(two, 'row', pairs_two)  3.18 us
    ppermute x1, waiting for transfers between devices, fast_device(): rim_other = lax.ppermute(rim, 'tm', swap)  2.32 us
    ppermute x1, starting transfers between devices, fast_device(): inner_other = lax.ppermute(inner, 'tm', swap)  1.27 us
    ppermute x1, starting transfers between devices, fast_device(): rim_other = lax.ppermute(rim, 'tm', swap)  1.27 us
  transfers between devices with their start and end apart: 7, of which 3 were waited for; matrix products, arithmetic and copies ran while one was open for 0% of the time, Pallas kernels for 50%

profile of v6, /device:TPU:9, one launch (start us, length us, event | category | flops | bytes accessed | tf_op | source)
XLA Modules:
  0.0 41.7 jit_solution(11711189437216714220)
XLA Ops:
  0.0 0.0 copy-start.3
  0.0 0.1 pad_add_fusion.odd
  0.1 0.0 copy-start
  0.1 3.1 %load_kernel.1 = (bf16[1,3,40,2432]{3,2,1,0:T(8,128)(2,1)S(1)}, bf16[1,3,40,2432]{3,2,1,0:T(8,128)(2,1)S(1)}, bf16[3,12,40,1152]{3,2,1,0:T(8,128)(2,1)S(1)}, bf16[1,12,40,128]{3,2,1,0:T(8,128)(2,1)S(1)}) custom-call(s32[2]{0:T(128)S(1)} %pad_add_fusion.odd, bf16[3,12,40,1152]{3,2,1,0:T(8,128)(2,1)} %bitcast.4, s32[12,1,40]{2,1,0:T(1,128)} %bitcast.5), custom_call_target="tpu_custom_call" | custom-call | tf_op jit(solution)/shard_map/load_kernel/pallas_call | solution.py:559
  3.2 0.7 %collective-permute-start = (bf16[1,3,40,2432]{3,2,1,0:T(8,128)(2,1)S(1)}, bf16[1,3,40,2432]{3,2,1,0:T(8,128)(2,1)S(1)}, u32[]{:S(2)}, u32[]{:S(2)}) collective-permute-start(bf16[1,3,40,2432]{3,2,1,0:T(8,128)(2,1)S(1)} %get-tuple-element.26), channel_id=1, source_target_pairs={{0,4},{8,12},{4,0},{12,8},{1,5},{9,13},{5,1},{13,9},{2,6},{10,14},... | collective-permute-start | bytes 1751048 | tf_op jit(solution)/shard_map/ppermute | solution.py:609
  3.9 3.2 %collective-permute-start.1 = (bf16[1,3,40,2432]{3,2,1,0:T(8,128)(2,1)S(1)}, bf16[1,3,40,2432]{3,2,1,0:T(8,128)(2,1)S(1)}, u32[]{:S(2)}, u32[]{:S(2)}) collective-permute-start(bf16[1,3,40,2432]{3,2,1,0:T(8,128)(2,1)S(1)} %get-tuple-element.27), channel_id=1, source_target_pairs={{4,8},{8,4},{5,9},{9,5},{6,10},{10,6},{7,11},{11,7},{20,24},{24,20... | collective-permute-start | bytes 1751048 | tf_op jit(solution)/shard_map/ppermute | solution.py:610
  7.1 0.0 copy-done.3
  7.1 3.3 %inner_kernel.1 = (bf16[192,1152]{1,0:T(8,128)(2,1)S(1)}, bf16[1,12,40,1152]{3,2,1,0:T(8,128)(2,1)S(1)}, bf16[1152,1152]{1,0:T(8,128)(2,1)S(1)}) custom-call(bf16[3,12,40,1152]{3,2,1,0:T(8,128)(2,1)S(1)} %get-tuple-element.24.qkv, bf16[1,12,40,128]{3,2,1,0:T(8,128)(2,1)S(1)} %get-tuple-element.25.keep, bf16[1,12,40,1152]{3,2,1,0:T(8,128)(2,1)} %resid_hbm.1, ...), custom_call_target="tpu_custom_call" | custom-call | tf_op jit(solution)/shard_map/inner_kernel/pallas_call | solution.py:559
  10.4 1.3 %collective-permute-start.4 = (bf16[192,1152]{1,0:T(8,128)(2,1)S(1)}, bf16[192,1152]{1,0:T(8,128)(2,1)S(1)}, u32[]{:S(2)}, u32[]{:S(2)}) collective-permute-start(bf16[192,1152]{1,0:T(8,128)(2,1)S(1)} %get-tuple-element.28.normed), channel_id=1, source_target_pairs={{0,16},{16,0},{1,17},{17,1},{2,18},{18,2},{3,19},{19,3},{4,20},{20... | collective-permute-start | bytes 1327112 | tf_op jit(solution)/shard_map/ppermute | solution.py:620
  11.7 0.0 copy-done
  11.7 2.9 %own_kernel.1 = (bf16[192,3456]{1,0:T(8,128)(2,1)S(1)}, bf16[12,3,2432]{2,1,0:T(4,128)(2,1)S(1)}, bf16[12,3,2432]{2,1,0:T(4,128)(2,1)S(1)}) custom-call(s32[2]{0:T(128)S(1)} %pad_add_fusion.odd, bf16[192,1152]{1,0:T(8,128)(2,1)S(1)} %get-tuple-element.28.normed, bf16[1152,3456]{1,0:T(8,128)(2,1)S(1)} %copy-done, ...), custom_call_target="tpu_custom_call" | custom-call | tf_op jit(solution)/shard_map/own_kernel/pallas_call | solution.py:559
  14.6 0.0 collective-permute-done.first
  14.6 0.7 %collective-permute-done.1.second = bf16[1,3,40,2432]{3,2,1,0:T(8,128)(2,1)S(1)} collective-permute-done((bf16[1,3,40,2432]{3,2,1,0:T(8,128)(2,1)S(1)}, bf16[1,3,40,2432]{3,2,1,0:T(8,128)(2,1)S(1)}, u32[]{:S(2)}, u32[]{:S(2)}) %collective-permute-start.1) | collective-permute-done | bytes 583712 | tf_op jit(solution)/shard_map/ppermute | solution.py:610
  15.4 0.9 %columns_kernel.1 = (bf16[1,18,3,2432]{3,2,1,0:T(4,128)(2,1)S(1)}, bf16[1,18,3,2432]{3,2,1,0:T(4,128)(2,1)S(1)}, bf16[2,3,40,2432]{3,2,1,0:T(8,128)(2,1)S(1)}) custom-call(s32[2]{0:T(128)S(1)} %pad_add_fusion.odd, bf16[1,3,40,2432]{3,2,1,0:T(8,128)(2,1)S(1)} %collective-permute-done.first, bf16[1,3,40,2432]{3,2,1,0:T(8,128)(2,1)S(1)} %collective-permute-done.1.second, ...), custom_call_target="tpu_custom_call" | custom-call | tf_op jit(solution)/shard_map/columns_kernel/pallas_call | solution.py:559
  16.3 0.1 collective-permute-start.2
  16.3 4.7 %collective-permute-start.3 = (bf16[1,18,3,2432]{3,2,1,0:T(4,128)(2,1)S(1)}, bf16[1,18,3,2432]{3,2,1,0:T(4,128)(2,1)S(1)}, u32[]{:S(2)}, u32[]{:S(2)}) collective-permute-start(bf16[1,18,3,2432]{3,2,1,0:T(4,128)(2,1)S(1)} %get-tuple-element.35), channel_id=1, source_target_pairs={{1,2},{2,1},{5,6},{6,5},{9,10},{10,9},{13,14},{14,13},{17,18},{18,... | collective-permute-start | bytes 787976 | tf_op jit(solution)/shard_map/ppermute | solution.py:636
  21.0 0.0 copy-start.1
  21.0 0.0 copy-start.2
  21.0 3.2 %rim_kernel.1.after.rim = bf16[192,1152]{1,0:T(8,128)(2,1)S(1)} custom-call(bf16[3,12,40,1152]{3,2,1,0:T(8,128)(2,1)S(1)} %get-tuple-element.24.qkv, bf16[1,12,40,128]{3,2,1,0:T(8,128)(2,1)S(1)} %get-tuple-element.25.keep, bf16[2,3,40,2432]{3,2,1,0:T(8,128)(2,1)S(1)} %get-tuple-element.31.halo, bf16[1,12,40,1152]{3,2,1,0:T(8,128)(2,1)S(1)} %get-tuple-element.32.resid, ...), custom_call_target="tpu_custom_call" | custom-call | tf_op jit(solution)/shard_map/rim_kernel/pallas_call | solution.py:559
  24.3 1.3 %collective-permute-start.6 = (bf16[192,1152]{1,0:T(8,128)(2,1)S(1)}, bf16[192,1152]{1,0:T(8,128)(2,1)S(1)}, u32[]{:S(2)}, u32[]{:S(2)}) collective-permute-start(bf16[192,1152]{1,0:T(8,128)(2,1)S(1)} %rim_kernel.1.after.rim), channel_id=1, source_target_pairs={{0,16},{16,0},{1,17},{17,1},{2,18},{18,2},{3,19},{19,3},{4,20},{20... | collective-permute-start | bytes 1327112 | tf_op jit(solution)/shard_map/ppermute | solution.py:645
  25.6 0.0 collective-permute-done.4.other
  25.6 0.0 copy-done.1
  25.6 0.0 copy-done.2
  25.6 2.2 %inner_done_kernel.1 = (bf16[6,40,1152]{2,1,0:T(8,128)(2,1)S(1)}, f32[6,16,1152]{2,1,0:T(8,128)S(1)}) custom-call(bf16[192,3456]{1,0:T(8,128)(2,1)S(1)} %get-tuple-element.36.own, bf16[192,1152]{1,0:T(8,128)(2,1)S(1)} %collective-permute-done.4.other, bf16[1152,3456]{1,0:T(8,128)(2,1)S(1)} %copy-done, bf16[1152,128]{1,0:T(8,128)(2,1)S(1)} %copy-done.2, ...), custom_call_target="tpu_custom_call" | custom-call | tf_op jit(solution)/shard_map/inner_done_kernel/pallas_call | solution.py:559
  27.8 0.0 collective-permute-done.2.side_one
  27.8 0.0 collective-permute-done.3.side_two
  27.8 3.3 %edge_kernel.1.edge = bf16[96,1152]{1,0:T(8,128)(2,1)S(1)} custom-call(s32[2]{0:T(128)S(1)} %pad_add_fusion.odd, bf16[3,12,40,1152]{3,2,1,0:T(8,128)(2,1)S(1)} %get-tuple-element.24.qkv, bf16[1,12,40,128]{3,2,1,0:T(8,128)(2,1)S(1)} %get-tuple-element.25.keep, bf16[2,3,40,2432]{3,2,1,0:T(8,128)(2,1)S(1)} %get-tuple-element.31.halo, ...), custom_call_target="tpu_custom_call" | custom-call | tf_op jit(solution)/shard_map/edge_kernel/pallas_call | solution.py:559
  31.1 0.3 collective-permute-start.5
  31.4 2.9 %late_own_kernel.1 = (bf16[192,3456]{1,0:T(8,128)(2,1)S(1)}, bf16[96,3456]{1,0:T(8,128)(2,1)S(1)}) custom-call(bf16[192,1152]{1,0:T(8,128)(2,1)S(1)} %rim_kernel.1.after.rim, bf16[96,1152]{1,0:T(8,128)(2,1)S(1)} %edge_kernel.1.edge, bf16[1152,3456]{1,0:T(8,128)(2,1)S(1)} %copy-done), custom_call_target="tpu_custom_call" | custom-call | tf_op jit(solution)/shard_map/late_own_kernel/pallas_call | solution.py:559
  34.3 2.3 %collective-permute-done.6.other = bf16[192,1152]{1,0:T(8,128)(2,1)S(1)} collective-permute-done((bf16[192,1152]{1,0:T(8,128)(2,1)S(1)}, bf16[192,1152]{1,0:T(8,128)(2,1)S(1)}, u32[]{:S(2)}, u32[]{:S(2)}) %collective-permute-start.6) | collective-permute-done | bytes 442400 | tf_op jit(solution)/shard_map/ppermute | solution.py:645
  36.6 2.2 %rim_done_kernel.1 = (bf16[6,40,1152]{2,1,0:T(8,128)(2,1)S(1)}, f32[6,16,1152]{2,1,0:T(8,128)S(1)}) custom-call(bf16[192,3456]{1,0:T(8,128)(2,1)S(1)} %get-tuple-element.40.own, bf16[192,1152]{1,0:T(8,128)(2,1)S(1)} %collective-permute-done.6.other, bf16[1152,3456]{1,0:T(8,128)(2,1)S(1)} %copy-done, bf16[1152,128]{1,0:T(8,128)(2,1)S(1)} %copy-done.2, ...), custom_call_target="tpu_custom_call" | custom-call | tf_op jit(solution)/shard_map/rim_done_kernel/pallas_call | solution.py:559
  38.8 0.5 %collective-permute-done.5.other = bf16[96,1152]{1,0:T(8,128)(2,1)S(1)} collective-permute-done((bf16[96,1152]{1,0:T(8,128)(2,1)S(1)}, bf16[96,1152]{1,0:T(8,128)(2,1)S(1)}, u32[]{:S(2)}, u32[]{:S(2)}) %collective-permute-start.5) | collective-permute-done | bytes 221216 | tf_op jit(solution)/shard_map/ppermute | solution.py:672
  39.2 2.3 %last_kernel.1 = bf16[1,12,40,1152]{3,2,1,0:T(8,128)(2,1)} custom-call(bf16[96,3456]{1,0:T(8,128)(2,1)S(1)} %get-tuple-element.38.own, bf16[96,1152]{1,0:T(8,128)(2,1)S(1)} %collective-permute-done.5.other, bf16[1152,3456]{1,0:T(8,128)(2,1)S(1)} %copy-done, bf16[1152,128]{1,0:T(8,128)(2,1)S(1)} %copy-done.2, bf16[128,1152]{1,0:T(8,128)(2,1)S(1)} %copy-done.1, ...), custom_call_target="tpu_custom_call" | custom-call | tf_op jit(solution)/shard_map/last_kernel/pallas_call | solution.py:559
Async XLA Ops:
  0.0 7.1 %copy-start.3 = (f32[2,1152]{1,0:T(2,128)S(1)}, f32[2,1152]{1,0:T(2,128)}, u32[]{:S(2)}) copy-start(f32[2,1152]{1,0:T(2,128)} %modulation.5) | copy-start | bytes 27652
  0.1 11.6 %copy-start = (bf16[1152,3456]{1,0:T(8,128)(2,1)S(1)}, bf16[1152,3456]{1,0:T(8,128)(2,1)}, u32[]{:S(2)}) copy-start(bf16[1152,3456]{1,0:T(8,128)(2,1)} %w_qkv.9) | copy-start | bytes 23887876
  3.2 11.4 %collective-permute-start = (bf16[1,3,40,2432]{3,2,1,0:T(8,128)(2,1)S(1)}, bf16[1,3,40,2432]{3,2,1,0:T(8,128)(2,1)S(1)}, u32[]{:S(2)}, u32[]{:S(2)}) collective-permute-start(bf16[1,3,40,2432]{3,2,1,0:T(8,128)(2,1)S(1)} %get-tuple-element.26), channel_id=1, source_target_pairs={{0,4},{8,12},{4,0},{12,8},{1,5},{9,13},{5,1},{13,9},{2,6},{10,14},... | collective-permute-start | bytes 1751048 | tf_op jit(solution)/shard_map/ppermute | solution.py:609
  3.9 11.4 %collective-permute-start.1 = (bf16[1,3,40,2432]{3,2,1,0:T(8,128)(2,1)S(1)}, bf16[1,3,40,2432]{3,2,1,0:T(8,128)(2,1)S(1)}, u32[]{:S(2)}, u32[]{:S(2)}) collective-permute-start(bf16[1,3,40,2432]{3,2,1,0:T(8,128)(2,1)S(1)} %get-tuple-element.27), channel_id=1, source_target_pairs={{4,8},{8,4},{5,9},{9,5},{6,10},{10,6},{7,11},{11,7},{20,24},{24,20... | collective-permute-start | bytes 1751048 | tf_op jit(solution)/shard_map/ppermute | solution.py:610
  10.4 15.1 %collective-permute-start.4 = (bf16[192,1152]{1,0:T(8,128)(2,1)S(1)}, bf16[192,1152]{1,0:T(8,128)(2,1)S(1)}, u32[]{:S(2)}, u32[]{:S(2)}) collective-permute-start(bf16[192,1152]{1,0:T(8,128)(2,1)S(1)} %get-tuple-element.28.normed), channel_id=1, source_target_pairs={{0,16},{16,0},{1,17},{17,1},{2,18},{18,2},{3,19},{19,3},{4,20},{20... | collective-permute-start | bytes 1327112 | tf_op jit(solution)/shard_map/ppermute | solution.py:620
  16.3 11.5 %collective-permute-start.2 = (bf16[1,18,3,2432]{3,2,1,0:T(4,128)(2,1)S(1)}, bf16[1,18,3,2432]{3,2,1,0:T(4,128)(2,1)S(1)}, u32[]{:S(2)}, u32[]{:S(2)}) collective-permute-start(bf16[1,18,3,2432]{3,2,1,0:T(4,128)(2,1)S(1)} %get-tuple-element.34), channel_id=1, source_target_pairs={{0,1},{2,3},{1,0},{3,2},{4,5},{6,7},{5,4},{7,6},{8,9},{10,11},{9,8... | collective-permute-start | bytes 787976 | tf_op jit(solution)/shard_map/ppermute | solution.py:635
  16.3 11.4 %collective-permute-start.3 = (bf16[1,18,3,2432]{3,2,1,0:T(4,128)(2,1)S(1)}, bf16[1,18,3,2432]{3,2,1,0:T(4,128)(2,1)S(1)}, u32[]{:S(2)}, u32[]{:S(2)}) collective-permute-start(bf16[1,18,3,2432]{3,2,1,0:T(4,128)(2,1)S(1)} %get-tuple-element.35), channel_id=1, source_target_pairs={{1,2},{2,1},{5,6},{6,5},{9,10},{10,9},{13,14},{14,13},{17,18},{18,... | collective-permute-start | bytes 787976 | tf_op jit(solution)/shard_map/ppermute | solution.py:636
  21.0 4.6 %copy-start.1 = (bf16[128,1152]{1,0:T(8,128)(2,1)S(1)}, bf16[128,1152]{1,0:T(8,128)(2,1)}, u32[]{:S(2)}) copy-start(bf16[128,1152]{1,0:T(8,128)(2,1)} %constant.29.clone.spread) | copy-start | bytes 884740
  21.0 4.5 %copy-start.2 = (bf16[1152,128]{1,0:T(8,128)(2,1)S(1)}, bf16[1152,128]{1,0:T(8,128)(2,1)}, u32[]{:S(2)}) copy-start(bf16[1152,128]{1,0:T(8,128)(2,1)} %constant.28.clone.marks) | copy-start | bytes 884740
  24.3 12.3 %collective-permute-start.6 = (bf16[192,1152]{1,0:T(8,128)(2,1)S(1)}, bf16[192,1152]{1,0:T(8,128)(2,1)S(1)}, u32[]{:S(2)}, u32[]{:S(2)}) collective-permute-start(bf16[192,1152]{1,0:T(8,128)(2,1)S(1)} %rim_kernel.1.after.rim), channel_id=1, source_target_pairs={{0,16},{16,0},{1,17},{17,1},{2,18},{18,2},{3,19},{19,3},{4,20},{20... | collective-permute-start | bytes 1327112 | tf_op jit(solution)/shard_map/ppermute | solution.py:645
  31.1 8.2 %collective-permute-start.5 = (bf16[96,1152]{1,0:T(8,128)(2,1)S(1)}, bf16[96,1152]{1,0:T(8,128)(2,1)S(1)}, u32[]{:S(2)}, u32[]{:S(2)}) collective-permute-start(bf16[96,1152]{1,0:T(8,128)(2,1)S(1)} %edge_kernel.1.edge), channel_id=1, source_target_pairs={{0,16},{16,0},{1,17},{17,1},{2,18},{18,2},{3,19},{19,3},{4,20},{20... | collective-permute-start | bytes 663560 | tf_op jit(solution)/shard_map/ppermute | solution.py:672

commit v7 on v6

--- a/solution.py
+++ b/solution.py
@@ -202,7 +202,10 @@
 
 
 def finish(heads, resid, w_out, modulation):
-    stream = resid + jnp.dot(heads, w_out, preferred_element_type=jnp.float32)
+    return adapt(resid + jnp.dot(heads, w_out, preferred_element_type=jnp.float32), modulation)
+
+
+def adapt(stream, modulation):
     average = jnp.mean(stream, -1, keepdims=True)
     centered = stream - average
     variance = jnp.mean(centered * centered, -1, keepdims=True)
@@ -241,8 +244,8 @@
 
 def inner_kernel(qkv, keep, resid_hbm, w_hbm, modulation, out, resid, w_out, heads, arrived):
     copies = [
-        pltpu.make_async_copy(resid_hbm, resid, arrived.at[0]),
-        pltpu.make_async_copy(w_hbm, w_out, arrived.at[1]),
+        pltpu.make_async_copy(w_hbm, w_out, arrived.at[0]),
+        pltpu.make_async_copy(resid_hbm, resid, arrived.at[1]),
     ]
     for copy in copies:
         copy.start()
@@ -268,10 +271,11 @@
             )
     mixed = batched(tiles, INNER_BATCH * rows // step)
     heads[...] = jnp.concatenate(mixed, axis=0).astype(jnp.bfloat16)
-    for copy in copies:
-        copy.wait()
+    copies[0].wait()
+    product = jnp.dot(heads[...], w_out[...], preferred_element_type=jnp.float32)
+    copies[1].wait()
     source = jnp.concatenate([middle(resid, 0, mine, strip) for strip in range(strips)], axis=0)
-    out[...] = finish(heads[...], source, w_out[...], modulation[...]).reshape(out.shape)
+    out[...] = adapt(source + product, modulation[...]).reshape(out.shape)
 
 
 def rim_kernel(qkv, keep, halo, resid, w_out, modulation, out, heads):
@@ -438,8 +442,9 @@
 
 
 def mark_heads(width):
-    row, feature = np.arange(LANES)[:, None], np.arange(width)[None, :]
-    return jnp.asarray((feature // (width // HEADS) == row % HEADS) & (row < 2 * HEADS), jnp.bfloat16)
+    row, feature = np.arange(LANES)[:, None], np.arange(2 * width)[None, :]
+    mine = (feature % width) // (width // HEADS) == row % HEADS
+    return jnp.asarray(mine & (row // (2 * HEADS) == feature // width), jnp.bfloat16)
 
 
 def halves_of(values):
@@ -462,15 +467,19 @@
     other_weight = jnp.exp(jnp.minimum(gap, 0.0))
     inverse = 1.0 / (own_weight + other_weight)
 
-    def share(weight):
-        part = weight.astype(jnp.bfloat16).astype(jnp.float32) * inverse
-        high, low = halves_of(part)
-        packed = jnp.where(lane < HEADS, high.astype(jnp.float32), low.astype(jnp.float32)).astype(jnp.bfloat16)
-        return jnp.dot(packed, spread, preferred_element_type=jnp.float32)
-
-    return share(own_weight) * own[:, 2 * width :].astype(jnp.float32) + share(other_weight) * other_value.astype(
-        jnp.float32
-    )
+    def halves(weight):
+        return [x.astype(jnp.float32) for x in halves_of(weight.astype(jnp.bfloat16).astype(jnp.float32) * inverse)]
+
+    own_high, own_low = halves(own_weight)
+    other_high, other_low = halves(other_weight)
+    packed = jnp.where(
+        lane < 2 * HEADS,
+        jnp.where(lane < HEADS, own_high, own_low),
+        jnp.where(lane < 3 * HEADS, other_high, other_low),
+    )
+    shares = jnp.dot(packed.astype(jnp.bfloat16), spread, preferred_element_type=jnp.float32)
+    own_part = shares[:, :width] * own[:, 2 * width :].astype(jnp.float32)
+    return own_part + shares[:, width:] * other_value.astype(jnp.float32)
 
 
 def place(pieces, ready, ends, mixed):

time: 41.9 us -> 41.9 us (level)
  no operation moved by 1% of the time
where the time goes in v7:
time: 41.9 us; the launch traced here: 41.8 us
  Pallas kernels  26.4 us (63%)
  starting transfers between devices  11.5 us (27%)
  waiting for transfers between devices  3.48 us (8%)
    pallas_call x10, Pallas kernels, call(): pl.pallas_call(body, out_shape=out_shape, in_specs=in_specs, out_specs=[V...  26.4 us
    ppermute x1, starting transfers between devices, fast_device(): side_two = lax.ppermute(two, 'col', pairs_two)  4.66 us
    ppermute x1, starting transfers between devices, fast_device(): second = lax.ppermute(two, 'row', pairs_two)  3.18 us
    ppermute x1, waiting for transfers between devices, fast_device(): rim_other = lax.ppermute(rim, 'tm', swap)  2.32 us
    ppermute x1, starting transfers between devices, fast_device(): inner_other = lax.ppermute(inner, 'tm', swap)  1.27 us
    ppermute x1, starting transfers between devices, fast_device(): rim_other = lax.ppermute(rim, 'tm', swap)  1.27 us
  transfers between devices with their start and end apart: 7, of which 3 were waited for; matrix products, arithmetic and copies ran while one was open for 0% of the time, Pallas kernels for 50%

profile of v7, /device:TPU:9, one launch (start us, length us, event | category | flops | bytes accessed | tf_op | source)
XLA Modules:
  0.0 41.8 jit_solution(16023073248777533)
XLA Ops:
  0.0 0.0 copy-start.3
  0.0 0.1 pad_add_fusion.odd
  0.1 0.0 copy-start
  0.1 3.1 %load_kernel.1 = (bf16[1,3,40,2432]{3,2,1,0:T(8,128)(2,1)S(1)}, bf16[1,3,40,2432]{3,2,1,0:T(8,128)(2,1)S(1)}, bf16[3,12,40,1152]{3,2,1,0:T(8,128)(2,1)S(1)}, bf16[1,12,40,128]{3,2,1,0:T(8,128)(2,1)S(1)}) custom-call(s32[2]{0:T(128)S(1)} %pad_add_fusion.odd, bf16[3,12,40,1152]{3,2,1,0:T(8,128)(2,1)} %bitcast.4, s32[12,1,40]{2,1,0:T(1,128)} %bitcast.5), custom_call_target="tpu_custom_call" | custom-call | tf_op jit(solution)/shard_map/load_kernel/pallas_call | solution.py:568
  3.2 0.7 %collective-permute-start = (bf16[1,3,40,2432]{3,2,1,0:T(8,128)(2,1)S(1)}, bf16[1,3,40,2432]{3,2,1,0:T(8,128)(2,1)S(1)}, u32[]{:S(2)}, u32[]{:S(2)}) collective-permute-start(bf16[1,3,40,2432]{3,2,1,0:T(8,128)(2,1)S(1)} %get-tuple-element.26), channel_id=1, source_target_pairs={{0,4},{8,12},{4,0},{12,8},{1,5},{9,13},{5,1},{13,9},{2,6},{10,14},... | collective-permute-start | bytes 1751048 | tf_op jit(solution)/shard_map/ppermute | solution.py:618
  3.9 3.2 %collective-permute-start.1 = (bf16[1,3,40,2432]{3,2,1,0:T(8,128)(2,1)S(1)}, bf16[1,3,40,2432]{3,2,1,0:T(8,128)(2,1)S(1)}, u32[]{:S(2)}, u32[]{:S(2)}) collective-permute-start(bf16[1,3,40,2432]{3,2,1,0:T(8,128)(2,1)S(1)} %get-tuple-element.27), channel_id=1, source_target_pairs={{4,8},{8,4},{5,9},{9,5},{6,10},{10,6},{7,11},{11,7},{20,24},{24,20... | collective-permute-start | bytes 1751048 | tf_op jit(solution)/shard_map/ppermute | solution.py:619
  7.1 0.0 copy-done.3
  7.1 3.4 %inner_kernel.1 = (bf16[192,1152]{1,0:T(8,128)(2,1)S(1)}, bf16[1,12,40,1152]{3,2,1,0:T(8,128)(2,1)S(1)}, bf16[1152,1152]{1,0:T(8,128)(2,1)S(1)}) custom-call(bf16[3,12,40,1152]{3,2,1,0:T(8,128)(2,1)S(1)} %get-tuple-element.24.qkv, bf16[1,12,40,128]{3,2,1,0:T(8,128)(2,1)S(1)} %get-tuple-element.25.keep, bf16[1,12,40,1152]{3,2,1,0:T(8,128)(2,1)} %resid_hbm.1, ...), custom_call_target="tpu_custom_call" | custom-call | tf_op jit(solution)/shard_map/inner_kernel/pallas_call | solution.py:568
  10.5 1.3 %collective-permute-start.4 = (bf16[192,1152]{1,0:T(8,128)(2,1)S(1)}, bf16[192,1152]{1,0:T(8,128)(2,1)S(1)}, u32[]{:S(2)}, u32[]{:S(2)}) collective-permute-start(bf16[192,1152]{1,0:T(8,128)(2,1)S(1)} %get-tuple-element.28.normed), channel_id=1, source_target_pairs={{0,16},{16,0},{1,17},{17,1},{2,18},{18,2},{3,19},{19,3},{4,20},{20... | collective-permute-start | bytes 1327112 | tf_op jit(solution)/shard_map/ppermute | solution.py:629
  11.8 0.0 copy-done
  11.8 2.9 %own_kernel.1 = (bf16[192,3456]{1,0:T(8,128)(2,1)S(1)}, bf16[12,3,2432]{2,1,0:T(4,128)(2,1)S(1)}, bf16[12,3,2432]{2,1,0:T(4,128)(2,1)S(1)}) custom-call(s32[2]{0:T(128)S(1)} %pad_add_fusion.odd, bf16[192,1152]{1,0:T(8,128)(2,1)S(1)} %get-tuple-element.28.normed, bf16[1152,3456]{1,0:T(8,128)(2,1)S(1)} %copy-done, ...), custom_call_target="tpu_custom_call" | custom-call | tf_op jit(solution)/shard_map/own_kernel/pallas_call | solution.py:568
  14.7 0.0 collective-permute-done.first
  14.7 0.7 %collective-permute-done.1.second = bf16[1,3,40,2432]{3,2,1,0:T(8,128)(2,1)S(1)} collective-permute-done((bf16[1,3,40,2432]{3,2,1,0:T(8,128)(2,1)S(1)}, bf16[1,3,40,2432]{3,2,1,0:T(8,128)(2,1)S(1)}, u32[]{:S(2)}, u32[]{:S(2)}) %collective-permute-start.1) | collective-permute-done | bytes 583712 | tf_op jit(solution)/shard_map/ppermute | solution.py:619
  15.4 0.9 %columns_kernel.1 = (bf16[1,18,3,2432]{3,2,1,0:T(4,128)(2,1)S(1)}, bf16[1,18,3,2432]{3,2,1,0:T(4,128)(2,1)S(1)}, bf16[2,3,40,2432]{3,2,1,0:T(8,128)(2,1)S(1)}) custom-call(s32[2]{0:T(128)S(1)} %pad_add_fusion.odd, bf16[1,3,40,2432]{3,2,1,0:T(8,128)(2,1)S(1)} %collective-permute-done.first, bf16[1,3,40,2432]{3,2,1,0:T(8,128)(2,1)S(1)} %collective-permute-done.1.second, ...), custom_call_target="tpu_custom_call" | custom-call | tf_op jit(solution)/shard_map/columns_kernel/pallas_call | solution.py:568
  16.3 0.1 collective-permute-start.2
  16.3 4.7 %collective-permute-start.3 = (bf16[1,18,3,2432]{3,2,1,0:T(4,128)(2,1)S(1)}, bf16[1,18,3,2432]{3,2,1,0:T(4,128)(2,1)S(1)}, u32[]{:S(2)}, u32[]{:S(2)}) collective-permute-start(bf16[1,18,3,2432]{3,2,1,0:T(4,128)(2,1)S(1)} %get-tuple-element.35), channel_id=1, source_target_pairs={{1,2},{2,1},{5,6},{6,5},{9,10},{10,9},{13,14},{14,13},{17,18},{18,... | collective-permute-start | bytes 787976 | tf_op jit(solution)/shard_map/ppermute | solution.py:645
  21.0 0.0 copy-start.1
  21.0 0.0 copy-start.2
  21.0 3.2 %rim_kernel.1.after.rim = bf16[192,1152]{1,0:T(8,128)(2,1)S(1)} custom-call(bf16[3,12,40,1152]{3,2,1,0:T(8,128)(2,1)S(1)} %get-tuple-element.24.qkv, bf16[1,12,40,128]{3,2,1,0:T(8,128)(2,1)S(1)} %get-tuple-element.25.keep, bf16[2,3,40,2432]{3,2,1,0:T(8,128)(2,1)S(1)} %get-tuple-element.31.halo, bf16[1,12,40,1152]{3,2,1,0:T(8,128)(2,1)S(1)} %get-tuple-element.32.resid, ...), custom_call_target="tpu_custom_call" | custom-call | tf_op jit(solution)/shard_map/rim_kernel/pallas_call | solution.py:568
  24.3 1.3 %collective-permute-start.6 = (bf16[192,1152]{1,0:T(8,128)(2,1)S(1)}, bf16[192,1152]{1,0:T(8,128)(2,1)S(1)}, u32[]{:S(2)}, u32[]{:S(2)}) collective-permute-start(bf16[192,1152]{1,0:T(8,128)(2,1)S(1)} %rim_kernel.1.after.rim), channel_id=1, source_target_pairs={{0,16},{16,0},{1,17},{17,1},{2,18},{18,2},{3,19},{19,3},{4,20},{20... | collective-permute-start | bytes 1327112 | tf_op jit(solution)/shard_map/ppermute | solution.py:654
  25.6 0.0 collective-permute-done.4.other
  25.6 0.0 copy-done.1
  25.6 0.0 copy-done.2
  25.6 2.2 %inner_done_kernel.1 = (bf16[6,40,1152]{2,1,0:T(8,128)(2,1)S(1)}, f32[6,16,1152]{2,1,0:T(8,128)S(1)}) custom-call(bf16[192,3456]{1,0:T(8,128)(2,1)S(1)} %get-tuple-element.36.own, bf16[192,1152]{1,0:T(8,128)(2,1)S(1)} %collective-permute-done.4.other, bf16[1152,3456]{1,0:T(8,128)(2,1)S(1)} %copy-done, bf16[1152,128]{1,0:T(8,128)(2,1)S(1)} %copy-done.2, ...), custom_call_target="tpu_custom_call" | custom-call | tf_op jit(solution)/shard_map/inner_done_kernel/pallas_call | solution.py:568
  27.8 0.0 collective-permute-done.2.side_one
  27.8 0.0 collective-permute-done.3.side_two
  27.8 3.3 %edge_kernel.1.edge = bf16[96,1152]{1,0:T(8,128)(2,1)S(1)} custom-call(s32[2]{0:T(128)S(1)} %pad_add_fusion.odd, bf16[3,12,40,1152]{3,2,1,0:T(8,128)(2,1)S(1)} %get-tuple-element.24.qkv, bf16[1,12,40,128]{3,2,1,0:T(8,128)(2,1)S(1)} %get-tuple-element.25.keep, bf16[2,3,40,2432]{3,2,1,0:T(8,128)(2,1)S(1)} %get-tuple-element.31.halo, ...), custom_call_target="tpu_custom_call" | custom-call | tf_op jit(solution)/shard_map/edge_kernel/pallas_call | solution.py:568
  31.1 0.3 collective-permute-start.5
  31.4 2.9 %late_own_kernel.1 = (bf16[192,3456]{1,0:T(8,128)(2,1)S(1)}, bf16[96,3456]{1,0:T(8,128)(2,1)S(1)}) custom-call(bf16[192,1152]{1,0:T(8,128)(2,1)S(1)} %rim_kernel.1.after.rim, bf16[96,1152]{1,0:T(8,128)(2,1)S(1)} %edge_kernel.1.edge, bf16[1152,3456]{1,0:T(8,128)(2,1)S(1)} %copy-done), custom_call_target="tpu_custom_call" | custom-call | tf_op jit(solution)/shard_map/late_own_kernel/pallas_call | solution.py:568
  34.3 2.3 %collective-permute-done.6.other = bf16[192,1152]{1,0:T(8,128)(2,1)S(1)} collective-permute-done((bf16[192,1152]{1,0:T(8,128)(2,1)S(1)}, bf16[192,1152]{1,0:T(8,128)(2,1)S(1)}, u32[]{:S(2)}, u32[]{:S(2)}) %collective-permute-start.6) | collective-permute-done | bytes 442400 | tf_op jit(solution)/shard_map/ppermute | solution.py:654
  36.6 2.2 %rim_done_kernel.1 = (bf16[6,40,1152]{2,1,0:T(8,128)(2,1)S(1)}, f32[6,16,1152]{2,1,0:T(8,128)S(1)}) custom-call(bf16[192,3456]{1,0:T(8,128)(2,1)S(1)} %get-tuple-element.40.own, bf16[192,1152]{1,0:T(8,128)(2,1)S(1)} %collective-permute-done.6.other, bf16[1152,3456]{1,0:T(8,128)(2,1)S(1)} %copy-done, bf16[1152,128]{1,0:T(8,128)(2,1)S(1)} %copy-done.2, ...), custom_call_target="tpu_custom_call" | custom-call | tf_op jit(solution)/shard_map/rim_done_kernel/pallas_call | solution.py:568
  38.8 0.5 %collective-permute-done.5.other = bf16[96,1152]{1,0:T(8,128)(2,1)S(1)} collective-permute-done((bf16[96,1152]{1,0:T(8,128)(2,1)S(1)}, bf16[96,1152]{1,0:T(8,128)(2,1)S(1)}, u32[]{:S(2)}, u32[]{:S(2)}) %collective-permute-start.5) | collective-permute-done | bytes 221216 | tf_op jit(solution)/shard_map/ppermute | solution.py:681
  39.3 2.3 %last_kernel.1 = bf16[1,12,40,1152]{3,2,1,0:T(8,128)(2,1)} custom-call(bf16[96,3456]{1,0:T(8,128)(2,1)S(1)} %get-tuple-element.38.own, bf16[96,1152]{1,0:T(8,128)(2,1)S(1)} %collective-permute-done.5.other, bf16[1152,3456]{1,0:T(8,128)(2,1)S(1)} %copy-done, bf16[1152,128]{1,0:T(8,128)(2,1)S(1)} %copy-done.2, bf16[128,2304]{1,0:T(8,128)(2,1)S(1)} %copy-done.1, ...), custom_call_target="tpu_custom_call" | custom-call | tf_op jit(solution)/shard_map/last_kernel/pallas_call | solution.py:568
Async XLA Ops:
  0.0 7.1 %copy-start.3 = (f32[2,1152]{1,0:T(2,128)S(1)}, f32[2,1152]{1,0:T(2,128)}, u32[]{:S(2)}) copy-start(f32[2,1152]{1,0:T(2,128)} %modulation.5) | copy-start | bytes 27652
  0.1 11.7 %copy-start = (bf16[1152,3456]{1,0:T(8,128)(2,1)S(1)}, bf16[1152,3456]{1,0:T(8,128)(2,1)}, u32[]{:S(2)}) copy-start(bf16[1152,3456]{1,0:T(8,128)(2,1)} %w_qkv.9) | copy-start | bytes 23887876
  3.2 11.5 %collective-permute-start = (bf16[1,3,40,2432]{3,2,1,0:T(8,128)(2,1)S(1)}, bf16[1,3,40,2432]{3,2,1,0:T(8,128)(2,1)S(1)}, u32[]{:S(2)}, u32[]{:S(2)}) collective-permute-start(bf16[1,3,40,2432]{3,2,1,0:T(8,128)(2,1)S(1)} %get-tuple-element.26), channel_id=1, source_target_pairs={{0,4},{8,12},{4,0},{12,8},{1,5},{9,13},{5,1},{13,9},{2,6},{10,14},... | collective-permute-start | bytes 1751048 | tf_op jit(solution)/shard_map/ppermute | solution.py:618
  3.9 11.4 %collective-permute-start.1 = (bf16[1,3,40,2432]{3,2,1,0:T(8,128)(2,1)S(1)}, bf16[1,3,40,2432]{3,2,1,0:T(8,128)(2,1)S(1)}, u32[]{:S(2)}, u32[]{:S(2)}) collective-permute-start(bf16[1,3,40,2432]{3,2,1,0:T(8,128)(2,1)S(1)} %get-tuple-element.27), channel_id=1, source_target_pairs={{4,8},{8,4},{5,9},{9,5},{6,10},{10,6},{7,11},{11,7},{20,24},{24,20... | collective-permute-start | bytes 1751048 | tf_op jit(solution)/shard_map/ppermute | solution.py:619
  10.5 15.1 %collective-permute-start.4 = (bf16[192,1152]{1,0:T(8,128)(2,1)S(1)}, bf16[192,1152]{1,0:T(8,128)(2,1)S(1)}, u32[]{:S(2)}, u32[]{:S(2)}) collective-permute-start(bf16[192,1152]{1,0:T(8,128)(2,1)S(1)} %get-tuple-element.28.normed), channel_id=1, source_target_pairs={{0,16},{16,0},{1,17},{17,1},{2,18},{18,2},{3,19},{19,3},{4,20},{20... | collective-permute-start | bytes 1327112 | tf_op jit(solution)/shard_map/ppermute | solution.py:629
  16.3 11.5 %collective-permute-start.2 = (bf16[1,18,3,2432]{3,2,1,0:T(4,128)(2,1)S(1)}, bf16[1,18,3,2432]{3,2,1,0:T(4,128)(2,1)S(1)}, u32[]{:S(2)}, u32[]{:S(2)}) collective-permute-start(bf16[1,18,3,2432]{3,2,1,0:T(4,128)(2,1)S(1)} %get-tuple-element.34), channel_id=1, source_target_pairs={{0,1},{2,3},{1,0},{3,2},{4,5},{6,7},{5,4},{7,6},{8,9},{10,11},{9,8... | collective-permute-start | bytes 787976 | tf_op jit(solution)/shard_map/ppermute | solution.py:644
  16.3 11.5 %collective-permute-start.3 = (bf16[1,18,3,2432]{3,2,1,0:T(4,128)(2,1)S(1)}, bf16[1,18,3,2432]{3,2,1,0:T(4,128)(2,1)S(1)}, u32[]{:S(2)}, u32[]{:S(2)}) collective-permute-start(bf16[1,18,3,2432]{3,2,1,0:T(4,128)(2,1)S(1)} %get-tuple-element.35), channel_id=1, source_target_pairs={{1,2},{2,1},{5,6},{6,5},{9,10},{10,9},{13,14},{14,13},{17,18},{18,... | collective-permute-start | bytes 787976 | tf_op jit(solution)/shard_map/ppermute | solution.py:645
  21.0 4.6 %copy-start.1 = (bf16[128,2304]{1,0:T(8,128)(2,1)S(1)}, bf16[128,2304]{1,0:T(8,128)(2,1)}, u32[]{:S(2)}) copy-start(bf16[128,2304]{1,0:T(8,128)(2,1)} %constant.29.clone.spread) | copy-start | bytes 1769476
  21.0 4.5 %copy-start.2 = (bf16[1152,128]{1,0:T(8,128)(2,1)S(1)}, bf16[1152,128]{1,0:T(8,128)(2,1)}, u32[]{:S(2)}) copy-start(bf16[1152,128]{1,0:T(8,128)(2,1)} %constant.28.clone.marks) | copy-start | bytes 884740
  24.3 12.3 %collective-permute-start.6 = (bf16[192,1152]{1,0:T(8,128)(2,1)S(1)}, bf16[192,1152]{1,0:T(8,128)(2,1)S(1)}, u32[]{:S(2)}, u32[]{:S(2)}) collective-permute-start(bf16[192,1152]{1,0:T(8,128)(2,1)S(1)} %rim_kernel.1.after.rim), channel_id=1, source_target_pairs={{0,16},{16,0},{1,17},{17,1},{2,18},{18,2},{3,19},{19,3},{4,20},{20... | collective-permute-start | bytes 1327112 | tf_op jit(solution)/shard_map/ppermute | solution.py:654
  31.1 8.2 %collective-permute-start.5 = (bf16[96,1152]{1,0:T(8,128)(2,1)S(1)}, bf16[96,1152]{1,0:T(8,128)(2,1)S(1)}, u32[]{:S(2)}, u32[]{:S(2)}) collective-permute-start(bf16[96,1152]{1,0:T(8,128)(2,1)S(1)} %edge_kernel.1.edge), channel_id=1, source_target_pairs={{0,16},{16,0},{1,17},{17,1},{2,18},{18,2},{3,19},{19,3},{4,20},{20... | collective-permute-start | bytes 663560 | tf_op jit(solution)/shard_map/ppermute | solution.py:681

commit v8 on v6

--- a/solution.py
+++ b/solution.py
@@ -202,7 +202,10 @@
 
 
 def finish(heads, resid, w_out, modulation):
-    stream = resid + jnp.dot(heads, w_out, preferred_element_type=jnp.float32)
+    return adapt(resid + jnp.dot(heads, w_out, preferred_element_type=jnp.float32), modulation)
+
+
+def adapt(stream, modulation):
     average = jnp.mean(stream, -1, keepdims=True)
     centered = stream - average
     variance = jnp.mean(centered * centered, -1, keepdims=True)
@@ -241,8 +244,8 @@
 
 def inner_kernel(qkv, keep, resid_hbm, w_hbm, modulation, out, resid, w_out, heads, arrived):
     copies = [
-        pltpu.make_async_copy(resid_hbm, resid, arrived.at[0]),
-        pltpu.make_async_copy(w_hbm, w_out, arrived.at[1]),
+        pltpu.make_async_copy(w_hbm, w_out, arrived.at[0]),
+        pltpu.make_async_copy(resid_hbm, resid, arrived.at[1]),
     ]
     for copy in copies:
         copy.start()
@@ -268,10 +271,11 @@
             )
     mixed = batched(tiles, INNER_BATCH * rows // step)
     heads[...] = jnp.concatenate(mixed, axis=0).astype(jnp.bfloat16)
-    for copy in copies:
-        copy.wait()
+    copies[0].wait()
+    product = jnp.dot(heads[...], w_out[...], preferred_element_type=jnp.float32)
+    copies[1].wait()
     source = jnp.concatenate([middle(resid, 0, mine, strip) for strip in range(strips)], axis=0)
-    out[...] = finish(heads[...], source, w_out[...], modulation[...]).reshape(out.shape)
+    out[...] = adapt(source + product, modulation[...]).reshape(out.shape)
 
 
 def rim_kernel(qkv, keep, halo, resid, w_out, modulation, out, heads):

time: 41.9 us -> 41.9 us (level)
  no operation moved by 1% of the time
where the time goes in v8:
time: 41.9 us; the launch traced here: 41.8 us
  Pallas kernels  26.3 us (63%)
  starting transfers between devices  11.5 us (27%)
  waiting for transfers between devices  3.53 us (8%)
    pallas_call x10, Pallas kernels, call(): pl.pallas_call(body, out_shape=out_shape, in_specs=in_specs, out_specs=[V...  26.3 us
    ppermute x1, starting transfers between devices, fast_device(): side_two = lax.ppermute(two, 'col', pairs_two)  4.66 us
    ppermute x1, starting transfers between devices, fast_device(): second = lax.ppermute(two, 'row', pairs_two)  3.18 us
    ppermute x1, waiting for transfers between devices, fast_device(): rim_other = lax.ppermute(rim, 'tm', swap)  2.32 us
    ppermute x1, starting transfers between devices, fast_device(): inner_other = lax.ppermute(inner, 'tm', swap)  1.27 us
    ppermute x1, starting transfers between devices, fast_device(): rim_other = lax.ppermute(rim, 'tm', swap)  1.27 us
  transfers between devices with their start and end apart: 7, of which 3 were waited for; matrix products, arithmetic and copies ran while one was open for 0% of the time, Pallas kernels for 50%

profile of v8, /device:TPU:9, one launch (start us, length us, event | category | flops | bytes accessed | tf_op | source)
XLA Modules:
  0.0 41.8 jit_solution(6204495633134249121)
XLA Ops:
  0.0 0.0 copy-start.3
  0.0 0.1 pad_add_fusion.odd
  0.1 0.0 copy-start
  0.1 3.1 %load_kernel.1 = (bf16[1,3,40,2432]{3,2,1,0:T(8,128)(2,1)S(1)}, bf16[1,3,40,2432]{3,2,1,0:T(8,128)(2,1)S(1)}, bf16[3,12,40,1152]{3,2,1,0:T(8,128)(2,1)S(1)}, bf16[1,12,40,128]{3,2,1,0:T(8,128)(2,1)S(1)}) custom-call(s32[2]{0:T(128)S(1)} %pad_add_fusion.odd, bf16[3,12,40,1152]{3,2,1,0:T(8,128)(2,1)} %bitcast.4, s32[12,1,40]{2,1,0:T(1,128)} %bitcast.5), custom_call_target="tpu_custom_call" | custom-call | tf_op jit(solution)/shard_map/load_kernel/pallas_call | solution.py:563
  3.2 0.7 %collective-permute-start = (bf16[1,3,40,2432]{3,2,1,0:T(8,128)(2,1)S(1)}, bf16[1,3,40,2432]{3,2,1,0:T(8,128)(2,1)S(1)}, u32[]{:S(2)}, u32[]{:S(2)}) collective-permute-start(bf16[1,3,40,2432]{3,2,1,0:T(8,128)(2,1)S(1)} %get-tuple-element.26), channel_id=1, source_target_pairs={{0,4},{8,12},{4,0},{12,8},{1,5},{9,13},{5,1},{13,9},{2,6},{10,14},... | collective-permute-start | bytes 1751048 | tf_op jit(solution)/shard_map/ppermute | solution.py:613
  3.9 3.2 %collective-permute-start.1 = (bf16[1,3,40,2432]{3,2,1,0:T(8,128)(2,1)S(1)}, bf16[1,3,40,2432]{3,2,1,0:T(8,128)(2,1)S(1)}, u32[]{:S(2)}, u32[]{:S(2)}) collective-permute-start(bf16[1,3,40,2432]{3,2,1,0:T(8,128)(2,1)S(1)} %get-tuple-element.27), channel_id=1, source_target_pairs={{4,8},{8,4},{5,9},{9,5},{6,10},{10,6},{7,11},{11,7},{20,24},{24,20... | collective-permute-start | bytes 1751048 | tf_op jit(solution)/shard_map/ppermute | solution.py:614
  7.1 0.0 copy-done.3
  7.1 3.4 %inner_kernel.1 = (bf16[192,1152]{1,0:T(8,128)(2,1)S(1)}, bf16[1,12,40,1152]{3,2,1,0:T(8,128)(2,1)S(1)}, bf16[1152,1152]{1,0:T(8,128)(2,1)S(1)}) custom-call(bf16[3,12,40,1152]{3,2,1,0:T(8,128)(2,1)S(1)} %get-tuple-element.24.qkv, bf16[1,12,40,128]{3,2,1,0:T(8,128)(2,1)S(1)} %get-tuple-element.25.keep, bf16[1,12,40,1152]{3,2,1,0:T(8,128)(2,1)} %resid_hbm.1, ...), custom_call_target="tpu_custom_call" | custom-call | tf_op jit(solution)/shard_map/inner_kernel/pallas_call | solution.py:563
  10.5 1.3 %collective-permute-start.4 = (bf16[192,1152]{1,0:T(8,128)(2,1)S(1)}, bf16[192,1152]{1,0:T(8,128)(2,1)S(1)}, u32[]{:S(2)}, u32[]{:S(2)}) collective-permute-start(bf16[192,1152]{1,0:T(8,128)(2,1)S(1)} %get-tuple-element.28.normed), channel_id=1, source_target_pairs={{0,16},{16,0},{1,17},{17,1},{2,18},{18,2},{3,19},{19,3},{4,20},{20... | collective-permute-start | bytes 1327112 | tf_op jit(solution)/shard_map/ppermute | solution.py:624
  11.8 0.0 copy-done
  11.8 2.9 %own_kernel.1 = (bf16[192,3456]{1,0:T(8,128)(2,1)S(1)}, bf16[12,3,2432]{2,1,0:T(4,128)(2,1)S(1)}, bf16[12,3,2432]{2,1,0:T(4,128)(2,1)S(1)}) custom-call(s32[2]{0:T(128)S(1)} %pad_add_fusion.odd, bf16[192,1152]{1,0:T(8,128)(2,1)S(1)} %get-tuple-element.28.normed, bf16[1152,3456]{1,0:T(8,128)(2,1)S(1)} %copy-done, ...), custom_call_target="tpu_custom_call" | custom-call | tf_op jit(solution)/shard_map/own_kernel/pallas_call | solution.py:563
  14.7 0.0 collective-permute-done.first
  14.7 0.7 %collective-permute-done.1.second = bf16[1,3,40,2432]{3,2,1,0:T(8,128)(2,1)S(1)} collective-permute-done((bf16[1,3,40,2432]{3,2,1,0:T(8,128)(2,1)S(1)}, bf16[1,3,40,2432]{3,2,1,0:T(8,128)(2,1)S(1)}, u32[]{:S(2)}, u32[]{:S(2)}) %collective-permute-start.1) | collective-permute-done | bytes 583712 | tf_op jit(solution)/shard_map/ppermute | solution.py:614
  15.4 0.9 %columns_kernel.1 = (bf16[1,18,3,2432]{3,2,1,0:T(4,128)(2,1)S(1)}, bf16[1,18,3,2432]{3,2,1,0:T(4,128)(2,1)S(1)}, bf16[2,3,40,2432]{3,2,1,0:T(8,128)(2,1)S(1)}) custom-call(s32[2]{0:T(128)S(1)} %pad_add_fusion.odd, bf16[1,3,40,2432]{3,2,1,0:T(8,128)(2,1)S(1)} %collective-permute-done.first, bf16[1,3,40,2432]{3,2,1,0:T(8,128)(2,1)S(1)} %collective-permute-done.1.second, ...), custom_call_target="tpu_custom_call" | custom-call | tf_op jit(solution)/shard_map/columns_kernel/pallas_call | solution.py:563
  16.3 0.1 collective-permute-start.2
  16.3 4.7 %collective-permute-start.3 = (bf16[1,18,3,2432]{3,2,1,0:T(4,128)(2,1)S(1)}, bf16[1,18,3,2432]{3,2,1,0:T(4,128)(2,1)S(1)}, u32[]{:S(2)}, u32[]{:S(2)}) collective-permute-start(bf16[1,18,3,2432]{3,2,1,0:T(4,128)(2,1)S(1)} %get-tuple-element.35), channel_id=1, source_target_pairs={{1,2},{2,1},{5,6},{6,5},{9,10},{10,9},{13,14},{14,13},{17,18},{18,... | collective-permute-start | bytes 787976 | tf_op jit(solution)/shard_map/ppermute | solution.py:640
  21.0 0.0 copy-start.1
  21.0 0.0 copy-start.2
  21.0 3.2 %rim_kernel.1.after.rim = bf16[192,1152]{1,0:T(8,128)(2,1)S(1)} custom-call(bf16[3,12,40,1152]{3,2,1,0:T(8,128)(2,1)S(1)} %get-tuple-element.24.qkv, bf16[1,12,40,128]{3,2,1,0:T(8,128)(2,1)S(1)} %get-tuple-element.25.keep, bf16[2,3,40,2432]{3,2,1,0:T(8,128)(2,1)S(1)} %get-tuple-element.31.halo, bf16[1,12,40,1152]{3,2,1,0:T(8,128)(2,1)S(1)} %get-tuple-element.32.resid, ...), custom_call_target="tpu_custom_call" | custom-call | tf_op jit(solution)/shard_map/rim_kernel/pallas_call | solution.py:563
  24.3 1.3 %collective-permute-start.6 = (bf16[192,1152]{1,0:T(8,128)(2,1)S(1)}, bf16[192,1152]{1,0:T(8,128)(2,1)S(1)}, u32[]{:S(2)}, u32[]{:S(2)}) collective-permute-start(bf16[192,1152]{1,0:T(8,128)(2,1)S(1)} %rim_kernel.1.after.rim), channel_id=1, source_target_pairs={{0,16},{16,0},{1,17},{17,1},{2,18},{18,2},{3,19},{19,3},{4,20},{20... | collective-permute-start | bytes 1327112 | tf_op jit(solution)/shard_map/ppermute | solution.py:649
  25.6 0.0 collective-permute-done.4.other
  25.6 0.0 copy-done.1
  25.6 0.0 copy-done.2
  25.6 2.2 %inner_done_kernel.1 = (bf16[6,40,1152]{2,1,0:T(8,128)(2,1)S(1)}, f32[6,16,1152]{2,1,0:T(8,128)S(1)}) custom-call(bf16[192,3456]{1,0:T(8,128)(2,1)S(1)} %get-tuple-element.36.own, bf16[192,1152]{1,0:T(8,128)(2,1)S(1)} %collective-permute-done.4.other, bf16[1152,3456]{1,0:T(8,128)(2,1)S(1)} %copy-done, bf16[1152,128]{1,0:T(8,128)(2,1)S(1)} %copy-done.2, ...), custom_call_target="tpu_custom_call" | custom-call | tf_op jit(solution)/shard_map/inner_done_kernel/pallas_call | solution.py:563
  27.8 0.0 collective-permute-done.2.side_one
  27.8 0.0 collective-permute-done.3.side_two
  27.8 3.3 %edge_kernel.1.edge = bf16[96,1152]{1,0:T(8,128)(2,1)S(1)} custom-call(s32[2]{0:T(128)S(1)} %pad_add_fusion.odd, bf16[3,12,40,1152]{3,2,1,0:T(8,128)(2,1)S(1)} %get-tuple-element.24.qkv, bf16[1,12,40,128]{3,2,1,0:T(8,128)(2,1)S(1)} %get-tuple-element.25.keep, bf16[2,3,40,2432]{3,2,1,0:T(8,128)(2,1)S(1)} %get-tuple-element.31.halo, ...), custom_call_target="tpu_custom_call" | custom-call | tf_op jit(solution)/shard_map/edge_kernel/pallas_call | solution.py:563
  31.1 0.3 collective-permute-start.5
  31.4 2.9 %late_own_kernel.1 = (bf16[192,3456]{1,0:T(8,128)(2,1)S(1)}, bf16[96,3456]{1,0:T(8,128)(2,1)S(1)}) custom-call(bf16[192,1152]{1,0:T(8,128)(2,1)S(1)} %rim_kernel.1.after.rim, bf16[96,1152]{1,0:T(8,128)(2,1)S(1)} %edge_kernel.1.edge, bf16[1152,3456]{1,0:T(8,128)(2,1)S(1)} %copy-done), custom_call_target="tpu_custom_call" | custom-call | tf_op jit(solution)/shard_map/late_own_kernel/pallas_call | solution.py:563
  34.3 2.3 %collective-permute-done.6.other = bf16[192,1152]{1,0:T(8,128)(2,1)S(1)} collective-permute-done((bf16[192,1152]{1,0:T(8,128)(2,1)S(1)}, bf16[192,1152]{1,0:T(8,128)(2,1)S(1)}, u32[]{:S(2)}, u32[]{:S(2)}) %collective-permute-start.6) | collective-permute-done | bytes 442400 | tf_op jit(solution)/shard_map/ppermute | solution.py:649
  36.6 2.2 %rim_done_kernel.1 = (bf16[6,40,1152]{2,1,0:T(8,128)(2,1)S(1)}, f32[6,16,1152]{2,1,0:T(8,128)S(1)}) custom-call(bf16[192,3456]{1,0:T(8,128)(2,1)S(1)} %get-tuple-element.40.own, bf16[192,1152]{1,0:T(8,128)(2,1)S(1)} %collective-permute-done.6.other, bf16[1152,3456]{1,0:T(8,128)(2,1)S(1)} %copy-done, bf16[1152,128]{1,0:T(8,128)(2,1)S(1)} %copy-done.2, ...), custom_call_target="tpu_custom_call" | custom-call | tf_op jit(solution)/shard_map/rim_done_kernel/pallas_call | solution.py:563
  38.8 0.5 %collective-permute-done.5.other = bf16[96,1152]{1,0:T(8,128)(2,1)S(1)} collective-permute-done((bf16[96,1152]{1,0:T(8,128)(2,1)S(1)}, bf16[96,1152]{1,0:T(8,128)(2,1)S(1)}, u32[]{:S(2)}, u32[]{:S(2)}) %collective-permute-start.5) | collective-permute-done | bytes 221216 | tf_op jit(solution)/shard_map/ppermute | solution.py:676
  39.3 2.3 %last_kernel.1 = bf16[1,12,40,1152]{3,2,1,0:T(8,128)(2,1)} custom-call(bf16[96,3456]{1,0:T(8,128)(2,1)S(1)} %get-tuple-element.38.own, bf16[96,1152]{1,0:T(8,128)(2,1)S(1)} %collective-permute-done.5.other, bf16[1152,3456]{1,0:T(8,128)(2,1)S(1)} %copy-done, bf16[1152,128]{1,0:T(8,128)(2,1)S(1)} %copy-done.2, bf16[128,1152]{1,0:T(8,128)(2,1)S(1)} %copy-done.1, ...), custom_call_target="tpu_custom_call" | custom-call | tf_op jit(solution)/shard_map/last_kernel/pallas_call | solution.py:563
Async XLA Ops:
  0.0 7.1 %copy-start.3 = (f32[2,1152]{1,0:T(2,128)S(1)}, f32[2,1152]{1,0:T(2,128)}, u32[]{:S(2)}) copy-start(f32[2,1152]{1,0:T(2,128)} %modulation.5) | copy-start | bytes 27652
  0.1 11.7 %copy-start = (bf16[1152,3456]{1,0:T(8,128)(2,1)S(1)}, bf16[1152,3456]{1,0:T(8,128)(2,1)}, u32[]{:S(2)}) copy-start(bf16[1152,3456]{1,0:T(8,128)(2,1)} %w_qkv.9) | copy-start | bytes 23887876
  3.2 11.5 %collective-permute-start = (bf16[1,3,40,2432]{3,2,1,0:T(8,128)(2,1)S(1)}, bf16[1,3,40,2432]{3,2,1,0:T(8,128)(2,1)S(1)}, u32[]{:S(2)}, u32[]{:S(2)}) collective-permute-start(bf16[1,3,40,2432]{3,2,1,0:T(8,128)(2,1)S(1)} %get-tuple-element.26), channel_id=1, source_target_pairs={{0,4},{8,12},{4,0},{12,8},{1,5},{9,13},{5,1},{13,9},{2,6},{10,14},... | collective-permute-start | bytes 1751048 | tf_op jit(solution)/shard_map/ppermute | solution.py:613
  3.9 11.4 %collective-permute-start.1 = (bf16[1,3,40,2432]{3,2,1,0:T(8,128)(2,1)S(1)}, bf16[1,3,40,2432]{3,2,1,0:T(8,128)(2,1)S(1)}, u32[]{:S(2)}, u32[]{:S(2)}) collective-permute-start(bf16[1,3,40,2432]{3,2,1,0:T(8,128)(2,1)S(1)} %get-tuple-element.27), channel_id=1, source_target_pairs={{4,8},{8,4},{5,9},{9,5},{6,10},{10,6},{7,11},{11,7},{20,24},{24,20... | collective-permute-start | bytes 1751048 | tf_op jit(solution)/shard_map/ppermute | solution.py:614
  10.5 15.1 %collective-permute-start.4 = (bf16[192,1152]{1,0:T(8,128)(2,1)S(1)}, bf16[192,1152]{1,0:T(8,128)(2,1)S(1)}, u32[]{:S(2)}, u32[]{:S(2)}) collective-permute-start(bf16[192,1152]{1,0:T(8,128)(2,1)S(1)} %get-tuple-element.28.normed), channel_id=1, source_target_pairs={{0,16},{16,0},{1,17},{17,1},{2,18},{18,2},{3,19},{19,3},{4,20},{20... | collective-permute-start | bytes 1327112 | tf_op jit(solution)/shard_map/ppermute | solution.py:624
  16.3 11.5 %collective-permute-start.2 = (bf16[1,18,3,2432]{3,2,1,0:T(4,128)(2,1)S(1)}, bf16[1,18,3,2432]{3,2,1,0:T(4,128)(2,1)S(1)}, u32[]{:S(2)}, u32[]{:S(2)}) collective-permute-start(bf16[1,18,3,2432]{3,2,1,0:T(4,128)(2,1)S(1)} %get-tuple-element.34), channel_id=1, source_target_pairs={{0,1},{2,3},{1,0},{3,2},{4,5},{6,7},{5,4},{7,6},{8,9},{10,11},{9,8... | collective-permute-start | bytes 787976 | tf_op jit(solution)/shard_map/ppermute | solution.py:639
  16.3 11.4 %collective-permute-start.3 = (bf16[1,18,3,2432]{3,2,1,0:T(4,128)(2,1)S(1)}, bf16[1,18,3,2432]{3,2,1,0:T(4,128)(2,1)S(1)}, u32[]{:S(2)}, u32[]{:S(2)}) collective-permute-start(bf16[1,18,3,2432]{3,2,1,0:T(4,128)(2,1)S(1)} %get-tuple-element.35), channel_id=1, source_target_pairs={{1,2},{2,1},{5,6},{6,5},{9,10},{10,9},{13,14},{14,13},{17,18},{18,... | collective-permute-start | bytes 787976 | tf_op jit(solution)/shard_map/ppermute | solution.py:640
  21.0 4.6 %copy-start.1 = (bf16[128,1152]{1,0:T(8,128)(2,1)S(1)}, bf16[128,1152]{1,0:T(8,128)(2,1)}, u32[]{:S(2)}) copy-start(bf16[128,1152]{1,0:T(8,128)(2,1)} %constant.29.clone.spread) | copy-start | bytes 884740
  21.0 4.5 %copy-start.2 = (bf16[1152,128]{1,0:T(8,128)(2,1)S(1)}, bf16[1152,128]{1,0:T(8,128)(2,1)}, u32[]{:S(2)}) copy-start(bf16[1152,128]{1,0:T(8,128)(2,1)} %constant.28.clone.marks) | copy-start | bytes 884740
  24.3 12.3 %collective-permute-start.6 = (bf16[192,1152]{1,0:T(8,128)(2,1)S(1)}, bf16[192,1152]{1,0:T(8,128)(2,1)S(1)}, u32[]{:S(2)}, u32[]{:S(2)}) collective-permute-start(bf16[192,1152]{1,0:T(8,128)(2,1)S(1)} %rim_kernel.1.after.rim), channel_id=1, source_target_pairs={{0,16},{16,0},{1,17},{17,1},{2,18},{18,2},{3,19},{19,3},{4,20},{20... | collective-permute-start | bytes 1327112 | tf_op jit(solution)/shard_map/ppermute | solution.py:649
  31.1 8.2 %collective-permute-start.5 = (bf16[96,1152]{1,0:T(8,128)(2,1)S(1)}, bf16[96,1152]{1,0:T(8,128)(2,1)S(1)}, u32[]{:S(2)}, u32[]{:S(2)}) collective-permute-start(bf16[96,1152]{1,0:T(8,128)(2,1)S(1)} %edge_kernel.1.edge), channel_id=1, source_target_pairs={{0,16},{16,0},{1,17},{17,1},{2,18},{18,2},{3,19},{19,3},{4,20},{20... | collective-permute-start | bytes 663560 | tf_op jit(solution)/shard_map/ppermute | solution.py:676

commit v9 on v6

--- a/solution.py
+++ b/solution.py
@@ -226,7 +226,7 @@
 
 
 INNER_ROWS = 6
-INNER_BATCH = 4
+INNER_BATCH = 2
 RIM_BATCH = 4
 RIM_STRIPS = 2
 EDGE_BATCH = 3

time: 41.9 us -> 41.9 us (level)
  no operation moved by 1% of the time
where the time goes in v9:
time: 41.9 us; the launch traced here: 41.7 us
  Pallas kernels  26.3 us (63%)
  starting transfers between devices  11.5 us (27%)
  waiting for transfers between devices  3.51 us (8%)
    pallas_call x10, Pallas kernels, call(): pl.pallas_call(body, out_shape=out_shape, in_specs=in_specs, out_specs=[V...  26.3 us
    ppermute x1, starting transfers between devices, fast_device(): side_two = lax.ppermute(two, 'col', pairs_two)  4.66 us
    ppermute x1, starting transfers between devices, fast_device(): second = lax.ppermute(two, 'row', pairs_two)  3.18 us
    ppermute x1, waiting for transfers between devices, fast_device(): rim_other = lax.ppermute(rim, 'tm', swap)  2.32 us
    ppermute x1, starting transfers between devices, fast_device(): inner_other = lax.ppermute(inner, 'tm', swap)  1.28 us
    ppermute x1, starting transfers between devices, fast_device(): rim_other = lax.ppermute(rim, 'tm', swap)  1.27 us
  transfers between devices with their start and end apart: 7, of which 3 were waited for; matrix products, arithmetic and copies ran while one was open for 0% of the time, Pallas kernels for 50%

profile of v9, /device:TPU:9, one launch (start us, length us, event | category | flops | bytes accessed | tf_op | source)
XLA Modules:
  0.0 41.7 jit_solution(110582583400923975)
XLA Ops:
  0.0 0.0 copy-start.3
  0.0 0.1 pad_add_fusion.odd
  0.1 0.0 copy-start
  0.1 3.1 %load_kernel.1 = (bf16[1,3,40,2432]{3,2,1,0:T(8,128)(2,1)S(1)}, bf16[1,3,40,2432]{3,2,1,0:T(8,128)(2,1)S(1)}, bf16[3,12,40,1152]{3,2,1,0:T(8,128)(2,1)S(1)}, bf16[1,12,40,128]{3,2,1,0:T(8,128)(2,1)S(1)}) custom-call(s32[2]{0:T(128)S(1)} %pad_add_fusion.odd, bf16[3,12,40,1152]{3,2,1,0:T(8,128)(2,1)} %bitcast.4, s32[12,1,40]{2,1,0:T(1,128)} %bitcast.5), custom_call_target="tpu_custom_call" | custom-call | tf_op jit(solution)/shard_map/load_kernel/pallas_call | solution.py:559
  3.2 0.7 %collective-permute-start = (bf16[1,3,40,2432]{3,2,1,0:T(8,128)(2,1)S(1)}, bf16[1,3,40,2432]{3,2,1,0:T(8,128)(2,1)S(1)}, u32[]{:S(2)}, u32[]{:S(2)}) collective-permute-start(bf16[1,3,40,2432]{3,2,1,0:T(8,128)(2,1)S(1)} %get-tuple-element.26), channel_id=1, source_target_pairs={{0,4},{8,12},{4,0},{12,8},{1,5},{9,13},{5,1},{13,9},{2,6},{10,14},... | collective-permute-start | bytes 1751048 | tf_op jit(solution)/shard_map/ppermute | solution.py:609
  3.9 3.2 %collective-permute-start.1 = (bf16[1,3,40,2432]{3,2,1,0:T(8,128)(2,1)S(1)}, bf16[1,3,40,2432]{3,2,1,0:T(8,128)(2,1)S(1)}, u32[]{:S(2)}, u32[]{:S(2)}) collective-permute-start(bf16[1,3,40,2432]{3,2,1,0:T(8,128)(2,1)S(1)} %get-tuple-element.27), channel_id=1, source_target_pairs={{4,8},{8,4},{5,9},{9,5},{6,10},{10,6},{7,11},{11,7},{20,24},{24,20... | collective-permute-start | bytes 1751048 | tf_op jit(solution)/shard_map/ppermute | solution.py:610
  7.1 0.0 copy-done.3
  7.1 3.3 %inner_kernel.1 = (bf16[192,1152]{1,0:T(8,128)(2,1)S(1)}, bf16[1,12,40,1152]{3,2,1,0:T(8,128)(2,1)S(1)}, bf16[1152,1152]{1,0:T(8,128)(2,1)S(1)}) custom-call(bf16[3,12,40,1152]{3,2,1,0:T(8,128)(2,1)S(1)} %get-tuple-element.24.qkv, bf16[1,12,40,128]{3,2,1,0:T(8,128)(2,1)S(1)} %get-tuple-element.25.keep, bf16[1,12,40,1152]{3,2,1,0:T(8,128)(2,1)} %resid_hbm.1, ...), custom_call_target="tpu_custom_call" | custom-call | tf_op jit(solution)/shard_map/inner_kernel/pallas_call | solution.py:559
  10.4 1.3 %collective-permute-start.4 = (bf16[192,1152]{1,0:T(8,128)(2,1)S(1)}, bf16[192,1152]{1,0:T(8,128)(2,1)S(1)}, u32[]{:S(2)}, u32[]{:S(2)}) collective-permute-start(bf16[192,1152]{1,0:T(8,128)(2,1)S(1)} %get-tuple-element.28.normed), channel_id=1, source_target_pairs={{0,16},{16,0},{1,17},{17,1},{2,18},{18,2},{3,19},{19,3},{4,20},{20... | collective-permute-start | bytes 1327112 | tf_op jit(solution)/shard_map/ppermute | solution.py:620
  11.7 0.0 copy-done
  11.7 2.9 %own_kernel.1 = (bf16[192,3456]{1,0:T(8,128)(2,1)S(1)}, bf16[12,3,2432]{2,1,0:T(4,128)(2,1)S(1)}, bf16[12,3,2432]{2,1,0:T(4,128)(2,1)S(1)}) custom-call(s32[2]{0:T(128)S(1)} %pad_add_fusion.odd, bf16[192,1152]{1,0:T(8,128)(2,1)S(1)} %get-tuple-element.28.normed, bf16[1152,3456]{1,0:T(8,128)(2,1)S(1)} %copy-done, ...), custom_call_target="tpu_custom_call" | custom-call | tf_op jit(solution)/shard_map/own_kernel/pallas_call | solution.py:559
  14.6 0.0 collective-permute-done.first
  14.6 0.7 %collective-permute-done.1.second = bf16[1,3,40,2432]{3,2,1,0:T(8,128)(2,1)S(1)} collective-permute-done((bf16[1,3,40,2432]{3,2,1,0:T(8,128)(2,1)S(1)}, bf16[1,3,40,2432]{3,2,1,0:T(8,128)(2,1)S(1)}, u32[]{:S(2)}, u32[]{:S(2)}) %collective-permute-start.1) | collective-permute-done | bytes 583712 | tf_op jit(solution)/shard_map/ppermute | solution.py:610
  15.4 0.9 %columns_kernel.1 = (bf16[1,18,3,2432]{3,2,1,0:T(4,128)(2,1)S(1)}, bf16[1,18,3,2432]{3,2,1,0:T(4,128)(2,1)S(1)}, bf16[2,3,40,2432]{3,2,1,0:T(8,128)(2,1)S(1)}) custom-call(s32[2]{0:T(128)S(1)} %pad_add_fusion.odd, bf16[1,3,40,2432]{3,2,1,0:T(8,128)(2,1)S(1)} %collective-permute-done.first, bf16[1,3,40,2432]{3,2,1,0:T(8,128)(2,1)S(1)} %collective-permute-done.1.second, ...), custom_call_target="tpu_custom_call" | custom-call | tf_op jit(solution)/shard_map/columns_kernel/pallas_call | solution.py:559
  16.3 0.1 collective-permute-start.2
  16.3 4.7 %collective-permute-start.3 = (bf16[1,18,3,2432]{3,2,1,0:T(4,128)(2,1)S(1)}, bf16[1,18,3,2432]{3,2,1,0:T(4,128)(2,1)S(1)}, u32[]{:S(2)}, u32[]{:S(2)}) collective-permute-start(bf16[1,18,3,2432]{3,2,1,0:T(4,128)(2,1)S(1)} %get-tuple-element.35), channel_id=1, source_target_pairs={{1,2},{2,1},{5,6},{6,5},{9,10},{10,9},{13,14},{14,13},{17,18},{18,... | collective-permute-start | bytes 787976 | tf_op jit(solution)/shard_map/ppermute | solution.py:636
  21.0 0.0 copy-start.1
  21.0 0.0 copy-start.2
  21.0 3.2 %rim_kernel.1.after.rim = bf16[192,1152]{1,0:T(8,128)(2,1)S(1)} custom-call(bf16[3,12,40,1152]{3,2,1,0:T(8,128)(2,1)S(1)} %get-tuple-element.24.qkv, bf16[1,12,40,128]{3,2,1,0:T(8,128)(2,1)S(1)} %get-tuple-element.25.keep, bf16[2,3,40,2432]{3,2,1,0:T(8,128)(2,1)S(1)} %get-tuple-element.31.halo, bf16[1,12,40,1152]{3,2,1,0:T(8,128)(2,1)S(1)} %get-tuple-element.32.resid, ...), custom_call_target="tpu_custom_call" | custom-call | tf_op jit(solution)/shard_map/rim_kernel/pallas_call | solution.py:559
  24.3 1.3 %collective-permute-start.6 = (bf16[192,1152]{1,0:T(8,128)(2,1)S(1)}, bf16[192,1152]{1,0:T(8,128)(2,1)S(1)}, u32[]{:S(2)}, u32[]{:S(2)}) collective-permute-start(bf16[192,1152]{1,0:T(8,128)(2,1)S(1)} %rim_kernel.1.after.rim), channel_id=1, source_target_pairs={{0,16},{16,0},{1,17},{17,1},{2,18},{18,2},{3,19},{19,3},{4,20},{20... | collective-permute-start | bytes 1327112 | tf_op jit(solution)/shard_map/ppermute | solution.py:645
  25.6 0.0 collective-permute-done.4.other
  25.6 0.0 copy-done.1
  25.6 0.0 copy-done.2
  25.6 2.2 %inner_done_kernel.1 = (bf16[6,40,1152]{2,1,0:T(8,128)(2,1)S(1)}, f32[6,16,1152]{2,1,0:T(8,128)S(1)}) custom-call(bf16[192,3456]{1,0:T(8,128)(2,1)S(1)} %get-tuple-element.36.own, bf16[192,1152]{1,0:T(8,128)(2,1)S(1)} %collective-permute-done.4.other, bf16[1152,3456]{1,0:T(8,128)(2,1)S(1)} %copy-done, bf16[1152,128]{1,0:T(8,128)(2,1)S(1)} %copy-done.2, ...), custom_call_target="tpu_custom_call" | custom-call | tf_op jit(solution)/shard_map/inner_done_kernel/pallas_call | solution.py:559
  27.8 0.0 collective-permute-done.2.side_one
  27.8 0.0 collective-permute-done.3.side_two
  27.8 3.3 %edge_kernel.1.edge = bf16[96,1152]{1,0:T(8,128)(2,1)S(1)} custom-call(s32[2]{0:T(128)S(1)} %pad_add_fusion.odd, bf16[3,12,40,1152]{3,2,1,0:T(8,128)(2,1)S(1)} %get-tuple-element.24.qkv, bf16[1,12,40,128]{3,2,1,0:T(8,128)(2,1)S(1)} %get-tuple-element.25.keep, bf16[2,3,40,2432]{3,2,1,0:T(8,128)(2,1)S(1)} %get-tuple-element.31.halo, ...), custom_call_target="tpu_custom_call" | custom-call | tf_op jit(solution)/shard_map/edge_kernel/pallas_call | solution.py:559
  31.1 0.3 collective-permute-start.5
  31.4 2.9 %late_own_kernel.1 = (bf16[192,3456]{1,0:T(8,128)(2,1)S(1)}, bf16[96,3456]{1,0:T(8,128)(2,1)S(1)}) custom-call(bf16[192,1152]{1,0:T(8,128)(2,1)S(1)} %rim_kernel.1.after.rim, bf16[96,1152]{1,0:T(8,128)(2,1)S(1)} %edge_kernel.1.edge, bf16[1152,3456]{1,0:T(8,128)(2,1)S(1)} %copy-done), custom_call_target="tpu_custom_call" | custom-call | tf_op jit(solution)/shard_map/late_own_kernel/pallas_call | solution.py:559
  34.3 2.3 %collective-permute-done.6.other = bf16[192,1152]{1,0:T(8,128)(2,1)S(1)} collective-permute-done((bf16[192,1152]{1,0:T(8,128)(2,1)S(1)}, bf16[192,1152]{1,0:T(8,128)(2,1)S(1)}, u32[]{:S(2)}, u32[]{:S(2)}) %collective-permute-start.6) | collective-permute-done | bytes 442400 | tf_op jit(solution)/shard_map/ppermute | solution.py:645
  36.6 2.2 %rim_done_kernel.1 = (bf16[6,40,1152]{2,1,0:T(8,128)(2,1)S(1)}, f32[6,16,1152]{2,1,0:T(8,128)S(1)}) custom-call(bf16[192,3456]{1,0:T(8,128)(2,1)S(1)} %get-tuple-element.40.own, bf16[192,1152]{1,0:T(8,128)(2,1)S(1)} %collective-permute-done.6.other, bf16[1152,3456]{1,0:T(8,128)(2,1)S(1)} %copy-done, bf16[1152,128]{1,0:T(8,128)(2,1)S(1)} %copy-done.2, ...), custom_call_target="tpu_custom_call" | custom-call | tf_op jit(solution)/shard_map/rim_done_kernel/pallas_call | solution.py:559
  38.8 0.5 %collective-permute-done.5.other = bf16[96,1152]{1,0:T(8,128)(2,1)S(1)} collective-permute-done((bf16[96,1152]{1,0:T(8,128)(2,1)S(1)}, bf16[96,1152]{1,0:T(8,128)(2,1)S(1)}, u32[]{:S(2)}, u32[]{:S(2)}) %collective-permute-start.5) | collective-permute-done | bytes 221216 | tf_op jit(solution)/shard_map/ppermute | solution.py:672
  39.2 2.3 %last_kernel.1 = bf16[1,12,40,1152]{3,2,1,0:T(8,128)(2,1)} custom-call(bf16[96,3456]{1,0:T(8,128)(2,1)S(1)} %get-tuple-element.38.own, bf16[96,1152]{1,0:T(8,128)(2,1)S(1)} %collective-permute-done.5.other, bf16[1152,3456]{1,0:T(8,128)(2,1)S(1)} %copy-done, bf16[1152,128]{1,0:T(8,128)(2,1)S(1)} %copy-done.2, bf16[128,1152]{1,0:T(8,128)(2,1)S(1)} %copy-done.1, ...), custom_call_target="tpu_custom_call" | custom-call | tf_op jit(solution)/shard_map/last_kernel/pallas_call | solution.py:559
Async XLA Ops:
  0.0 7.1 %copy-start.3 = (f32[2,1152]{1,0:T(2,128)S(1)}, f32[2,1152]{1,0:T(2,128)}, u32[]{:S(2)}) copy-start(f32[2,1152]{1,0:T(2,128)} %modulation.5) | copy-start | bytes 27652
  0.1 11.6 %copy-start = (bf16[1152,3456]{1,0:T(8,128)(2,1)S(1)}, bf16[1152,3456]{1,0:T(8,128)(2,1)}, u32[]{:S(2)}) copy-start(bf16[1152,3456]{1,0:T(8,128)(2,1)} %w_qkv.9) | copy-start | bytes 23887876
  3.2 11.4 %collective-permute-start = (bf16[1,3,40,2432]{3,2,1,0:T(8,128)(2,1)S(1)}, bf16[1,3,40,2432]{3,2,1,0:T(8,128)(2,1)S(1)}, u32[]{:S(2)}, u32[]{:S(2)}) collective-permute-start(bf16[1,3,40,2432]{3,2,1,0:T(8,128)(2,1)S(1)} %get-tuple-element.26), channel_id=1, source_target_pairs={{0,4},{8,12},{4,0},{12,8},{1,5},{9,13},{5,1},{13,9},{2,6},{10,14},... | collective-permute-start | bytes 1751048 | tf_op jit(solution)/shard_map/ppermute | solution.py:609
  3.9 11.4 %collective-permute-start.1 = (bf16[1,3,40,2432]{3,2,1,0:T(8,128)(2,1)S(1)}, bf16[1,3,40,2432]{3,2,1,0:T(8,128)(2,1)S(1)}, u32[]{:S(2)}, u32[]{:S(2)}) collective-permute-start(bf16[1,3,40,2432]{3,2,1,0:T(8,128)(2,1)S(1)} %get-tuple-element.27), channel_id=1, source_target_pairs={{4,8},{8,4},{5,9},{9,5},{6,10},{10,6},{7,11},{11,7},{20,24},{24,20... | collective-permute-start | bytes 1751048 | tf_op jit(solution)/shard_map/ppermute | solution.py:610
  10.4 15.1 %collective-permute-start.4 = (bf16[192,1152]{1,0:T(8,128)(2,1)S(1)}, bf16[192,1152]{1,0:T(8,128)(2,1)S(1)}, u32[]{:S(2)}, u32[]{:S(2)}) collective-permute-start(bf16[192,1152]{1,0:T(8,128)(2,1)S(1)} %get-tuple-element.28.normed), channel_id=1, source_target_pairs={{0,16},{16,0},{1,17},{17,1},{2,18},{18,2},{3,19},{19,3},{4,20},{20... | collective-permute-start | bytes 1327112 | tf_op jit(solution)/shard_map/ppermute | solution.py:620
  16.3 11.5 %collective-permute-start.2 = (bf16[1,18,3,2432]{3,2,1,0:T(4,128)(2,1)S(1)}, bf16[1,18,3,2432]{3,2,1,0:T(4,128)(2,1)S(1)}, u32[]{:S(2)}, u32[]{:S(2)}) collective-permute-start(bf16[1,18,3,2432]{3,2,1,0:T(4,128)(2,1)S(1)} %get-tuple-element.34), channel_id=1, source_target_pairs={{0,1},{2,3},{1,0},{3,2},{4,5},{6,7},{5,4},{7,6},{8,9},{10,11},{9,8... | collective-permute-start | bytes 787976 | tf_op jit(solution)/shard_map/ppermute | solution.py:635
  16.3 11.4 %collective-permute-start.3 = (bf16[1,18,3,2432]{3,2,1,0:T(4,128)(2,1)S(1)}, bf16[1,18,3,2432]{3,2,1,0:T(4,128)(2,1)S(1)}, u32[]{:S(2)}, u32[]{:S(2)}) collective-permute-start(bf16[1,18,3,2432]{3,2,1,0:T(4,128)(2,1)S(1)} %get-tuple-element.35), channel_id=1, source_target_pairs={{1,2},{2,1},{5,6},{6,5},{9,10},{10,9},{13,14},{14,13},{17,18},{18,... | collective-permute-start | bytes 787976 | tf_op jit(solution)/shard_map/ppermute | solution.py:636
  21.0 4.6 %copy-start.1 = (bf16[128,1152]{1,0:T(8,128)(2,1)S(1)}, bf16[128,1152]{1,0:T(8,128)(2,1)}, u32[]{:S(2)}) copy-start(bf16[128,1152]{1,0:T(8,128)(2,1)} %constant.29.clone.spread) | copy-start | bytes 884740
  21.0 4.5 %copy-start.2 = (bf16[1152,128]{1,0:T(8,128)(2,1)S(1)}, bf16[1152,128]{1,0:T(8,128)(2,1)}, u32[]{:S(2)}) copy-start(bf16[1152,128]{1,0:T(8,128)(2,1)} %constant.28.clone.marks) | copy-start | bytes 884740
  24.3 12.3 %collective-permute-start.6 = (bf16[192,1152]{1,0:T(8,128)(2,1)S(1)}, bf16[192,1152]{1,0:T(8,128)(2,1)S(1)}, u32[]{:S(2)}, u32[]{:S(2)}) collective-permute-start(bf16[192,1152]{1,0:T(8,128)(2,1)S(1)} %rim_kernel.1.after.rim), channel_id=1, source_target_pairs={{0,16},{16,0},{1,17},{17,1},{2,18},{18,2},{3,19},{19,3},{4,20},{20... | collective-permute-start | bytes 1327112 | tf_op jit(solution)/shard_map/ppermute | solution.py:645
  31.1 8.2 %collective-permute-start.5 = (bf16[96,1152]{1,0:T(8,128)(2,1)S(1)}, bf16[96,1152]{1,0:T(8,128)(2,1)S(1)}, u32[]{:S(2)}, u32[]{:S(2)}) collective-permute-start(bf16[96,1152]{1,0:T(8,128)(2,1)S(1)} %edge_kernel.1.edge), channel_id=1, source_target_pairs={{0,16},{16,0},{1,17},{17,1},{2,18},{18,2},{3,19},{19,3},{4,20},{20... | collective-permute-start | bytes 663560 | tf_op jit(solution)/shard_map/ppermute | solution.py:672
